TPU v7x, 32 devices: a whole 2x2x4 slice. The times are simulated.
32 devices in a mesh: blk: 8 (over z, core), head: 4 (over y, x).
Axes of the slice: x: 2, y: 2, z: 4, core: 2. Of those that a mesh axis runs over, the one named last changes fastest.
Arguments:
- inputs: bfloat16 [4096, 1024], P(('blk', 'head')), may hold values from -6 to 6
- token_place: int32 [4096], replicated, may hold values from 0 to 4095, as said below
- lengths: int32 [4], replicated, may hold values from 256 to 2048, as said below
- w_norm1: float32 [1024], replicated, may hold values from 0.1 to 1.9
- w_query: bfloat16 [1024, 1024], P('blk', 'head'), may hold values from -0.1875 to 0.1875
- key_weight: bfloat16 [1024, 512], P('blk', 'head'), may hold values from -0.1875 to 0.1875
- value_weight: bfloat16 [1024, 512], P('blk', 'head'), may hold values from -0.1875 to 0.1875
- w_out: bfloat16 [1024, 1024], P('head', 'blk'), may hold values from -0.75 to 0.75
- w_norm2: float32 [1024], replicated, may hold values from 0.1 to 1.9
- router: bfloat16 [1024, 32], replicated, may hold values from -0.09375 to 0.09375
- routes: int32 [4096, 8], P(('blk', 'head')), may hold values from 0 to 31, all different within a row
- slot_order: int32 [4096, 8], P(('blk', 'head')), may hold values from 0 to 1023, as said below
- w_gate: bfloat16 [32, 1024, 512], P('head', 'blk'), may hold values from -0.1875 to 0.1875
- w_up: bfloat16 [32, 1024, 512], P('head', 'blk'), may hold values from -0.1875 to 0.1875
- w_down: bfloat16 [32, 512, 1024], P('head', None, 'blk'), may hold values from -1 to 1
- grad_out: bfloat16 [4096, 1024], P(('blk', 'head')), may hold values from -6 to 6
Outputs:
- output: bfloat16 [4096, 1024], P(('blk', 'head'))
- grad_inputs: float32 [4096, 1024], P(('blk', 'head'))
- grad_norm1: float32 [1024], replicated
- grad_query: float32 [1024, 1024], P('blk', 'head')
- grad_key: float32 [1024, 512], P('blk', 'head')
- grad_value: float32 [1024, 512], P('blk', 'head')
- grad_w_out: float32 [1024, 1024], P('head', 'blk')
- grad_norm2: float32 [1024], replicated
- grad_router: float32 [1024, 32], replicated
- grad_gate: float32 [32, 1024, 512], P('head', 'blk')
- grad_up: float32 [32, 1024, 512], P('head', 'blk')
- grad_down: float32 [32, 512, 1024], P('head', None, 'blk')
Inputs may be any that keep to these rules, and one draw needn't show every extreme that they name: `token_place`: A permutation. With the stream cut into blocks of 256 places, the p-th aligned group of 512 rows holds, in some order, blocks p and 15 - p. `lengths`: the sequences fill the 4096 places in order; the first or the last has 2048 places, the others 4096/16 or more, one of them exactly that. `routes`: each row names 8 different experts. `slot_order`: each aligned block of 128 rows holds every number of 0 to 1023 once.
All inputs are finite; a program needn't handle non-finite values.
Results may differ from a plain program's by a relative error of at most 0.025.
Values may be sent and summed in bfloat16 or wider, within the bound.
A program may use at most 192 MiB of HBM per device.

v0:
```python
import math

import jax
import jax.numpy as jnp
from jax import lax
from jax.sharding import PartitionSpec as P

MODEL_WIDTH = 1024
HEAD_SIZE = 64
E = 32
TOPK = 8
CAP = 40


eps = 1e-06
rope_base = 10000.0


def seq_begin(token_position, lengths):
    starts = jnp.cumsum(lengths) - lengths
    inside = token_position[:, None] >= starts[None, 1:]
    return jnp.sum(jnp.where(inside, lengths[None, :-1], 0), axis=1)


def rotation(token_position, begin_index, width):
    half = width // 2
    freq = jnp.exp(jnp.arange(half, dtype=jnp.float32) * (-2.0 * math.log(rope_base) / width))
    angle = (token_position - begin_index).astype(jnp.float32)[:, None] * freq[None, :]
    return (jnp.cos(angle)[:, None, :], jnp.sin(angle)[:, None, :])


def turn_index(values, cosine_table, sine_table):
    half = values.shape[-1] // 2
    leading = values[..., :half]
    trailing = values[..., half:]
    return jnp.concatenate(
        [
            leading * cosine_table - trailing * sine_table,
            trailing * cosine_table + leading * sine_table,
        ],
        axis=-1,
    )


def slot_numbers(routes, slot_order):
    flat_expert = routes.reshape(-1)
    rank = slot_order.reshape(-1)
    count = flat_expert.shape[0]
    by_rank = jnp.zeros((count,), jnp.int32).at[rank].set(jnp.arange(count, dtype=jnp.int32))
    expert_sorted = flat_expert[by_rank]
    onehot = (expert_sorted[:, None] == jnp.arange(E, dtype=jnp.int32)[None, :]).astype(jnp.int32)
    before = jnp.cumsum(onehot, axis=0) - onehot
    slot_sorted = jnp.sum(before * onehot, axis=1)
    slot = slot_sorted[rank].reshape(routes.shape)
    return (slot, slot < CAP)


def along_rows(left, right):
    return lax.dot_general(
        left, right, (((0,), (0,)), ((), ())), preferred_element_type=jnp.float32
    )


def against(left, right):
    return lax.dot_general(
        left, right, (((1,), (1,)), ((), ())), preferred_element_type=jnp.float32
    )


def fetch_attention(w_query, key_weight, value_weight, w_out):
    return (
        lax.all_gather(w_query, "blk", axis=0, tiled=True),
        lax.all_gather(key_weight, "blk", axis=0, tiled=True),
        lax.all_gather(value_weight, "blk", axis=0, tiled=True),
        lax.all_gather(w_out, "blk", axis=1, tiled=True),
    )


def fetch_experts(w_gate, w_up, w_down):
    return (
        lax.all_gather(w_gate, "blk", axis=1, tiled=True),
        lax.all_gather(w_up, "blk", axis=1, tiled=True),
        lax.all_gather(w_down, "blk", axis=2, tiled=True),
    )


def fetch_keys(rotated_key, value_rows):
    return (
        lax.all_gather(rotated_key, "blk", axis=0, tiled=True),
        lax.all_gather(value_rows, "blk", axis=0, tiled=True),
    )


def on_device(
    inputs,
    token_place,
    lengths,
    w_norm1,
    w_query,
    key_weight,
    value_weight,
    w_out,
    w_norm2,
    router,
    routes,
    slot_order,
    w_gate,
    w_up,
    w_down,
    grad_out,
):
    rows = inputs.shape[0]
    blk_count = lax.axis_size("blk")
    head_count = lax.axis_size("head")
    group_rows = rows * head_count
    heads_local = w_query.shape[1] // HEAD_SIZE
    kv_local = key_weight.shape[1] // HEAD_SIZE
    head_groups = heads_local // kv_local
    experts_local = E // head_count
    scale = 1.0 / math.sqrt(HEAD_SIZE)
    query_all, key_all, value_all, out_all = fetch_attention(
        w_query, key_weight, value_weight, w_out
    )
    gate_all, up_all, down_all = fetch_experts(w_gate, w_up, w_down)
    hidden = inputs.astype(jnp.float32)
    scale_one = lax.rsqrt(jnp.mean(hidden * hidden, axis=-1, keepdims=True) + eps)
    unit_one = hidden * scale_one
    normed = (unit_one * w_norm1).astype(jnp.bfloat16)
    gathered = lax.all_gather(normed, "head", axis=0, tiled=True)
    begin_index = seq_begin(token_place, lengths)
    first_row = lax.axis_index("blk") * group_rows
    own_place = lax.dynamic_slice_in_dim(token_place, first_row, group_rows)
    own_begin = lax.dynamic_slice_in_dim(begin_index, first_row, group_rows)
    cosine_table, sine_table = rotation(own_place, own_begin, HEAD_SIZE)
    query = jnp.dot(gathered, query_all, preferred_element_type=jnp.float32)
    key = jnp.dot(gathered, key_all, preferred_element_type=jnp.float32)
    value_rows = jnp.dot(gathered, value_all, preferred_element_type=jnp.float32).astype(
        jnp.bfloat16
    )
    rotated_query = turn_index(
        query.reshape(group_rows, heads_local, HEAD_SIZE), cosine_table, sine_table
    ).astype(jnp.bfloat16)
    rotated_key = (
        turn_index(key.reshape(group_rows, kv_local, HEAD_SIZE), cosine_table, sine_table)
        .astype(jnp.bfloat16)
        .reshape(group_rows, kv_local * HEAD_SIZE)
    )
    keys_all, values_all = fetch_keys(rotated_key, value_rows)
    query_heads = rotated_query.reshape(group_rows, kv_local, head_groups, HEAD_SIZE)
    steps = jnp.arange(blk_count, dtype=jnp.int32)

    def block_scores(key_source, value_source, index):
        start = index * group_rows
        key_block = lax.dynamic_slice_in_dim(key_source, start, group_rows).reshape(
            group_rows, kv_local, HEAD_SIZE
        )
        value_block = lax.dynamic_slice_in_dim(value_source, start, group_rows).reshape(
            group_rows, kv_local, HEAD_SIZE
        )
        key_place = lax.dynamic_slice_in_dim(token_place, start, group_rows)
        scores = (
            jnp.einsum("qhgd,khd->hgqk", query_heads, key_block, preferred_element_type=jnp.float32)
            * scale
        )
        allowed = (key_place[None, :] <= own_place[:, None]) & (
            key_place[None, :] >= own_begin[:, None]
        )
        return (scores, allowed, key_block, value_block)

    def stats_step(carry, index):
        top, total = carry
        scores, allowed, unused_keys, unused_values = block_scores(keys_all, values_all, index)
        masked = jnp.where(allowed, scores, -1e30)
        new_top = jnp.maximum(top, jnp.max(masked, axis=-1))
        total = total * jnp.exp(top - new_top) + jnp.sum(
            jnp.where(allowed, jnp.exp(masked - new_top[..., None]), 0.0), axis=-1
        )
        return ((new_top, total), None)

    start_top = jnp.full((kv_local, head_groups, group_rows), -1e30, jnp.float32)
    start_total = jnp.zeros((kv_local, head_groups, group_rows), jnp.float32)
    (top, total), unused = lax.scan(stats_step, (start_top, start_total), steps)
    log_total = top + jnp.log(total)

    def out_step(acc, index):
        scores, allowed, unused_keys, value_block = block_scores(keys_all, values_all, index)
        probs = jnp.where(allowed, jnp.exp(scores - log_total[..., None]), 0.0).astype(jnp.bfloat16)
        acc = acc + jnp.einsum(
            "hgqk,khd->qhgd", probs, value_block, preferred_element_type=jnp.float32
        )
        return (acc, None)

    attended32, unused = lax.scan(
        out_step, jnp.zeros((group_rows, kv_local, head_groups, HEAD_SIZE), jnp.float32), steps
    )
    attended_rows = attended32.reshape(group_rows, heads_local * HEAD_SIZE).astype(jnp.bfloat16)
    middle = hidden + lax.psum_scatter(
        jnp.dot(attended_rows, out_all, preferred_element_type=jnp.float32).astype(jnp.bfloat16),
        "head",
        scatter_dimension=0,
        tiled=True,
    ).astype(jnp.float32)
    scale_two = lax.rsqrt(jnp.mean(middle * middle, axis=-1, keepdims=True) + eps)
    unit_two = middle * scale_two
    normed_two = (unit_two * w_norm2).astype(jnp.bfloat16)
    logits = jnp.dot(normed_two, router, preferred_element_type=jnp.float32)
    chosen = jnp.take_along_axis(logits, routes, axis=1)
    shifted = jnp.exp(chosen - jnp.max(chosen, axis=-1, keepdims=True))
    gates = shifted / jnp.sum(shifted, axis=-1, keepdims=True)
    slot, kept = slot_numbers(routes, slot_order)
    target = routes * CAP + slot
    slot_ids = jnp.arange(E * CAP, dtype=jnp.int32)
    match = (target[None, :, :] == slot_ids[:, None, None]) & kept[None, :, :]
    dispatch = jnp.any(match, axis=-1).astype(jnp.bfloat16)
    buffer = jnp.dot(dispatch, normed_two, preferred_element_type=jnp.float32).astype(jnp.bfloat16)
    arrived = lax.all_to_all(
        buffer.reshape(head_count, experts_local, CAP, MODEL_WIDTH),
        "head",
        split_axis=0,
        concat_axis=0,
        tiled=True,
    )
    gate_pre = jnp.einsum("secd,edf->secf", arrived, gate_all, preferred_element_type=jnp.float32)
    up_pre = jnp.einsum("secd,edf->secf", arrived, up_all, preferred_element_type=jnp.float32)
    sigma = jax.nn.sigmoid(gate_pre)
    swish = gate_pre * sigma
    activated = (swish * up_pre).astype(jnp.bfloat16)
    expert_out = jnp.einsum(
        "secf,efd->secd", activated, down_all, preferred_element_type=jnp.float32
    ).astype(jnp.bfloat16)
    returned = lax.all_to_all(expert_out, "head", split_axis=0, concat_axis=0, tiled=True).reshape(
        E * CAP, MODEL_WIDTH
    )
    picked = returned[jnp.where(kept, target, 0)].astype(jnp.float32)
    mixed = jnp.sum(jnp.where(kept, gates, 0.0)[..., None] * picked, axis=1)
    output = (middle + mixed).astype(jnp.bfloat16)
    query_all, key_all, value_all, out_all = fetch_attention(
        w_query, key_weight, value_weight, w_out
    )
    gate_all, up_all, down_all = fetch_experts(w_gate, w_up, w_down)
    keys_all, values_all = fetch_keys(rotated_key, value_rows)
    upstream = grad_out.astype(jnp.float32)
    d_gates = jnp.where(kept, jnp.sum(picked * upstream[:, None, :], axis=-1), 0.0)
    token_ids = jnp.broadcast_to(jnp.arange(rows, dtype=jnp.int32)[:, None], (rows, TOPK))
    slot_token = jnp.sum(jnp.where(match, token_ids[None], 0), axis=(1, 2))
    slot_gate = jnp.sum(jnp.where(match, gates[None], 0.0), axis=(1, 2))
    d_slots = (slot_gate[:, None] * upstream[slot_token]).astype(jnp.bfloat16)
    d_returned = lax.all_to_all(
        d_slots.reshape(head_count, experts_local, CAP, MODEL_WIDTH),
        "head",
        split_axis=0,
        concat_axis=0,
        tiled=True,
    )
    d_activated = jnp.einsum(
        "secd,efd->secf", d_returned, down_all, preferred_element_type=jnp.float32
    )
    d_gate_pre = (d_activated * up_pre * sigma * (1.0 + gate_pre * (1.0 - sigma))).astype(
        jnp.bfloat16
    )
    d_up_pre = (d_activated * swish).astype(jnp.bfloat16)
    d_arrived = jnp.einsum(
        "secf,edf->secd", d_gate_pre, gate_all, preferred_element_type=jnp.float32
    )
    d_arrived = (
        d_arrived
        + jnp.einsum("secf,edf->secd", d_up_pre, up_all, preferred_element_type=jnp.float32)
    ).astype(jnp.bfloat16)
    d_buffer = lax.all_to_all(d_arrived, "head", split_axis=0, concat_axis=0, tiled=True).reshape(
        E * CAP, MODEL_WIDTH
    )
    d_normed_two = along_rows(dispatch, d_buffer)
    weighted = jnp.sum(gates * d_gates, axis=-1, keepdims=True)
    d_chosen = gates * (d_gates - weighted)
    route_hits = routes[..., None] == jnp.arange(E, dtype=jnp.int32)[None, None, :]
    d_logits = jnp.sum(jnp.where(route_hits, d_chosen[..., None], 0.0), axis=1)
    router_wide = router.astype(jnp.float32)
    d_normed_two = d_normed_two + lax.dot_general(
        d_logits, router_wide, (((1,), (1,)), ((), ())), precision=lax.Precision.HIGHEST
    )
    grad_router = lax.dot_general(
        normed_two.astype(jnp.float32),
        d_logits,
        (((0,), (0,)), ((), ())),
        precision=lax.Precision.HIGHEST,
    )
    weighted_two = d_normed_two * w_norm2
    grad_norm2 = jnp.sum(d_normed_two * unit_two, axis=0)
    d_middle = upstream + scale_two * (
        weighted_two - unit_two * jnp.mean(unit_two * weighted_two, axis=-1, keepdims=True)
    )
    d_branch = lax.all_gather(d_middle.astype(jnp.bfloat16), "head", axis=0, tiled=True)
    grad_out_w = along_rows(attended_rows, d_branch)
    d_attended = against(d_branch, out_all).astype(jnp.bfloat16)
    d_heads = d_attended.reshape(group_rows, kv_local, head_groups, HEAD_SIZE)
    delta = jnp.transpose(jnp.sum(d_heads.astype(jnp.float32) * attended32, axis=-1), (1, 2, 0))

    def back_step(acc, index):
        scores, allowed, key_block, value_block = block_scores(keys_all, values_all, index)
        probs = jnp.where(allowed, jnp.exp(scores - log_total[..., None]), 0.0)
        d_probs = jnp.einsum(
            "qhgd,khd->hgqk", d_heads, value_block, preferred_element_type=jnp.float32
        )
        d_scores = (probs * (d_probs - delta[..., None])).astype(jnp.bfloat16)
        acc = acc + jnp.einsum(
            "hgqk,khd->qhgd", d_scores, key_block, preferred_element_type=jnp.float32
        )
        d_keys = (
            jnp.einsum("hgqk,qhgd->khd", d_scores, query_heads, preferred_element_type=jnp.float32)
            * scale
        )
        d_values = jnp.einsum(
            "hgqk,qhgd->khd",
            probs.astype(jnp.bfloat16),
            d_heads,
            preferred_element_type=jnp.float32,
        )
        return (
            acc,
            (
                d_keys.reshape(group_rows, kv_local * HEAD_SIZE),
                d_values.reshape(group_rows, kv_local * HEAD_SIZE),
            ),
        )

    d_query_acc, (key_pieces, value_pieces) = lax.scan(
        back_step, jnp.zeros((group_rows, kv_local, head_groups, HEAD_SIZE), jnp.float32), steps
    )
    d_key_rot, d_value_sum = (
        lax.psum_scatter(
            key_pieces.reshape(blk_count * group_rows, kv_local * HEAD_SIZE).astype(jnp.bfloat16),
            "blk",
            scatter_dimension=0,
            tiled=True,
        ).astype(jnp.float32),
        lax.psum_scatter(
            value_pieces.reshape(blk_count * group_rows, kv_local * HEAD_SIZE).astype(jnp.bfloat16),
            "blk",
            scatter_dimension=0,
            tiled=True,
        ).astype(jnp.float32),
    )
    d_query = (
        turn_index(
            d_query_acc.reshape(group_rows, heads_local, HEAD_SIZE) * scale,
            cosine_table,
            -sine_table,
        )
        .reshape(group_rows, heads_local * HEAD_SIZE)
        .astype(jnp.bfloat16)
    )
    d_key = (
        turn_index(d_key_rot.reshape(group_rows, kv_local, HEAD_SIZE), cosine_table, -sine_table)
        .reshape(group_rows, kv_local * HEAD_SIZE)
        .astype(jnp.bfloat16)
    )
    d_value = d_value_sum.astype(jnp.bfloat16)
    grad_query_w = along_rows(gathered, d_query)
    grad_key_w = along_rows(gathered, d_key)
    grad_value_w = along_rows(gathered, d_value)
    total = against(d_query, query_all)
    total = total + against(d_key, key_all)
    d_normed = lax.psum_scatter(
        (total + against(d_value, value_all)).astype(jnp.bfloat16),
        "head",
        scatter_dimension=0,
        tiled=True,
    ).astype(jnp.float32)
    weighted_one = d_normed * w_norm1
    grad_norm1 = jnp.sum(d_normed * unit_one, axis=0)
    grad_inputs = d_middle + scale_one * (
        weighted_one - unit_one * jnp.mean(unit_one * weighted_one, axis=-1, keepdims=True)
    )
    grad_gate = jnp.einsum(
        "secd,secf->edf", arrived, d_gate_pre, preferred_element_type=jnp.float32
    )
    grad_up = jnp.einsum("secd,secf->edf", arrived, d_up_pre, preferred_element_type=jnp.float32)
    grad_down = jnp.einsum(
        "secf,secd->efd", activated, d_returned, preferred_element_type=jnp.float32
    )
    sharded = (
        lax.psum_scatter(
            grad_query_w.astype(jnp.bfloat16), "blk", scatter_dimension=0, tiled=True
        ).astype(jnp.float32),
        lax.psum_scatter(
            grad_key_w.astype(jnp.bfloat16), "blk", scatter_dimension=0, tiled=True
        ).astype(jnp.float32),
        lax.psum_scatter(
            grad_value_w.astype(jnp.bfloat16), "blk", scatter_dimension=0, tiled=True
        ).astype(jnp.float32),
        lax.psum_scatter(
            grad_out_w.astype(jnp.bfloat16), "blk", scatter_dimension=1, tiled=True
        ).astype(jnp.float32),
        lax.psum_scatter(
            grad_gate.astype(jnp.bfloat16), "blk", scatter_dimension=1, tiled=True
        ).astype(jnp.float32),
        lax.psum_scatter(
            grad_up.astype(jnp.bfloat16), "blk", scatter_dimension=1, tiled=True
        ).astype(jnp.float32),
        lax.psum_scatter(
            grad_down.astype(jnp.bfloat16), "blk", scatter_dimension=2, tiled=True
        ).astype(jnp.float32),
    )
    small = lax.psum((grad_norm1, grad_norm2, grad_router), ("blk", "head"))
    return (
        output,
        grad_inputs,
        small[0],
        sharded[0],
        sharded[1],
        sharded[2],
        sharded[3],
        small[1],
        small[2],
        sharded[4],
        sharded[5],
        sharded[6],
    )


def solution(mesh):
    return jax.shard_map(
        on_device,
        mesh=mesh,
        in_specs=(
            P(("blk", "head"), None),
            P(),
            P(),
            P(),
            P("blk", "head"),
            P("blk", "head"),
            P("blk", "head"),
            P("head", "blk"),
            P(),
            P(),
            P(("blk", "head"), None),
            P(("blk", "head"), None),
            P("head", "blk", None),
            P("head", "blk", None),
            P("head", None, "blk"),
            P(("blk", "head"), None),
        ),
        out_specs=(
            P(("blk", "head"), None),
            P(("blk", "head"), None),
            P(),
            P("blk", "head"),
            P("blk", "head"),
            P("blk", "head"),
            P("head", "blk"),
            P(),
            P(),
            P("head", "blk", None),
            P("head", "blk", None),
            P("head", None, "blk"),
        ),
        check_vma=False,
    )
```

profile of v0, /device:TPU:0, one launch (start us, length us, event | category | flops | bytes accessed | tf_op | source)
XLA Modules:
  0.0 1356.6 jit_solution(968035119991813735)
XLA Ops:
  14.0 16.1 %all_gather.45 = bf16[1024,128]{1,0:T(8,128)(2,1)S(1)} all-gather(bf16[128,128]{1,0:T(8,128)(2,1)} %param.27), channel_id=1, replica_groups=mesh['blk'=8,'head'=4] {'blk'}, dimensions={0}, use_global_device_ids=true | all-gather | bytes 294912 | tf_op jit(solution)/shard_map/all_gather | solution.py:73
  42.8 14.6 %all_gather.43 = bf16[1024,128]{1,0:T(8,128)(2,1)S(1)} all-gather(bf16[128,128]{1,0:T(8,128)(2,1)S(1)} %copy-done.46), channel_id=1, replica_groups=mesh['blk'=8,'head'=4] {'blk'}, dimensions={0}, use_global_device_ids=true | all-gather | bytes 294912 | tf_op jit(solution)/shard_map/all_gather | solution.py:74
  57.5 15.5 %all_gather.47 = bf16[1024,256]{1,0:T(8,128)(2,1)S(1)} all-gather(bf16[128,256]{1,0:T(8,128)(2,1)S(1)} %copy-done.41), channel_id=1, replica_groups=mesh['blk'=8,'head'=4] {'blk'}, dimensions={0}, use_global_device_ids=true | all-gather | bytes 589824 | tf_op jit(solution)/shard_map/all_gather | solution.py:72
  72.9 13.7 %all_gather.48 = bf16[256,1024]{1,0:T(8,128)(2,1)S(1)} all-gather(bf16[256,128]{1,0:T(8,128)(2,1)S(1)} %copy-done.42), channel_id=1, replica_groups=mesh['blk'=8,'head'=4] {'blk'}, dimensions={1}, use_global_device_ids=true | all-gather | bytes 589824 | tf_op jit(solution)/shard_map/all_gather | solution.py:75
  88.5 74.8 %while.39 = (s32[]{:T(128)}, f32[2,2,512]{2,1,0:T(2,128)S(1)}, f32[2,2,512]{2,1,0:T(2,128)S(1)}, s32[8]{0:T(128)S(1)}, s32[4096]{0:T(1024)}, /*index=5*/s32[512]...) while((s32[]{:T(128)}, f32[2,2,512]{2,1,0:T(2,128)S(1)}, ...), condition=%wide.region_6.7_spmd.clone, body=%wide.region_3.6_spmd.clone.sunk | while | flops 143403008 | bytes 9947346 | solution.py:182
  165.6 37.2 %while.40 = (s32[]{:T(128)}, f32[512,2,2,64]{0,3,2,1:T(8,128)S(1)}, s32[8]{0:T(128)S(1)}, bf16[4096,128]{0,1:T(8,128)(2,1)}, s32[4096]{0:T(1024)}, /*index=5*/s3...) while((s32[]{:T(128)}, f32[512,2,2,64]{0,3,2,1:T(8,128)S(1)}, ...), condition=%wide.region_8.9_spmd.clone, body=%wide.region_7.8_spmd.clone.sunk | while | flops 273678336 | bytes 2640089 | solution.py:193
  266.0 23.7 %select_reduce_fusion.1 = s32[1280]{0:T(1024)S(1)} fusion(s32[128,8]{0,1:T(8,128)S(1)} %get-tuple-element.546, pred[128,8]{0,1:T(8,128)(4,1)S(1)} %get-tuple-element.544), kind=kLoop, calls=%fused_computation.66 | loop fusion | flops 5241600 | bytes 10240 | tf_op jit(solution)/shard_map/reduce_sum | solution.py:245
  321.9 75.7 %all-gather.14.cloned.1.call-done = bf16[8,1024,512]{2,1,0:T(8,128)(2,1)} async-done(((bf16[8,128,512]{2,1,0:T(8,128)(2,1)}), bf16[8,1024,512]{2,1,0:T(8,128)(2,1)}) %all-gather.14.cloned.1.call-update) | async-done | bytes 8388624 | tf_op jit(solution)/shard_map/all_gather | solution.py:81
  404.1 76.2 %all-gather.18.cloned.1.call-done = bf16[8,512,1024]{2,1,0:T(8,128)(2,1)} async-done(((bf16[8,512,128]{2,1,0:T(8,128)(2,1)}), bf16[8,512,1024]{2,1,0:T(8,128)(2,1)}) %all-gather.18.cloned.1.call-update) | async-done | bytes 8388624 | tf_op jit(solution)/shard_map/all_gather | solution.py:83
  517.7 24.0 %all-to-all-done.3 = bf16[4,8,40,1024]{3,2,1,0:T(8,128)(2,1)} async-done(((bf16[4,8,40,1024]{3,2,1,0:T(8,128)(2,1)}), bf16[4,8,40,1024]{3,2,1,0:T(8,128)(2,1)}, u32[]{:S(2)}, u32[]{:S(2)}) %all-to-all-start.3) | async-done | bytes 2621472 | tf_op jit(solution)/shard_map/all_to_all | solution.py:269
  550.9 24.8 %all-to-all-done.1 = bf16[4,8,40,1024]{3,2,1,0:T(8,128)(2,1)S(1)} async-done(((bf16[4,8,40,1024]{3,2,1,0:T(8,128)(2,1)}), bf16[4,8,40,1024]{3,2,1,0:T(8,128)(2,1)S(1)}, u32[]{:S(2)}, u32[]{:S(2)}) %all-to-all-start.1) | async-done | bytes 2621472 | tf_op jit(solution)/shard_map/all_to_all | solution.py:231
  587.2 24.6 %all-gather.20.cloned.1.call-done = bf16[512,1024]{1,0:T(8,128)(2,1)} async-done(((bf16[128,1024]{1,0:T(8,128)(2,1)}), bf16[512,1024]{1,0:T(8,128)(2,1)}) %all-gather.20.cloned.1.call-update) | async-done | bytes 1048592 | tf_op jit(solution)/shard_map/all_gather | solution.py:292
  614.4 113.1 %while.41 = (s32[]{:T(128)}, f32[512,2,2,64]{0,3,2,1:T(8,128)S(1)}, bf16[8,512,128]{2,1,0:T(8,128)(2,1)}, bf16[8,512,128]{2,1,0:T(8,128)(2,1)}, s32[8]{0:T(128)S...) while((s32[]{:T(128)}, f32[512,2,2,64]{0,3,2,1:T(8,128)S(1)}, ...), condition=%wide.region_27.28_spmd.clone, body=%wide.region_26.27_spmd.clone.sunk | while | flops 682754048 | bytes 43944304 | solution.py:326
  732.6 27.3 %reduce-scatter.18.cloned.1.call-done = bf16[512,128]{1,0:T(8,128)(2,1)} async-done(((bf16[4096,128]{1,0:T(8,128)(2,1)}), bf16[512,128]{1,0:T(8,128)(2,1)}) %reduce-scatter.18.cloned.1.call-update) | async-done | bytes 131088 | tf_op jit(solution)/shard_map/reduce_scatter | solution.py:330
  762.5 30.3 %reduce-scatter.20.cloned.1.call-done = bf16[512,128]{1,0:T(8,128)(2,1)} async-done(((bf16[4096,128]{1,0:T(8,128)(2,1)}), bf16[512,128]{1,0:T(8,128)(2,1)}) %reduce-scatter.20.cloned.1.call-update) | async-done | bytes 131088 | tf_op jit(solution)/shard_map/reduce_scatter | solution.py:336
  807.4 12.6 copy.228
  857.9 30.0 %reduce-scatter.26.cloned.1.call-done = bf16[128,128]{1,0:T(8,128)(2,1)} async-done(((bf16[1024,128]{1,0:T(8,128)(2,1)}), bf16[128,128]{1,0:T(8,128)(2,1)}) %reduce-scatter.26.cloned.1.call-update) | async-done | bytes 32784 | tf_op jit(solution)/shard_map/reduce_scatter | solution.py:385
  889.3 29.2 %reduce-scatter.28.cloned.1.call-done = bf16[128,128]{1,0:T(8,128)(2,1)} async-done(((bf16[1024,128]{1,0:T(8,128)(2,1)}), bf16[128,128]{1,0:T(8,128)(2,1)}) %reduce-scatter.28.cloned.1.call-update) | async-done | bytes 32784 | tf_op jit(solution)/shard_map/reduce_scatter | solution.py:388
  919.9 28.1 %reduce-scatter.22.cloned.1.call-done = bf16[128,1024]{1,0:T(8,128)(2,1)} async-done(((bf16[512,1024]{1,0:T(8,128)(2,1)}), bf16[128,1024]{1,0:T(8,128)(2,1)}) %reduce-scatter.22.cloned.1.call-update) | async-done | bytes 262160 | tf_op jit(solution)/shard_map/reduce_scatter | solution.py:363
  951.5 41.3 %all-reduce = (f32[1024]{0:T(1024)}, f32[1024]{0:T(1024)}) all-reduce(f32[1024]{0:T(1024)S(1)} %get-tuple-element.472, f32[1024]{0:T(1024)S(1)} %get-tuple-element.470), channel_id=1, replica_groups=mesh['blk'=8,'head'=4] {'blk','head'}, use_global_device_ids=true, to_apply=%region_33.34 | all-reduce | flops 2048 | bytes 16384 | tf_op jit(solution)/shard_map/psum | solution.py:404
  992.8 48.0 %reduce-scatter.36.cloned.1.call-done = bf16[128,4096]{1,0:T(8,128)(2,1)} async-done(((bf16[1024,4096]{1,0:T(8,128)(2,1)}), bf16[128,4096]{1,0:T(8,128)(2,1)}) %reduce-scatter.36.cloned.1.call-update) | async-done | bytes 1048592
  1044.9 86.0 %reduce-scatter.30.cloned.1.call-done = bf16[8,128,512]{2,1,0:T(8,128)(2,1)} async-done(((bf16[8,1024,512]{2,1,0:T(8,128)(2,1)}), bf16[8,128,512]{2,1,0:T(8,128)(2,1)}) %reduce-scatter.30.cloned.1.call-update) | async-done | bytes 1048592 | tf_op jit(solution)/shard_map/reduce_scatter | solution.py:394
  1133.8 87.3 %reduce-scatter.32.cloned.1.call-done = bf16[8,128,512]{2,1,0:T(8,128)(2,1)} async-done(((bf16[8,1024,512]{2,1,0:T(8,128)(2,1)}), bf16[8,128,512]{2,1,0:T(8,128)(2,1)}) %reduce-scatter.32.cloned.1.call-update) | async-done | bytes 1048592 | tf_op jit(solution)/shard_map/reduce_scatter | solution.py:397
  1223.9 124.1 %all-reduce.3.cloned.1.call-done = f32[1024,32]{0,1:T(8,128)} async-done(((f32[1024,32]{0,1:T(8,128)}), f32[1024,32]{0,1:T(8,128)}) %all-reduce.3.cloned.1.call-update) | async-done | bytes 131088 | tf_op jit(solution)/shard_map/psum | solution.py:404
  (568 shorter events, 470.6 us)
Async XLA Ops:
  7.2 33.0 %all-gather.8.cloned.1.call-start = ((), (), s32[]{:S(2)}) async-start(), calls=%async_computation.15 | async-start | bytes 1310720 | tf_op jit(solution)/shard_map/all_gather | solution.py:129
  10.7 77.7 %all-gather.12.cloned.1.call-start = ((), (), s32[]{:S(2)}) async-start(), calls=%async_computation.17 | async-start | bytes 1179648 | tf_op jit(solution)/shard_map/all_gather | solution.py:89
  42.8 120.6 %all-gather.10.cloned.1.call-start = ((), (), s32[]{:S(2)}) async-start(), calls=%async_computation.16 | async-start | bytes 1179648 | tf_op jit(solution)/shard_map/all_gather | solution.py:90
  88.4 143.4 %reduce-scatter.16.cloned.1.call-start = ((), (), s32[]{:S(2)}) async-start(), calls=%async_computation.18 | async-start | bytes 1310720 | tf_op jit(solution)/shard_map/reduce_scatter | solution.py:197
  204.4 111.0 %all-gather.16.cloned.1.call-start = ((), (), s32[]{:S(2)}) async-start(), calls=%async_computation.20 | async-start | bytes 9437184 | tf_op jit(solution)/shard_map/all_gather | solution.py:82
  205.0 192.6 %all-gather.14.cloned.1.call-start = ((), (), s32[]{:S(2)}) async-start(), calls=%async_computation.19 | async-start | bytes 9437184 | tf_op jit(solution)/shard_map/all_gather | solution.py:81
  205.6 274.7 %all-gather.18.cloned.1.call-start = ((), (), s32[]{:S(2)}) async-start(), calls=%async_computation.21 | async-start | bytes 9437184 | tf_op jit(solution)/shard_map/all_gather | solution.py:83
  251.7 48.1 %all-to-all-start = ((bf16[4,8,40,1024]{3,2,1,0:T(8,128)(2,1)}), bf16[4,8,40,1024]{3,2,1,0:T(8,128)(2,1)S(1)}, u32[]{:S(2)}, u32[]{:S(2)}) async-start(bf16[4,8,40,1024]{3,2,1,0:T(8,128)(2,1)} %bitcast.350), calls=%async_computation.1 | async-start | bytes 5242880 | tf_op jit(solution)/shard_map/all_to_all | solution.py:216
  299.8 104.3 %all-to-all-start.2 = ((bf16[4,8,40,1024]{3,2,1,0:T(8,128)(2,1)}), bf16[4,8,40,1024]{3,2,1,0:T(8,128)(2,1)}, u32[]{:S(2)}, u32[]{:S(2)}) async-start(bf16[4,8,40,1024]{3,2,1,0:T(8,128)(2,1)} %multiply_convert_fusion), calls=%async_computation.3 | async-start | bytes 5242880 | tf_op jit(solution)/shard_map/all_to_all | solution.py:248
  505.7 36.0 %all-to-all-start.3 = ((bf16[4,8,40,1024]{3,2,1,0:T(8,128)(2,1)}), bf16[4,8,40,1024]{3,2,1,0:T(8,128)(2,1)}, u32[]{:S(2)}, u32[]{:S(2)}) async-start(bf16[4,8,40,1024]{3,2,1,0:T(8,128)(2,1)} %copy.202), calls=%async_computation.4 | async-start | bytes 5242880 | tf_op jit(solution)/shard_map/all_to_all | solution.py:269
  541.7 34.0 %all-to-all-start.1 = ((bf16[4,8,40,1024]{3,2,1,0:T(8,128)(2,1)}), bf16[4,8,40,1024]{3,2,1,0:T(8,128)(2,1)S(1)}, u32[]{:S(2)}, u32[]{:S(2)}) async-start(bf16[4,8,40,1024]{3,2,1,0:T(8,128)(2,1)} %copy.199), calls=%async_computation.2 | async-start | bytes 5242880 | tf_op jit(solution)/shard_map/all_to_all | solution.py:231
  545.4 66.4 %all-gather.20.cloned.1.call-start = ((), (), s32[]{:S(2)}) async-start(), calls=%async_computation.22 | async-start | bytes 1310720 | tf_op jit(solution)/shard_map/all_gather | solution.py:292
  587.1 172.8 %reduce-scatter.18.cloned.1.call-start = ((), (), s32[]{:S(2)}) async-start(), calls=%async_computation.23 | async-start | bytes 1179648 | tf_op jit(solution)/shard_map/reduce_scatter | solution.py:330
  727.5 65.3 %reduce-scatter.20.cloned.1.call-start = ((), (), s32[]{:S(2)}) async-start(), calls=%async_computation.24 | async-start | bytes 1179648 | tf_op jit(solution)/shard_map/reduce_scatter | solution.py:336
  728.1 121.9 %reduce-scatter.34.cloned.1.call-start = ((), (), s32[]{:S(2)}) async-start(), calls=%async_computation.32 | async-start | bytes 589824
  731.0 125.3 %reduce-scatter.24.cloned.1.call-start = ((), (), s32[]{:S(2)}) async-start(), calls=%async_computation.26 | async-start | bytes 589824 | tf_op jit(solution)/shard_map/reduce_scatter | solution.py:382
  732.6 155.3 %reduce-scatter.26.cloned.1.call-start = ((), (), s32[]{:S(2)}) async-start(), calls=%async_computation.27 | async-start | bytes 294912 | tf_op jit(solution)/shard_map/reduce_scatter | solution.py:385
  762.2 156.3 %reduce-scatter.28.cloned.1.call-start = ((), (), s32[]{:S(2)}) async-start(), calls=%async_computation.28 | async-start | bytes 294912 | tf_op jit(solution)/shard_map/reduce_scatter | solution.py:388
  796.5 151.5 %reduce-scatter.22.cloned.1.call-start = ((), (), s32[]{:S(2)}) async-start(), calls=%async_computation.25 | async-start | bytes 1310720 | tf_op jit(solution)/shard_map/reduce_scatter | solution.py:363
  799.5 241.3 %reduce-scatter.36.cloned.1.call-start = ((), (), s32[]{:S(2)}) async-start(), calls=%async_computation.33 | async-start | bytes 9437184
  832.3 298.7 %reduce-scatter.30.cloned.1.call-start = ((), (), s32[]{:S(2)}) async-start(), calls=%async_computation.30 | async-start | bytes 9437184 | tf_op jit(solution)/shard_map/reduce_scatter | solution.py:394
  841.0 380.1 %reduce-scatter.32.cloned.1.call-start = ((), (), s32[]{:S(2)}) async-start(), calls=%async_computation.31 | async-start | bytes 9437184 | tf_op jit(solution)/shard_map/reduce_scatter | solution.py:397
  848.2 499.8 %all-reduce.3.cloned.1.call-start = ((), (), s32[]{:S(2)}) async-start(), calls=%async_computation.29 | async-start | bytes 262144 | tf_op jit(solution)/shard_map/psum | solution.py:404
  1043.5 306.1 %copy-start.1 = (bf16[1024,32]{0,1:T(8,128)(2,1)S(1)}, bf16[1024,32]{0,1:T(8,128)(2,1)}, u32[]{:S(2)}) copy-start(bf16[1024,32]{0,1:T(8,128)(2,1)} %param.31) | copy-start | bytes 196612
  (84 other events, 1886.5 us)
Sparse Core Ops, SparseCore 0:
  10.9 29.3 all-gather.7
  42.9 23.2 all-gather.11
  88.5 21.6 all-gather.9
  204.5 27.2 reduce-scatter.15
  233.3 82.0 all-gather.15
  317.0 80.5 all-gather.13
  399.3 81.0 all-gather.17
  587.2 24.5 all-gather.19
  727.6 32.2 reduce-scatter.17
  762.2 30.6 reduce-scatter.19
  795.2 29.1 reduce-scatter.33
  827.1 29.2 reduce-scatter.23
  859.3 28.5 reduce-scatter.25
  890.0 28.4 reduce-scatter.27
  922.1 25.8 reduce-scatter.21
  950.1 90.6 reduce-scatter.35
  1043.0 87.9 reduce-scatter.29
  1133.1 87.9 reduce-scatter.31
  1227.2 120.7 all-reduce.2
where the time goes:
time: 1370 us; the launch traced here: 1360 us
  waiting for transfers between devices  745 us (54%)
  matrix products  182 us (13%)
  local copies, waits for them, and re-layouts  159 us (12%)
  other arithmetic  120 us (9%)
  blocking collectives  101 us (7%)
  starting transfers between devices  17.9 us (1%)
  loops' own time  17.3 us (1%)
  between operations  15.5 us (1%)
    psum x1, waiting for transfers between devices, on_device(): small = lax.psum((grad_norm1, grad_norm2, grad_router), ('blk', 'head'))  124 us
    reduce_scatter x1, waiting for transfers between devices, on_device(): lax.psum_scatter(grad_up.astype(jnp.bfloat16), 'blk', scatter_dimension=1...  87.3 us
    reduce_scatter x1, waiting for transfers between devices, on_device(): lax.psum_scatter(grad_gate.astype(jnp.bfloat16), 'blk', scatter_dimension...  86 us
    all_gather x1, waiting for transfers between devices, fetch_experts(): lax.all_gather(w_down, 'blk', axis=2, tiled=True)  76.2 us
    all_gather x1, waiting for transfers between devices, fetch_experts(): lax.all_gather(w_gate, 'blk', axis=1, tiled=True)  75.7 us
    unnamed x21, waiting for transfers between devices  50.6 us
    psum x1, blocking collectives, on_device(): small = lax.psum((grad_norm1, grad_norm2, grad_router), ('blk', 'head'))  41.3 us
    unnamed x116, local copies, waits for them, and re-layouts  37 us
  transfers between devices with their start and end apart: 23, of which 18 were waited for; matrix products, arithmetic and copies ran while one was open for 20% of the time, Pallas kernels for 0%

commit v1 on v0

--- a/solution.py
+++ b/solution.py
@@ -1,8 +1,11 @@
+import functools
 import math
 
 import jax
 import jax.numpy as jnp
 from jax import lax
+from jax.experimental import pallas as pl
+from jax.experimental.pallas import tpu as pltpu
 from jax.sharding import PartitionSpec as P
 
 MODEL_WIDTH = 1024
@@ -10,10 +13,418 @@
 E = 32
 TOPK = 8
 CAP = 40
-
+MESH = pl.DeviceIdType.MESH
+VMEM = pl.BlockSpec(memory_space=pltpu.VMEM)
+ANY = pl.BlockSpec(memory_space=pl.ANY)
+BF = jnp.bfloat16
+F32 = jnp.float32
 
 eps = 1e-06
 rope_base = 10000.0
+
+
+def nn(a, b, **kw):
+    return lax.dot_general(a, b, (((1,), (0,)), ((), ())), preferred_element_type=F32, **kw)
+
+
+def nt(a, b, **kw):
+    return lax.dot_general(a, b, (((1,), (1,)), ((), ())), preferred_element_type=F32, **kw)
+
+
+def tn(a, b, **kw):
+    return lax.dot_general(a, b, (((0,), (0,)), ((), ())), preferred_element_type=F32, **kw)
+
+
+def remote(src, dst, send, recv, device):
+    return pltpu.make_async_remote_copy(
+        src_ref=src,
+        dst_ref=dst,
+        send_sem=send,
+        recv_sem=recv,
+        device_id=device,
+        device_id_type=MESH,
+    )
+
+
+class Place:
+    def __init__(self, nb, nh):
+        self.nb, self.nh, self.nz = nb, nh, nb // 2
+        self.b, self.h = lax.axis_index("blk"), lax.axis_index("head")
+        self.z, self.core = self.b // 2, lax.rem(self.b, 2)
+        self.sibling = 2 * self.z + 1 - self.core
+
+    def in_blk(self, b):
+        return (b, self.h)
+
+    def in_head(self, h):
+        return (self.b, h)
+
+    def head_peer(self, k):
+        return lax.rem(self.h + k, self.nh)
+
+    def blk_peer(self, k):
+        return lax.rem(self.b + k, self.nb)
+
+    def meet(self):
+        barrier = pltpu.get_barrier_semaphore()
+        for k in range(1, self.nh):
+            pl.semaphore_signal(
+                barrier, inc=1, device_id=self.in_head(self.head_peer(k)), device_id_type=MESH
+            )
+        for k in range(1, self.nb):
+            pl.semaphore_signal(
+                barrier, inc=1, device_id=self.in_blk(self.blk_peer(k)), device_id_type=MESH
+            )
+        pl.semaphore_wait(barrier, self.nh + self.nb - 2)
+
+
+class Relay:
+    def __init__(self, at, buf, send, recv):
+        self.at, self.buf, self.send, self.recv = at, buf, send, recv
+
+    def copy(self, s, way, device):
+        return remote(
+            self.buf.at[s], self.buf.at[s], self.send.at[way, s], self.recv.at[s], device
+        )
+
+    def right(self, s):
+        return self.copy(s, 0, self.at.in_blk(jnp.minimum(self.at.b + 2, self.at.nb - 2 + self.at.core)))
+
+    def left(self, s):
+        return self.copy(s, 1, self.at.in_blk(jnp.maximum(self.at.b - 2, self.at.core)))
+
+    def across(self, s):
+        return self.copy(s, 2, self.at.in_blk(self.at.sibling))
+
+    def begin(self):
+        at = self.at
+        pl.when(at.z + 1 < at.nz)(lambda: self.right(at.b).start())
+        pl.when(at.z > 0)(lambda: self.left(at.b).start())
+        self.across(at.b).start()
+
+    def hop(self, i):
+        at = self.at
+
+        @pl.when(at.z >= i)
+        def _():
+            s = at.b - 2 * i
+            self.across(s).wait_recv()
+            pl.when(at.z + 1 < at.nz)(lambda: self.right(s).start())
+            self.across(s).start()
+
+        @pl.when(at.z + i < at.nz)
+        def _():
+            s = at.b + 2 * i
+            self.across(s).wait_recv()
+            pl.when(at.z > 0)(lambda: self.left(s).start())
+            self.across(s).start()
+
+    def take_sibling(self, z):
+        self.across(2 * z + 1 - self.at.core).wait_recv()
+
+    def finish(self):
+        at = self.at
+        for i in range(at.nz):
+
+            @pl.when(at.z >= i)
+            def _():
+                s = at.b - 2 * i
+                pl.when(at.z + 1 < at.nz)(lambda: self.right(s).wait_send())
+                self.across(s).wait_send()
+
+            if i == 0:
+                pl.when(at.z > 0)(lambda: self.left(at.b).wait_send())
+            else:
+
+                @pl.when(at.z + i < at.nz)
+                def _():
+                    s = at.b + 2 * i
+                    pl.when(at.z > 0)(lambda: self.left(s).wait_send())
+                    self.across(s).wait_send()
+
+    def all(self):
+        self.begin()
+        for i in range(1, self.at.nz):
+            self.hop(i)
+        for z in range(self.at.nz):
+            self.take_sibling(z)
+
+
+def sorted_place(at, half, shape, axis):
+    s = lax.broadcasted_iota(jnp.int32, shape, axis)
+    return jnp.where(
+        s < half, at.b * half + s, (2 * at.nb - 1 - at.b) * half + s - half
+    )
+
+
+def block_base(at, b, second, half):
+    return jnp.where(second == 0, b * half, (2 * at.nb - 1 - b) * half)
+
+
+def turn_rows(values, cos, sin):
+    half = HEAD_SIZE // 2
+    pieces = []
+    for first in range(0, values.shape[0], HEAD_SIZE):
+        lead = values[first : first + half]
+        trail = values[first + half : first + HEAD_SIZE]
+        pieces.append(lead * cos - trail * sin)
+        pieces.append(trail * cos + lead * sin)
+    return jnp.concatenate(pieces, axis=0)
+
+
+def front_kernel(
+    nb,
+    nh,
+    hl,
+    kl,
+    inputs,
+    w_norm1,
+    w_norm2,
+    w_own,
+    place_row,
+    place_col,
+    cos,
+    sin,
+    begin,
+    xg,
+    wg,
+    qn,
+    kv,
+    lse,
+    attn_t,
+    ao,
+    middle,
+    n2,
+    qt,
+    perm,
+    top,
+    total,
+    out_send,
+    out_recv,
+    x_sems,
+    w_send,
+    w_recv,
+    kv_send,
+    kv_recv,
+    o_sems,
+):
+    at = Place(nb, nh)
+    rows = inputs.shape[0]
+    group = rows * nh
+    half = group // 2
+    qw, kw = hl * HEAD_SIZE, kl * HEAD_SIZE
+    width = qw + 2 * kw
+
+    hidden = inputs[...].astype(F32)
+    unit = hidden * lax.rsqrt(jnp.mean(hidden * hidden, axis=-1, keepdims=True) + eps)
+    xg[at.h] = (unit * w_norm1[...]).astype(BF)
+    wg[at.b] = w_own[...]
+    at.meet()
+    x_copies = [
+        remote(xg.at[at.h], xg.at[at.h], x_sems.at[0, k], x_sems.at[1, k], at.in_head(at.head_peer(k)))
+        for k in range(1, nh)
+    ]
+    for c in x_copies:
+        c.start()
+    weights = Relay(at, wg, w_send, w_recv)
+    weights.begin()
+    perm[...] = jnp.where(
+        place_row[...] == sorted_place(at, half, (group, group), 0), 1.0, 0.0
+    ).astype(BF)
+    for i in range(1, nb // 2):
+        weights.hop(i)
+    for z in range(nb // 2):
+        weights.take_sibling(z)
+    for c in x_copies:
+        c.wait_recv()
+    x = xg[...].reshape(group, MODEL_WIDTH)
+    w = wg[...].reshape(MODEL_WIDTH, width + qw)
+    qkv_t = nn(x, w[:, :width]).T
+    qkv_t = jnp.concatenate(
+        [turn_rows(qkv_t[: qw + kw], cos[...], sin[...]), qkv_t[qw + kw :]], axis=0
+    ).astype(BF)
+    order = perm[...]
+    kv_rows = nt(order, qkv_t[qw:]).astype(BF)
+    kv[at.b, 0] = kv_rows[:half]
+    kv[at.b, 1] = kv_rows[half:]
+
+    def kv_copy(p, second, way, device):
+        return remote(
+            kv.at[p, second], kv.at[p, second], kv_send.at[way, p], kv_recv.at[p], device
+        )
+
+    right = at.in_blk(jnp.minimum(at.b + 2, nb - 2 + at.core))
+    left = at.in_blk(jnp.maximum(at.b - 2, at.core))
+    across = at.in_blk(at.sibling)
+    pl.when(at.z + 1 < at.nz)(lambda: kv_copy(at.b, 0, 0, right).start())
+    pl.when(at.z > 0)(lambda: kv_copy(at.b, 1, 0, left).start())
+    kv_copy(at.b, at.core, 1, across).start()
+    q_rows = nt(order, qkv_t[:qw]).astype(BF)
+    qn[...] = q_rows
+    q_cols = (nt(qkv_t[:qw], order) * (1.0 / math.sqrt(HEAD_SIZE))).astype(BF)
+    qt[0] = q_cols[:, :half]
+    qt[1] = q_cols[:, half:]
+    top[...] = jnp.full(top.shape, -1e30, F32)
+    total[...] = jnp.zeros(total.shape, F32)
+    attn_t[...] = jnp.zeros(attn_t.shape, F32)
+
+    def attend(p, second):
+        old_top, old_total = top[second], total[second]
+        tops, totals = [], []
+        block = kv[p, second]
+        key_place = block_base(at, p, second, half) + lax.broadcasted_iota(
+            jnp.int32, (half, half), 0
+        )
+        own_place = block_base(at, at.b, second, half) + lax.broadcasted_iota(
+            jnp.int32, (half, half), 1
+        )
+        allowed = (key_place <= own_place) & (key_place >= begin[second])
+        for a in range(hl):
+            g = a // (hl // kl)
+            rows_a = slice(a * HEAD_SIZE, (a + 1) * HEAD_SIZE)
+            scores = nn(block[:, g * HEAD_SIZE : (g + 1) * HEAD_SIZE], qt[second, rows_a])
+            scores = jnp.where(allowed, scores, -1e30)
+            old = old_top[a : a + 1]
+            new = jnp.maximum(old, jnp.max(scores, axis=0, keepdims=True))
+            probs = jnp.exp(scores - new)
+            fade = jnp.exp(old - new)
+            totals.append(old_total[a : a + 1] * fade + jnp.sum(probs, axis=0, keepdims=True))
+            tops.append(new)
+            attn_t[second, rows_a] = attn_t[second, rows_a] * fade + tn(
+                block[:, kw + g * HEAD_SIZE : kw + (g + 1) * HEAD_SIZE], probs.astype(BF)
+            )
+        top[second, :hl] = jnp.concatenate(tops, axis=0)
+        total[second, :hl] = jnp.concatenate(totals, axis=0)
+
+    def visit(step, unused):
+        i = step // 4
+        second = lax.rem(step, 2)
+        same = lax.rem(step // 2, 2) == 0
+        z = jnp.where(second == 0, at.z - i, at.z + i)
+        p = 2 * z + jnp.where(same, at.core, 1 - at.core)
+        exists = (z >= 0) & (z < nb // 2) & ((i > 0) | same | (at.core != second))
+
+        @pl.when(exists)
+        def _():
+            @pl.when(p != at.b)
+            def _():
+                kv_copy(p, second, 1, across).wait_recv()
+
+            @pl.when((i > 0) & same)
+            def _():
+                @pl.when((second == 0) & (at.z + 1 < at.nz))
+                def _():
+                    kv_copy(p, second, 0, right).start()
+
+                @pl.when((second == 1) & (at.z > 0))
+                def _():
+                    kv_copy(p, second, 0, left).start()
+
+                kv_copy(p, second, 1, across).start()
+
+            attend(p, second)
+
+        return 0
+
+    lax.fori_loop(0, 4 * (nb // 2), visit, 0)
+    for second in range(2):
+        sums = total[second]
+        for a in range(hl):
+            rows_a = slice(a * HEAD_SIZE, (a + 1) * HEAD_SIZE)
+            attn_t[second, rows_a] = attn_t[second, rows_a] / sums[a : a + 1]
+    lse[...] = top[...] + jnp.log(total[...])
+    back = jnp.where(place_col[...] == sorted_place(at, half, (group, group), 1), 1.0, 0.0).astype(BF)
+    attn_rows = (
+        nt(back[:, :half], attn_t[0].astype(BF)) + nt(back[:, half:], attn_t[1].astype(BF))
+    ).astype(BF)
+    ao[...] = attn_rows
+    o_copies = []
+    for k in range(nh):
+        peer = at.head_peer(k)
+        chunk = nt(ao[pl.ds(peer * rows, rows)], w[:, width:])
+        if k == 0:
+            middle[...] = hidden + chunk
+            continue
+        out_send[peer] = chunk.astype(BF)
+        c = remote(
+            out_send.at[peer], out_recv.at[at.h], o_sems.at[0, k], o_sems.at[1, k], at.in_head(peer)
+        )
+        c.start()
+        o_copies.append(c)
+    for k in range(1, nh):
+        o_copies[k - 1].wait_recv()
+        middle[...] += out_recv[lax.rem(at.h + nh - k, nh)].astype(F32)
+    mid = middle[...]
+    n2[...] = (
+        mid * lax.rsqrt(jnp.mean(mid * mid, axis=-1, keepdims=True) + eps) * w_norm2[...]
+    ).astype(BF)
+    weights.finish()
+    for c in x_copies + o_copies:
+        c.wait_send()
+
+    def drain(step, unused):
+        i = step // 2
+        second = lax.rem(step, 2)
+        z = jnp.where(second == 0, at.z - i, at.z + i)
+        p = 2 * z + at.core
+
+        @pl.when((z >= 0) & (z < nb // 2))
+        def _():
+            @pl.when((second == 0) & (at.z + 1 < at.nz))
+            def _():
+                kv_copy(p, second, 0, right).wait_send()
+
+            @pl.when((second == 1) & (at.z > 0))
+            def _():
+                kv_copy(p, second, 0, left).wait_send()
+
+            @pl.when((i > 0) | (second == at.core))
+            def _():
+                kv_copy(p, second, 1, across).wait_send()
+
+        return 0
+
+    lax.fori_loop(0, nb, drain, 0)
+
+
+def front(nb, nh, hl, kl, inputs, w_norm1, w_norm2, w_own, place_row, place_col, cos, sin, begin):
+    rows = inputs.shape[0]
+    group, half = rows * nh, rows * nh // 2
+    dl, wide = w_own.shape
+    qw, kw = hl * HEAD_SIZE, kl * HEAD_SIZE
+    shape = jax.ShapeDtypeStruct
+    return pl.pallas_call(
+        functools.partial(front_kernel, nb, nh, hl, kl),
+        out_shape=(
+            shape((nh, rows, MODEL_WIDTH), BF),
+            shape((nb, dl, wide), BF),
+            shape((group, qw), BF),
+            shape((nb, 2, half, 2 * kw), BF),
+            shape((2, max(hl, 8), half), F32),
+            shape((2, qw, half), F32),
+            shape((group, qw), BF),
+            shape((rows, MODEL_WIDTH), F32),
+            shape((rows, MODEL_WIDTH), BF),
+        ),
+        in_specs=[VMEM] * 9,
+        out_specs=[VMEM] * 9,
+        scratch_shapes=[
+            pltpu.VMEM((2, qw, half), BF),
+            pltpu.VMEM((group, group), BF),
+            pltpu.VMEM((2, max(hl, 8), half), F32),
+            pltpu.VMEM((2, max(hl, 8), half), F32),
+            pltpu.VMEM((nh, rows, MODEL_WIDTH), BF),
+            pltpu.VMEM((nh, rows, MODEL_WIDTH), BF),
+            pltpu.SemaphoreType.DMA((2, nh)),
+            pltpu.SemaphoreType.DMA((3, nb)),
+            pltpu.SemaphoreType.DMA((nb,)),
+            pltpu.SemaphoreType.DMA((2, nb)),
+            pltpu.SemaphoreType.DMA((nb,)),
+            pltpu.SemaphoreType.DMA((2, nh)),
+        ],
+        compiler_params=pltpu.CompilerParams(collective_id=1, vmem_limit_bytes=48 * 2**20),
+        name="front",
+    )(inputs, w_norm1, w_norm2, w_own, place_row, place_col, cos, sin, begin)
 
 
 def seq_begin(token_position, lengths):
@@ -22,7 +433,29 @@
     return jnp.sum(jnp.where(inside, lengths[None, :-1], 0), axis=1)
 
 
-def rotation(token_position, begin_index, width):
+def rotation_rows(token_position, begin_index):
+    half = HEAD_SIZE // 2
+    freq = jnp.exp(
+        jnp.arange(half, dtype=F32) * (-2.0 * math.log(rope_base) / HEAD_SIZE)
+    )
+    angle = freq[:, None] * (token_position - begin_index).astype(F32)[None, :]
+    return jnp.cos(angle), jnp.sin(angle)
+
+
+def head_inputs(nb, nh, rows, token_place, lengths, w_query, key_weight, value_weight, w_out):
+    group, half = rows * nh, rows * nh // 2
+    b = lax.axis_index("blk")
+    own = lax.dynamic_slice_in_dim(token_place, b * group, group)
+    s = jnp.arange(group, dtype=jnp.int32)
+    in_order = jnp.where(s < half, b * half + s, (2 * nb - 1 - b) * half + s - half)
+    begin_s = seq_begin(in_order, lengths)
+    cos_o, sin_o = rotation_rows(own, seq_begin(own, lengths))
+    cos_s, sin_s = rotation_rows(in_order, begin_s)
+    w_own = jnp.concatenate([w_query, key_weight, value_weight, w_out.T], axis=1)
+    return own, begin_s.reshape(2, 1, half), cos_o, sin_o, cos_s, sin_s, w_own
+
+
+def seq_rotation(token_position, begin_index, width):
     half = width // 2
     freq = jnp.exp(jnp.arange(half, dtype=jnp.float32) * (-2.0 * math.log(rope_base) / width))
     angle = (token_position - begin_index).astype(jnp.float32)[:, None] * freq[None, :]
@@ -131,7 +564,7 @@
     first_row = lax.axis_index("blk") * group_rows
     own_place = lax.dynamic_slice_in_dim(token_place, first_row, group_rows)
     own_begin = lax.dynamic_slice_in_dim(begin_index, first_row, group_rows)
-    cosine_table, sine_table = rotation(own_place, own_begin, HEAD_SIZE)
+    cosine_table, sine_table = seq_rotation(own_place, own_begin, HEAD_SIZE)
     query = jnp.dot(gathered, query_all, preferred_element_type=jnp.float32)
     key = jnp.dot(gathered, key_all, preferred_element_type=jnp.float32)
     value_rows = jnp.dot(gathered, value_all, preferred_element_type=jnp.float32).astype(
@@ -194,12 +627,13 @@
         out_step, jnp.zeros((group_rows, kv_local, head_groups, HEAD_SIZE), jnp.float32), steps
     )
     attended_rows = attended32.reshape(group_rows, heads_local * HEAD_SIZE).astype(jnp.bfloat16)
-    middle = hidden + lax.psum_scatter(
-        jnp.dot(attended_rows, out_all, preferred_element_type=jnp.float32).astype(jnp.bfloat16),
-        "head",
-        scatter_dimension=0,
-        tiled=True,
-    ).astype(jnp.float32)
+    own, begin_s, cos_o, sin_o, cos_s, sin_s, w_own = head_inputs(
+        blk_count, head_count, rows, token_place, lengths, w_query, key_weight, value_weight, w_out
+    )
+    middle = front(
+        blk_count, head_count, heads_local, kv_local, inputs, w_norm1.reshape(1, -1), w_norm2.reshape(1, -1),
+        w_own, own.reshape(1, -1), own.reshape(-1, 1), cos_o, sin_o, begin_s,
+    )[7]
     scale_two = lax.rsqrt(jnp.mean(middle * middle, axis=-1, keepdims=True) + eps)
     unit_two = middle * scale_two
     normed_two = (unit_two * w_norm2).astype(jnp.bfloat16)

time: 1370 us -> 1320 us (0.964)
  waiting for transfers between devices: 745 us -> 558 us
  Pallas kernels: 0 us -> 59.8 us
  matrix products: 182 us -> 213 us
  local copies, waits for them, and re-layouts: 159 us -> 180 us
    all_gather x1, waiting for transfers between devices: 75.7 us -> 0.02 us  [fetch_experts(): lax.all_gather(w_gate, 'blk', axis=1, tiled=True)]
    pallas_call x0 -> x1, Pallas kernels: none -> 59.8 us  [front(): pl.pallas_call(functools.partial(front_kernel, nb, nh, hl, kl), out_shape...]
    all_gather x1, waiting for transfers between devices: 76.2 us -> 48.8 us  [fetch_experts(): lax.all_gather(w_down, 'blk', axis=2, tiled=True)]
    all_gather x1, waiting for transfers between devices: 24.6 us -> 0.02 us  [on_device(): lax.all_gather(d_middle.astype(jnp.bfloat16), 'head', axis=0, tiled=True)]
    all_to_all x1, waiting for transfers between devices: 24 us -> 0.01 us  [on_device(): lax.all_to_all(d_arrived, 'head', split_axis=0, concat_axis=0, tiled=True)]
    dynamic_update_slice x24, local copies, waits for them, and re-layouts: 14.9 us -> 34.5 us  [on_device(): lax.scan(back_step, jnp.zeros((group_rows, kv_local, head_groups, HEAD_SI...]
    and x24, other arithmetic: 6.52 us -> 23.1 us  [block_scores(): (key_place[None, :] <= own_place[:, None]) & (key_place[None, :] >= own_b...]
    unnamed x116 -> x127, local copies, waits for them, and re-layouts: 37 us -> 40.5 us
  transfers between devices with their start and end apart: 23 -> 22, of which waited for: 18 -> 12; matrix products, arithmetic and copies ran while one was open for 20% -> 27% of each run, Pallas kernels for 0% -> 5%
where the time goes in v1:
time: 1320 us; the launch traced here: 1300 us
  waiting for transfers between devices  558 us (42%)
  matrix products  213 us (16%)
  local copies, waits for them, and re-layouts  180 us (14%)
  other arithmetic  132 us (10%)
  blocking collectives  105 us (8%)
  Pallas kernels  59.8 us (5%)
  starting transfers between devices  20.1 us (2%)
  loops' own time  17.5 us (1%)
  between operations  15.7 us (1%)
    psum x1, waiting for transfers between devices, on_device(): small = lax.psum((grad_norm1, grad_norm2, grad_router), ('blk', 'head'))  125 us
    reduce_scatter x1, waiting for transfers between devices, on_device(): lax.psum_scatter(grad_up.astype(jnp.bfloat16), 'blk', scatter_dimension=1...  87.4 us
    reduce_scatter x1, waiting for transfers between devices, on_device(): lax.psum_scatter(grad_gate.astype(jnp.bfloat16), 'blk', scatter_dimension...  86.1 us
    pallas_call x1, Pallas kernels, front(): pl.pallas_call(functools.partial(front_kernel, nb, nh, hl, kl), out_shape...  59.8 us
    unnamed x20, waiting for transfers between devices  51.1 us
    all_gather x1, waiting for transfers between devices, fetch_experts(): lax.all_gather(w_down, 'blk', axis=2, tiled=True)  48.8 us
    psum x1, blocking collectives, on_device(): small = lax.psum((grad_norm1, grad_norm2, grad_router), ('blk', 'head'))  41.3 us
    unnamed x127, local copies, waits for them, and re-layouts  40.5 us
  transfers between devices with their start and end apart: 22, of which 12 were waited for; matrix products, arithmetic and copies ran while one was open for 27% of the time, Pallas kernels for 5%

profile of v1, /device:TPU:0, one launch (start us, length us, event | category | flops | bytes accessed | tf_op | source)
XLA Modules:
  0.0 1301.6 jit_solution(6443154823194909534)
XLA Ops:
  16.0 59.8 %front.1 = (bf16[4,128,1024]{2,1,0:T(8,128)(2,1)}, bf16[8,128,768]{2,1,0:T(8,128)(2,1)}, bf16[512,256]{1,0:T(8,128)(2,1)}, bf16[8,2,256,256]{3,2,1,0:T(8,128)(2,...) custom-call(bf16[128,1024]{1,0:T(8,128)(2,1)S(1)} %copy-done.2, ...), custom_call_target="tpu_custom_call" | custom-call | tf_op jit(solution)/shard_map/front/pallas_call | solution.py:396
  133.4 15.0 %all_gather.45 = bf16[1024,128]{1,0:T(8,128)(2,1)S(1)} all-gather(bf16[128,128]{1,0:T(8,128)(2,1)S(1)} %copy-done.44), channel_id=1, replica_groups=mesh['blk'=8,'head'=4] {'blk'}, dimensions={0}, use_global_device_ids=true | all-gather | bytes 294912 | tf_op jit(solution)/shard_map/all_gather | solution.py:506
  151.0 23.5 %select_reduce_fusion.1 = s32[1280]{0:T(1024)S(1)} fusion(s32[128,8]{0,1:T(8,128)S(1)} %get-tuple-element.553, pred[128,8]{0,1:T(8,128)(4,1)S(1)} %get-tuple-element.551), kind=kLoop, calls=%fused_computation.66 | loop fusion | flops 5241600 | bytes 10240 | tf_op jit(solution)/shard_map/reduce_sum | solution.py:679
  180.0 17.1 %all_gather.47 = bf16[1024,256]{1,0:T(8,128)(2,1)S(1)} all-gather(bf16[128,256]{1,0:T(8,128)(2,1)S(1)} %copy-done.39), channel_id=1, replica_groups=mesh['blk'=8,'head'=4] {'blk'}, dimensions={0}, use_global_device_ids=true | all-gather | bytes 589824 | tf_op jit(solution)/shard_map/all_gather | solution.py:505
  206.5 15.2 %all_gather.48 = bf16[1024,128]{1,0:T(8,128)(2,1)S(1)} all-gather(bf16[128,128]{1,0:T(8,128)(2,1)S(1)} %copy-done.46), channel_id=1, replica_groups=mesh['blk'=8,'head'=4] {'blk'}, dimensions={0}, use_global_device_ids=true | all-gather | bytes 294912 | tf_op jit(solution)/shard_map/all_gather | solution.py:507
  221.7 16.7 %all_gather.51 = bf16[256,1024]{1,0:T(8,128)(2,1)} all-gather(bf16[256,128]{1,0:T(8,128)(2,1)S(1)} %copy-done.37), channel_id=1, replica_groups=mesh['blk'=8,'head'=4] {'blk'}, dimensions={1}, use_global_device_ids=true | all-gather | bytes 589824 | tf_op jit(solution)/shard_map/all_gather | solution.py:508
  254.4 48.8 %all-gather.12.cloned.1.call-done = bf16[8,512,1024]{2,1,0:T(8,128)(2,1)} async-done(((bf16[8,512,128]{2,1,0:T(8,128)(2,1)}), bf16[8,512,1024]{2,1,0:T(8,128)(2,1)}) %all-gather.12.cloned.1.call-update) | async-done | bytes 8388624 | tf_op jit(solution)/shard_map/all_gather | solution.py:516
  303.2 10.4 fusion.42
  341.6 15.3 %all-to-all-done.1 = bf16[4,8,40,1024]{3,2,1,0:T(8,128)(2,1)} async-done(((bf16[4,8,40,1024]{3,2,1,0:T(8,128)(2,1)}), bf16[4,8,40,1024]{3,2,1,0:T(8,128)(2,1)}, u32[]{:S(2)}, u32[]{:S(2)}) %all-to-all-start.1) | async-done | bytes 2621472 | tf_op jit(solution)/shard_map/all_to_all | solution.py:665
  361.5 80.2 %while.39 = (s32[]{:T(128)}, f32[2,2,512]{2,1,0:T(2,128)S(1)}, f32[2,2,512]{2,1,0:T(2,128)S(1)}, s32[8]{0:T(128)S(1)}, s32[4096]{0:T(1024)}, /*index=5*/s32[512]...) while((s32[]{:T(128)}, f32[2,2,512]{2,1,0:T(2,128)S(1)}, ...), condition=%wide.region_23.24_spmd.clone, body=%wide.region_20.23_spmd.clone.sunk | while | flops 143403008 | bytes 9947338 | solution.py:615
  462.6 48.7 %while.40 = (s32[]{:T(128)}, f32[512,2,2,64]{0,3,2,1:T(8,128)S(1)}, s32[8]{0:T(128)S(1)}, bf16[4096,128]{0,1:T(8,128)(2,1)}, s32[4096]{0:T(1024)}, /*index=5*/s3...) while((s32[]{:T(128)}, f32[512,2,2,64]{0,3,2,1:T(8,128)S(1)}, ...), condition=%wide.region_25.26_spmd.clone, body=%wide.region_24.25_spmd.clone.sunk | while | flops 273678336 | bytes 2640081 | solution.py:626
  513.8 159.2 %while.41 = (s32[]{:T(128)}, f32[512,2,2,64]{0,3,2,1:T(8,128)}, bf16[8,512,128]{2,1,0:T(8,128)(2,1)}, bf16[8,512,128]{2,1,0:T(8,128)(2,1)}, s32[8]{0:T(128)S(1)}...) while((s32[]{:T(128)}, f32[512,2,2,64]{0,3,2,1:T(8,128)}, ...), condition=%wide.region_28.29_spmd.clone, body=%wide.region_27.28_spmd.clone.sunk | while | flops 682754048 | bytes 42896200 | solution.py:760
  679.0 25.5 %reduce-scatter.15.cloned.1.call-done = bf16[512,128]{1,0:T(8,128)(2,1)} async-done(((bf16[4096,128]{1,0:T(8,128)(2,1)}), bf16[512,128]{1,0:T(8,128)(2,1)}) %reduce-scatter.15.cloned.1.call-update) | async-done | bytes 131088 | tf_op jit(solution)/shard_map/reduce_scatter | solution.py:764
  707.6 29.8 %reduce-scatter.17.cloned.1.call-done = bf16[512,128]{1,0:T(8,128)(2,1)} async-done(((bf16[4096,128]{1,0:T(8,128)(2,1)}), bf16[512,128]{1,0:T(8,128)(2,1)}) %reduce-scatter.17.cloned.1.call-update) | async-done | bytes 131088 | tf_op jit(solution)/shard_map/reduce_scatter | solution.py:770
  752.0 12.7 copy.241
  764.8 12.2 copy.261
  802.4 29.2 %reduce-scatter.23.cloned.1.call-done = bf16[128,128]{1,0:T(8,128)(2,1)} async-done(((bf16[1024,128]{1,0:T(8,128)(2,1)}), bf16[128,128]{1,0:T(8,128)(2,1)}) %reduce-scatter.23.cloned.1.call-update) | async-done | bytes 32784 | tf_op jit(solution)/shard_map/reduce_scatter | solution.py:819
  833.1 29.5 %reduce-scatter.25.cloned.1.call-done = bf16[128,128]{1,0:T(8,128)(2,1)} async-done(((bf16[1024,128]{1,0:T(8,128)(2,1)}), bf16[128,128]{1,0:T(8,128)(2,1)}) %reduce-scatter.25.cloned.1.call-update) | async-done | bytes 32784 | tf_op jit(solution)/shard_map/reduce_scatter | solution.py:822
  864.0 27.8 %reduce-scatter.19.cloned.1.call-done = bf16[128,1024]{1,0:T(8,128)(2,1)} async-done(((bf16[512,1024]{1,0:T(8,128)(2,1)}), bf16[128,1024]{1,0:T(8,128)(2,1)}) %reduce-scatter.19.cloned.1.call-update) | async-done | bytes 262160 | tf_op jit(solution)/shard_map/reduce_scatter | solution.py:797
  895.2 41.3 %all-reduce = (f32[1024]{0:T(1024)}, f32[1024]{0:T(1024)}) all-reduce(f32[1024]{0:T(1024)S(1)} %get-tuple-element.474, f32[1024]{0:T(1024)S(1)} %copy-done.51), channel_id=1, replica_groups=mesh['blk'=8,'head'=4] {'blk','head'}, use_global_device_ids=true, to_apply=%region_34.35 | all-reduce | flops 2048 | bytes 16384 | tf_op jit(solution)/shard_map/psum | solution.py:838
  936.4 48.3 %reduce-scatter.33.cloned.1.call-done = bf16[128,4096]{1,0:T(8,128)(2,1)} async-done(((bf16[1024,4096]{1,0:T(8,128)(2,1)}), bf16[128,4096]{1,0:T(8,128)(2,1)}) %reduce-scatter.33.cloned.1.call-update) | async-done | bytes 1048592
  988.8 86.1 %reduce-scatter.27.cloned.1.call-done = bf16[8,128,512]{2,1,0:T(8,128)(2,1)} async-done(((bf16[8,1024,512]{2,1,0:T(8,128)(2,1)}), bf16[8,128,512]{2,1,0:T(8,128)(2,1)}) %reduce-scatter.27.cloned.1.call-update) | async-done | bytes 1048592 | tf_op jit(solution)/shard_map/reduce_scatter | solution.py:828
  1077.8 87.4 %reduce-scatter.29.cloned.1.call-done = bf16[8,128,512]{2,1,0:T(8,128)(2,1)} async-done(((bf16[8,1024,512]{2,1,0:T(8,128)(2,1)}), bf16[8,128,512]{2,1,0:T(8,128)(2,1)}) %reduce-scatter.29.cloned.1.call-update) | async-done | bytes 1048592 | tf_op jit(solution)/shard_map/reduce_scatter | solution.py:831
  1168.0 124.9 %all-reduce.3.cloned.1.call-done = f32[1024,32]{0,1:T(8,128)} async-done(((f32[1024,32]{0,1:T(8,128)}), f32[1024,32]{0,1:T(8,128)}) %all-reduce.3.cloned.1.call-update) | async-done | bytes 131088 | tf_op jit(solution)/shard_map/psum | solution.py:838
  (565 shorter events, 491.7 us)
Async XLA Ops:
  7.3 141.2 %all-gather.14.cloned.1.call-start = ((), (), s32[]{:S(2)}) async-start(), calls=%async_computation.17 | async-start | bytes 1310720 | tf_op jit(solution)/shard_map/all_gather | solution.py:562
  10.3 229.3 %all-gather.8.cloned.1.call-start = ((), (), s32[]{:S(2)}) async-start(), calls=%async_computation.14 | async-start | bytes 9437184 | tf_op jit(solution)/shard_map/all_gather | solution.py:514
  11.1 235.8 %all-gather.10.cloned.1.call-start = ((), (), s32[]{:S(2)}) async-start(), calls=%async_computation.15 | async-start | bytes 9437184 | tf_op jit(solution)/shard_map/all_gather | solution.py:515
  11.8 291.3 %all-gather.12.cloned.1.call-start = ((), (), s32[]{:S(2)}) async-start(), calls=%async_computation.16 | async-start | bytes 9437184 | tf_op jit(solution)/shard_map/all_gather | solution.py:516
  116.6 85.1 %all-to-all-start = ((bf16[4,8,40,1024]{3,2,1,0:T(8,128)(2,1)}), bf16[4,8,40,1024]{3,2,1,0:T(8,128)(2,1)}, u32[]{:S(2)}, u32[]{:S(2)}) async-start(bf16[4,8,40,1024]{3,2,1,0:T(8,128)(2,1)} %bitcast.13), calls=%async_computation | async-start | bytes 5242880 | tf_op jit(solution)/shard_map/all_to_all | solution.py:650
  121.2 240.3 %all-gather.16.cloned.1.call-start = ((), (), s32[]{:S(2)}) async-start(), calls=%async_computation.18 | async-start | bytes 1179648 | tf_op jit(solution)/shard_map/all_gather | solution.py:522
  197.1 128.5 %copy-start.10 = (bf16[1024,256]{1,0:T(8,128)(2,1)}, bf16[1024,256]{1,0:T(8,128)(2,1)S(1)}, u32[]{:S(2)}) copy-start(bf16[1024,256]{1,0:T(8,128)(2,1)S(1)} %all_gather.47) | copy-start | bytes 1572868
  201.7 52.7 %all-to-all-start.2 = ((bf16[4,8,40,1024]{3,2,1,0:T(8,128)(2,1)}), bf16[4,8,40,1024]{3,2,1,0:T(8,128)(2,1)}, u32[]{:S(2)}, u32[]{:S(2)}) async-start(bf16[4,8,40,1024]{3,2,1,0:T(8,128)(2,1)} %multiply_convert_fusion), calls=%async_computation.2 | async-start | bytes 5242880 | tf_op jit(solution)/shard_map/all_to_all | solution.py:682
  206.5 235.3 %all-gather.18.cloned.1.call-start = ((), (), s32[]{:S(2)}) async-start(), calls=%async_computation.19 | async-start | bytes 1179648 | tf_op jit(solution)/shard_map/all_gather | solution.py:523
  320.9 36.0 %all-to-all-start.1 = ((bf16[4,8,40,1024]{3,2,1,0:T(8,128)(2,1)}), bf16[4,8,40,1024]{3,2,1,0:T(8,128)(2,1)}, u32[]{:S(2)}, u32[]{:S(2)}) async-start(bf16[4,8,40,1024]{3,2,1,0:T(8,128)(2,1)} %copy.211), calls=%async_computation.1 | async-start | bytes 5242880 | tf_op jit(solution)/shard_map/all_to_all | solution.py:665
  356.9 100.3 %all-to-all-start.3 = ((bf16[4,8,40,1024]{3,2,1,0:T(8,128)(2,1)}), bf16[4,8,40,1024]{3,2,1,0:T(8,128)(2,1)}, u32[]{:S(2)}, u32[]{:S(2)}) async-start(bf16[4,8,40,1024]{3,2,1,0:T(8,128)(2,1)} %copy.214), calls=%async_computation.3 | async-start | bytes 5242880 | tf_op jit(solution)/shard_map/all_to_all | solution.py:703
  361.4 149.9 %all-gather.20.cloned.1.call-start = ((), (), s32[]{:S(2)}) async-start(), calls=%async_computation.20 | async-start | bytes 1310720 | tf_op jit(solution)/shard_map/all_gather | solution.py:726
  462.5 242.1 %reduce-scatter.15.cloned.1.call-start = ((), (), s32[]{:S(2)}) async-start(), calls=%async_computation.21 | async-start | bytes 1179648 | tf_op jit(solution)/shard_map/reduce_scatter | solution.py:764
  673.1 64.3 %reduce-scatter.17.cloned.1.call-start = ((), (), s32[]{:S(2)}) async-start(), calls=%async_computation.22 | async-start | bytes 1179648 | tf_op jit(solution)/shard_map/reduce_scatter | solution.py:770
  673.8 122.7 %reduce-scatter.31.cloned.1.call-start = ((), (), s32[]{:S(2)}) async-start(), calls=%async_computation.30 | async-start | bytes 589824
  676.7 124.2 %reduce-scatter.21.cloned.1.call-start = ((), (), s32[]{:S(2)}) async-start(), calls=%async_computation.24 | async-start | bytes 589824 | tf_op jit(solution)/shard_map/reduce_scatter | solution.py:816
  679.0 152.7 %reduce-scatter.23.cloned.1.call-start = ((), (), s32[]{:S(2)}) async-start(), calls=%async_computation.25 | async-start | bytes 294912 | tf_op jit(solution)/shard_map/reduce_scatter | solution.py:819
  707.5 155.1 %reduce-scatter.25.cloned.1.call-start = ((), (), s32[]{:S(2)}) async-start(), calls=%async_computation.26 | async-start | bytes 294912 | tf_op jit(solution)/shard_map/reduce_scatter | solution.py:822
  741.0 150.7 %reduce-scatter.19.cloned.1.call-start = ((), (), s32[]{:S(2)}) async-start(), calls=%async_computation.23 | async-start | bytes 1310720 | tf_op jit(solution)/shard_map/reduce_scatter | solution.py:797
  744.2 240.5 %reduce-scatter.33.cloned.1.call-start = ((), (), s32[]{:S(2)}) async-start(), calls=%async_computation.31 | async-start | bytes 9437184
  777.1 297.9 %reduce-scatter.27.cloned.1.call-start = ((), (), s32[]{:S(2)}) async-start(), calls=%async_computation.28 | async-start | bytes 9437184 | tf_op jit(solution)/shard_map/reduce_scatter | solution.py:828
  785.8 379.4 %reduce-scatter.29.cloned.1.call-start = ((), (), s32[]{:S(2)}) async-start(), calls=%async_computation.29 | async-start | bytes 9437184 | tf_op jit(solution)/shard_map/reduce_scatter | solution.py:831
  794.7 498.2 %all-reduce.3.cloned.1.call-start = ((), (), s32[]{:S(2)}) async-start(), calls=%async_computation.27 | async-start | bytes 262144 | tf_op jit(solution)/shard_map/psum | solution.py:838
  987.3 307.2 %copy-start.1 = (bf16[1024,32]{0,1:T(8,128)(2,1)S(1)}, bf16[1024,32]{0,1:T(8,128)(2,1)}, u32[]{:S(2)}) copy-start(bf16[1024,32]{0,1:T(8,128)(2,1)} %param.31) | copy-start | bytes 196612
  (80 other events, 1309.4 us)
Sparse Core Ops, SparseCore 0:
  10.5 35.6 all-gather.13
  47.9 82.0 all-gather.7
  131.6 86.2 all-gather.9
  219.3 83.8 all-gather.11
  305.2 21.0 all-gather.15
  328.3 21.4 all-gather.17
  462.6 25.7 all-gather.19
  673.2 31.3 reduce-scatter.14
  706.8 30.5 reduce-scatter.16
  739.5 29.3 reduce-scatter.30
  771.8 29.0 reduce-scatter.20
  803.0 28.6 reduce-scatter.22
  834.0 28.5 reduce-scatter.24
  865.9 25.8 reduce-scatter.18
  894.0 90.6 reduce-scatter.32
  987.0 87.9 reduce-scatter.26
  1077.2 87.9 reduce-scatter.28
  1172.1 120.7 all-reduce.2

commit v2 on v1

--- a/solution.py
+++ b/solution.py
@@ -188,14 +188,14 @@
     begin,
     xg,
     wg,
-    qn,
+    qt,
     kv,
     lse,
     attn_t,
-    ao,
+    ao_t,
     middle,
     n2,
-    qt,
+    ao,
     perm,
     top,
     total,
@@ -259,8 +259,6 @@
     pl.when(at.z + 1 < at.nz)(lambda: kv_copy(at.b, 0, 0, right).start())
     pl.when(at.z > 0)(lambda: kv_copy(at.b, 1, 0, left).start())
     kv_copy(at.b, at.core, 1, across).start()
-    q_rows = nt(order, qkv_t[:qw]).astype(BF)
-    qn[...] = q_rows
     q_cols = (nt(qkv_t[:qw], order) * (1.0 / math.sqrt(HEAD_SIZE))).astype(BF)
     qt[0] = q_cols[:, :half]
     qt[1] = q_cols[:, half:]
@@ -338,6 +336,9 @@
         nt(back[:, :half], attn_t[0].astype(BF)) + nt(back[:, half:], attn_t[1].astype(BF))
     ).astype(BF)
     ao[...] = attn_rows
+    ao_t[...] = (
+        nn(attn_t[0].astype(BF), perm[:half]) + nn(attn_t[1].astype(BF), perm[half:])
+    ).astype(BF)
     o_copies = []
     for k in range(nh):
         peer = at.head_peer(k)
@@ -398,18 +399,18 @@
         out_shape=(
             shape((nh, rows, MODEL_WIDTH), BF),
             shape((nb, dl, wide), BF),
-            shape((group, qw), BF),
+            shape((2, qw, half), BF),
             shape((nb, 2, half, 2 * kw), BF),
             shape((2, max(hl, 8), half), F32),
             shape((2, qw, half), F32),
-            shape((group, qw), BF),
+            shape((qw, group), BF),
             shape((rows, MODEL_WIDTH), F32),
             shape((rows, MODEL_WIDTH), BF),
         ),
         in_specs=[VMEM] * 9,
         out_specs=[VMEM] * 9,
         scratch_shapes=[
-            pltpu.VMEM((2, qw, half), BF),
+            pltpu.VMEM((group, qw), BF),
             pltpu.VMEM((group, group), BF),
             pltpu.VMEM((2, max(hl, 8), half), F32),
             pltpu.VMEM((2, max(hl, 8), half), F32),
@@ -455,24 +456,405 @@
     return own, begin_s.reshape(2, 1, half), cos_o, sin_o, cos_s, sin_s, w_own
 
 
-def seq_rotation(token_position, begin_index, width):
-    half = width // 2
-    freq = jnp.exp(jnp.arange(half, dtype=jnp.float32) * (-2.0 * math.log(rope_base) / width))
-    angle = (token_position - begin_index).astype(jnp.float32)[:, None] * freq[None, :]
-    return (jnp.cos(angle)[:, None, :], jnp.sin(angle)[:, None, :])
-
-
-def turn_index(values, cosine_table, sine_table):
-    half = values.shape[-1] // 2
-    leading = values[..., :half]
-    trailing = values[..., half:]
-    return jnp.concatenate(
-        [
-            leading * cosine_table - trailing * sine_table,
-            trailing * cosine_table + leading * sine_table,
+class Scatter:
+    def __init__(self, at, sib_out, sib_in, z_out, z_in, sems):
+        self.at, self.sib_out, self.sib_in, self.z_out, self.z_in = at, sib_out, sib_in, z_out, z_in
+        self.sems = sems
+
+    def across(self, z):
+        return remote(
+            self.sib_out.at[z],
+            self.sib_in.at[z],
+            self.sems.at[0, z],
+            self.sems.at[1, z],
+            self.at.in_blk(self.at.sibling),
+        )
+
+    def along(self, z):
+        return remote(
+            self.z_out.at[z],
+            self.z_in.at[self.at.z],
+            self.sems.at[2, z],
+            self.sems.at[3, self.at.z],
+            self.at.in_blk(2 * z + self.at.core),
+        )
+
+    def give_sibling(self, z, value):
+        self.sib_out[z] = value.astype(BF)
+        self.across(z).start()
+
+    def from_sibling(self, z):
+        self.across(z).wait_recv()
+        return self.sib_in[z].astype(F32)
+
+    def give(self, z, value):
+        self.z_out[z] = value.astype(BF)
+        self.along(z).start()
+
+    def taken(self, z):
+        remote(
+            self.z_out.at[z],
+            self.z_in.at[z],
+            self.sems.at[2, z],
+            self.sems.at[3, z],
+            self.at.in_blk(2 * z + self.at.core),
+        ).wait_recv()
+        return self.z_in[z].astype(F32)
+
+    def finish(self):
+        at = self.at
+        for z in range(at.nz):
+            self.across(z).wait_send()
+            pl.when(at.z != z)(lambda: self.along(z).wait_send())
+
+
+class Total:
+    def __init__(self, at, part, by_head, by_blk, whole, sems):
+        self.at, self.part, self.by_head, self.by_blk, self.whole = at, part, by_head, by_blk, whole
+        self.sems = sems
+
+    def copy(self, stage, k):
+        at = self.at
+        peer = at.blk_peer(k) if stage == 1 else at.head_peer(k)
+        device = at.in_blk(peer) if stage == 1 else at.in_head(peer)
+        if stage == 0:
+            src, dst = self.part.at[peer], self.by_head.at[at.h]
+        elif stage == 1:
+            src, dst = self.by_blk.at[at.b], self.by_blk.at[at.b]
+        else:
+            src, dst = self.whole.at[at.h], self.whole.at[at.h]
+        return remote(src, dst, self.sems.at[0, stage, k], self.sems.at[1, stage, k], device)
+
+    def peers(self, stage):
+        return range(1, self.at.nb if stage == 1 else self.at.nh)
+
+    def begin(self, stage):
+        at = self.at
+        if stage == 0:
+            self.by_head[at.h] = self.part[at.h]
+        elif stage == 1:
+            self.by_blk[at.b] = sum_slots(self.by_head, at.nh)
+        else:
+            self.whole[at.h] = sum_slots(self.by_blk, at.nb)
+        for k in self.peers(stage):
+            self.copy(stage, k).start()
+
+    def end(self, stage):
+        for k in self.peers(stage):
+            self.copy(stage, k).wait_recv()
+
+    def finish(self):
+        for stage in range(3):
+            for k in self.peers(stage):
+                self.copy(stage, k).wait_send()
+
+
+def sum_slots(ref, n):
+    total = ref[0]
+    for s in range(1, n):
+        total = total + ref[s]
+    return total
+
+
+def back_kernel(
+    nb,
+    nh,
+    hl,
+    kl,
+    inputs,
+    w_norm1,
+    d_middle,
+    wg,
+    xg,
+    ao_t,
+    qt,
+    kv,
+    lse,
+    attn_t,
+    place_row,
+    place_col,
+    cos,
+    sin,
+    begin,
+    small,
+    grad_in,
+    grad_w,
+    grad_n1,
+    small_sum,
+    dbg,
+    perm,
+    d_rows_ref,
+    do_t,
+    delta,
+    dq_t,
+    own_kv,
+    kv_bufs,
+    w_part,
+    w_bufs,
+    out_send,
+    out_recv,
+    n1_head,
+    n1_blk,
+    s_head,
+    s_blk,
+    d_sems,
+    kv_sems,
+    w_sems,
+    o_sems,
+    n_sems,
+    s_sems,
+):
+    at = Place(nb, nh)
+    nz = at.nz
+    rows = inputs.shape[0]
+    group = rows * nh
+    half = group // 2
+    qw, kw = hl * HEAD_SIZE, kl * HEAD_SIZE
+    width = qw + 2 * kw
+    dl = MODEL_WIDTH // nb
+    scale = 1.0 / math.sqrt(HEAD_SIZE)
+
+    dbg[at.h] = d_middle[...].astype(BF)
+    at.meet()
+    d_copies = [
+        remote(dbg.at[at.h], dbg.at[at.h], d_sems.at[0, k], d_sems.at[1, k], at.in_head(at.head_peer(k)))
+        for k in range(1, nh)
+    ]
+    for c in d_copies:
+        c.start()
+    totals = Total(at, small, s_head, s_blk, small_sum, s_sems)
+    totals.begin(0)
+    perm[...] = jnp.where(
+        place_row[...] == sorted_place(at, half, (group, group), 0), 1.0, 0.0
+    ).astype(BF)
+    dq_t[...] = jnp.zeros(dq_t.shape, F32)
+    for c in d_copies:
+        c.wait_recv()
+    totals.end(0)
+    totals.begin(1)
+    d_branch = dbg[...].reshape(group, MODEL_WIDTH)
+    w = wg[...].reshape(MODEL_WIDTH, width + qw)
+    d_attn_t = nn(d_branch, w[:, width:]).T.astype(BF)
+    d_sorted = nt(d_attn_t, perm[...])
+    for second in range(2):
+        piece = d_sorted[:, second * half : (second + 1) * half]
+        do_t[second] = piece.astype(BF)
+        product = piece * attn_t[second]
+        delta[second, :hl] = jnp.concatenate(
+            [
+                jnp.sum(product[a * HEAD_SIZE : (a + 1) * HEAD_SIZE], axis=0, keepdims=True)
+                for a in range(hl)
+            ],
+            axis=0,
+        )
+
+    def step_back(p, second):
+        block = kv[p, second]
+        lse_all, delta_all = lse[second], delta[second]
+        key_place = block_base(at, p, second, half) + lax.broadcasted_iota(
+            jnp.int32, (half, half), 0
+        )
+        own_place = block_base(at, at.b, second, half) + lax.broadcasted_iota(
+            jnp.int32, (half, half), 1
+        )
+        allowed = (key_place <= own_place) & (key_place >= begin[second])
+        d_keys, d_values = [None] * kl, [None] * kl
+        for a in range(hl):
+            g = a // (hl // kl)
+            rows_a = slice(a * HEAD_SIZE, (a + 1) * HEAD_SIZE)
+            key = block[:, g * HEAD_SIZE : (g + 1) * HEAD_SIZE]
+            value = block[:, kw + g * HEAD_SIZE : kw + (g + 1) * HEAD_SIZE]
+            scores = jnp.where(allowed, nn(key, qt[second, rows_a]), -1e30)
+            probs = jnp.exp(scores - lse_all[a : a + 1])
+            d_probs = nn(value, do_t[second, rows_a])
+            d_scores = (probs * (d_probs - delta_all[a : a + 1])).astype(BF)
+            d_key = nt(qt[second, rows_a], d_scores)
+            d_value = nt(do_t[second, rows_a], probs.astype(BF))
+            d_keys[g] = d_key if d_keys[g] is None else d_keys[g] + d_key
+            d_values[g] = d_value if d_values[g] is None else d_values[g] + d_value
+            dq_t[second, rows_a] += tn(key, d_scores)
+        return jnp.concatenate(d_keys + d_values, axis=0)
+
+    scatter = Scatter(at, *(kv_bufs.at[j] for j in range(4)), kv_sems)
+
+    def visit(step, unused):
+        i = nz - 1 - step // 4
+        second = lax.rem(step // 2, 2)
+        same = lax.rem(step, 2) == 1
+        z = jnp.where(second == 0, at.z - i, at.z + i)
+        p = 2 * z + jnp.where(same, at.core, 1 - at.core)
+        exists = (z >= 0) & (z < nz) & ((i > 0) | same | (at.core != second))
+
+        @pl.when(exists)
+        def _():
+            part = step_back(p, second)
+
+            @pl.when(jnp.logical_not(same))
+            def _():
+                scatter.give_sibling(z, part)
+
+            @pl.when(same & (i > 0))
+            def _():
+                scatter.give(z, part + scatter.from_sibling(z))
+
+            @pl.when(same & (i == 0))
+            def _():
+                own_kv[second] = part
+
+        return 0
+
+    lax.fori_loop(0, 4 * nz, visit, 0)
+    totals.end(1)
+    totals.begin(2)
+    wide = 256
+
+    def weight_part(first, left):
+        for c in range(MODEL_WIDTH // wide):
+            source = xg if first == 0 else dbg
+            piece = nn(left, source[:, :, c * wide : (c + 1) * wide].reshape(group, wide))
+            for j in range(wide // dl):
+                w_part[c * (wide // dl) + j, first : first + left.shape[0]] = piece[
+                    :, j * dl : (j + 1) * dl
+                ]
+
+    weight_part(width, ao_t[...])
+    own_kv[at.core] += scatter.from_sibling(at.z)
+    for z in range(nz):
+
+        @pl.when(at.z != z)
+        def _():
+            own_kv[jnp.where(at.z < z, 0, 1)] += scatter.taken(z)
+
+    d_sorted_t = []
+    for second in range(2):
+        cols = slice(second * half, (second + 1) * half)
+        both = own_kv[second]
+        turned = jnp.concatenate([dq_t[second] * scale, both[:kw]], axis=0)
+        turned = turn_rows(turned, cos[:, cols], -sin[:, cols])
+        d_sorted_t.append(jnp.concatenate([turned, both[kw:]], axis=0).astype(BF))
+    back = jnp.where(place_col[...] == sorted_place(at, half, (group, group), 1), 1.0, 0.0).astype(BF)
+    d_rows = (
+        nt(back[:, :half], d_sorted_t[0]) + nt(back[:, half:], d_sorted_t[1])
+    ).astype(BF)
+    d_rows_ref[...] = d_rows.reshape(nh, rows, width)
+    d_cols = (nn(d_sorted_t[0], perm[:half]) + nn(d_sorted_t[1], perm[half:])).astype(BF)
+    o_copies = []
+    for k in range(1, nh):
+        peer = at.head_peer(k)
+        out_send[peer] = nt(d_rows_ref[peer], w[:, :width]).astype(BF)
+        c = remote(
+            out_send.at[peer], out_recv.at[at.h], o_sems.at[0, k], o_sems.at[1, k], at.in_head(peer)
+        )
+        c.start()
+        o_copies.append(c)
+    own_normed = nt(d_rows_ref[at.h], w[:, :width])
+    weight_part(0, d_cols)
+    w_scatter = Scatter(at, *(w_bufs.at[j] for j in range(4)), w_sems)
+
+    def w_sib(step, unused):
+        z = lax.rem(at.z + 1 + step, nz)
+        w_scatter.give_sibling(z, w_part[2 * z + 1 - at.core])
+        return 0
+
+    lax.fori_loop(0, nz, w_sib, 0)
+
+    def w_along(step, unused):
+        z = lax.rem(at.z + 1 + step, nz)
+        w_scatter.give(z, w_part[2 * z + at.core] + w_scatter.from_sibling(z))
+        return 0
+
+    lax.fori_loop(0, nz - 1, w_along, 0)
+    for k in range(1, nh):
+        o_copies[k - 1].wait_recv()
+        own_normed = own_normed + out_recv[lax.rem(at.h + nh - k, nh)].astype(F32)
+    hidden = inputs[...].astype(F32)
+    factor = lax.rsqrt(jnp.mean(hidden * hidden, axis=-1, keepdims=True) + eps)
+    unit = hidden * factor
+    n1_head[at.h] = jnp.sum(own_normed * unit, axis=0, keepdims=True)
+    n1_copies = [
+        remote(n1_head.at[at.h], n1_head.at[at.h], n_sems.at[0, k], n_sems.at[1, k], at.in_head(at.head_peer(k)))
+        for k in range(1, nh)
+    ]
+    for c in n1_copies:
+        c.start()
+    weighted = own_normed * w_norm1[...]
+    grad_in[...] = d_middle[...] + factor * (
+        weighted - unit * jnp.mean(unit * weighted, axis=-1, keepdims=True)
+    )
+    for c in n1_copies:
+        c.wait_recv()
+    n1_blk[at.b] = sum_slots(n1_head, nh)
+    n1_blk_copies = [
+        remote(n1_blk.at[at.b], n1_blk.at[at.b], n_sems.at[0, nh + k], n_sems.at[1, nh + k], at.in_blk(at.blk_peer(k)))
+        for k in range(1, nb)
+    ]
+    for c in n1_blk_copies:
+        c.start()
+    total_w = w_part[at.b] + w_scatter.from_sibling(at.z)
+    grad_w[...] = total_w
+    for z in range(nz):
+
+        @pl.when(at.z != z)
+        def _():
+            grad_w[...] += w_scatter.taken(z)
+
+    for c in n1_blk_copies:
+        c.wait_recv()
+    grad_n1[...] = sum_slots(n1_blk, nb)
+    totals.end(2)
+    totals.finish()
+    scatter.finish()
+    w_scatter.finish()
+    for c in d_copies + o_copies + n1_copies + n1_blk_copies:
+        c.wait_send()
+
+
+def back(nb, nh, hl, kl, *operands):
+    inputs, kv, small = operands[0], operands[7], operands[15]
+    rows = inputs.shape[0]
+    group, half = rows * nh, rows * nh // 2
+    nz, dl = nb // 2, MODEL_WIDTH // nb
+    qw, kw = hl * HEAD_SIZE, kl * HEAD_SIZE
+    width = qw + 2 * kw
+    shape = jax.ShapeDtypeStruct
+    chunk = small.shape[1:]
+    return pl.pallas_call(
+        functools.partial(back_kernel, nb, nh, hl, kl),
+        out_shape=(
+            shape((rows, MODEL_WIDTH), F32),
+            shape((width + qw, dl), F32),
+            shape((1, MODEL_WIDTH), F32),
+            shape((nh,) + chunk, F32),
+        ),
+        in_specs=[VMEM] * 16,
+        out_specs=[VMEM] * 4,
+        scratch_shapes=[
+            pltpu.VMEM((nh, rows, MODEL_WIDTH), BF),
+            pltpu.VMEM((group, group), BF),
+            pltpu.VMEM((nh, rows, width), BF),
+            pltpu.VMEM((2, qw, half), BF),
+            pltpu.VMEM((2, max(hl, 8), half), F32),
+            pltpu.VMEM((2, qw, half), F32),
+            pltpu.VMEM((2, 2 * kw, half), F32),
+            pltpu.VMEM((4, nz, 2 * kw, half), BF),
+            pltpu.VMEM((nb, width + qw, dl), F32),
+            pltpu.VMEM((4, nz, width + qw, dl), BF),
+            pltpu.VMEM((nh, rows, MODEL_WIDTH), BF),
+            pltpu.VMEM((nh, rows, MODEL_WIDTH), BF),
+            pltpu.VMEM((nh, 1, MODEL_WIDTH), F32),
+            pltpu.VMEM((nb, 1, MODEL_WIDTH), F32),
+            pltpu.VMEM((nh,) + chunk, F32),
+            pltpu.VMEM((nb,) + chunk, F32),
+            pltpu.SemaphoreType.DMA((2, nh)),
+            pltpu.SemaphoreType.DMA((4, nz)),
+            pltpu.SemaphoreType.DMA((4, nz)),
+            pltpu.SemaphoreType.DMA((2, nh)),
+            pltpu.SemaphoreType.DMA((2, nh + nb)),
+            pltpu.SemaphoreType.DMA((2, 3, max(nh, nb))),
         ],
-        axis=-1,
-    )
+        compiler_params=pltpu.CompilerParams(collective_id=2, vmem_limit_bytes=56 * 2**20),
+        name="back",
+    )(*operands)
 
 
 def slot_numbers(routes, slot_order):
@@ -500,27 +882,11 @@
     )
 
 
-def fetch_attention(w_query, key_weight, value_weight, w_out):
-    return (
-        lax.all_gather(w_query, "blk", axis=0, tiled=True),
-        lax.all_gather(key_weight, "blk", axis=0, tiled=True),
-        lax.all_gather(value_weight, "blk", axis=0, tiled=True),
-        lax.all_gather(w_out, "blk", axis=1, tiled=True),
-    )
-
-
 def fetch_experts(w_gate, w_up, w_down):
     return (
         lax.all_gather(w_gate, "blk", axis=1, tiled=True),
         lax.all_gather(w_up, "blk", axis=1, tiled=True),
         lax.all_gather(w_down, "blk", axis=2, tiled=True),
-    )
-
-
-def fetch_keys(rotated_key, value_rows):
-    return (
-        lax.all_gather(rotated_key, "blk", axis=0, tiled=True),
-        lax.all_gather(value_rows, "blk", axis=0, tiled=True),
     )
 
 
@@ -551,92 +917,18 @@
     head_groups = heads_local // kv_local
     experts_local = E // head_count
     scale = 1.0 / math.sqrt(HEAD_SIZE)
-    query_all, key_all, value_all, out_all = fetch_attention(
-        w_query, key_weight, value_weight, w_out
-    )
     gate_all, up_all, down_all = fetch_experts(w_gate, w_up, w_down)
-    hidden = inputs.astype(jnp.float32)
-    scale_one = lax.rsqrt(jnp.mean(hidden * hidden, axis=-1, keepdims=True) + eps)
-    unit_one = hidden * scale_one
-    normed = (unit_one * w_norm1).astype(jnp.bfloat16)
-    gathered = lax.all_gather(normed, "head", axis=0, tiled=True)
-    begin_index = seq_begin(token_place, lengths)
-    first_row = lax.axis_index("blk") * group_rows
-    own_place = lax.dynamic_slice_in_dim(token_place, first_row, group_rows)
-    own_begin = lax.dynamic_slice_in_dim(begin_index, first_row, group_rows)
-    cosine_table, sine_table = seq_rotation(own_place, own_begin, HEAD_SIZE)
-    query = jnp.dot(gathered, query_all, preferred_element_type=jnp.float32)
-    key = jnp.dot(gathered, key_all, preferred_element_type=jnp.float32)
-    value_rows = jnp.dot(gathered, value_all, preferred_element_type=jnp.float32).astype(
-        jnp.bfloat16
-    )
-    rotated_query = turn_index(
-        query.reshape(group_rows, heads_local, HEAD_SIZE), cosine_table, sine_table
-    ).astype(jnp.bfloat16)
-    rotated_key = (
-        turn_index(key.reshape(group_rows, kv_local, HEAD_SIZE), cosine_table, sine_table)
-        .astype(jnp.bfloat16)
-        .reshape(group_rows, kv_local * HEAD_SIZE)
-    )
-    keys_all, values_all = fetch_keys(rotated_key, value_rows)
-    query_heads = rotated_query.reshape(group_rows, kv_local, head_groups, HEAD_SIZE)
-    steps = jnp.arange(blk_count, dtype=jnp.int32)
-
-    def block_scores(key_source, value_source, index):
-        start = index * group_rows
-        key_block = lax.dynamic_slice_in_dim(key_source, start, group_rows).reshape(
-            group_rows, kv_local, HEAD_SIZE
-        )
-        value_block = lax.dynamic_slice_in_dim(value_source, start, group_rows).reshape(
-            group_rows, kv_local, HEAD_SIZE
-        )
-        key_place = lax.dynamic_slice_in_dim(token_place, start, group_rows)
-        scores = (
-            jnp.einsum("qhgd,khd->hgqk", query_heads, key_block, preferred_element_type=jnp.float32)
-            * scale
-        )
-        allowed = (key_place[None, :] <= own_place[:, None]) & (
-            key_place[None, :] >= own_begin[:, None]
-        )
-        return (scores, allowed, key_block, value_block)
-
-    def stats_step(carry, index):
-        top, total = carry
-        scores, allowed, unused_keys, unused_values = block_scores(keys_all, values_all, index)
-        masked = jnp.where(allowed, scores, -1e30)
-        new_top = jnp.maximum(top, jnp.max(masked, axis=-1))
-        total = total * jnp.exp(top - new_top) + jnp.sum(
-            jnp.where(allowed, jnp.exp(masked - new_top[..., None]), 0.0), axis=-1
-        )
-        return ((new_top, total), None)
-
-    start_top = jnp.full((kv_local, head_groups, group_rows), -1e30, jnp.float32)
-    start_total = jnp.zeros((kv_local, head_groups, group_rows), jnp.float32)
-    (top, total), unused = lax.scan(stats_step, (start_top, start_total), steps)
-    log_total = top + jnp.log(total)
-
-    def out_step(acc, index):
-        scores, allowed, unused_keys, value_block = block_scores(keys_all, values_all, index)
-        probs = jnp.where(allowed, jnp.exp(scores - log_total[..., None]), 0.0).astype(jnp.bfloat16)
-        acc = acc + jnp.einsum(
-            "hgqk,khd->qhgd", probs, value_block, preferred_element_type=jnp.float32
-        )
-        return (acc, None)
-
-    attended32, unused = lax.scan(
-        out_step, jnp.zeros((group_rows, kv_local, head_groups, HEAD_SIZE), jnp.float32), steps
-    )
-    attended_rows = attended32.reshape(group_rows, heads_local * HEAD_SIZE).astype(jnp.bfloat16)
     own, begin_s, cos_o, sin_o, cos_s, sin_s, w_own = head_inputs(
         blk_count, head_count, rows, token_place, lengths, w_query, key_weight, value_weight, w_out
     )
-    middle = front(
-        blk_count, head_count, heads_local, kv_local, inputs, w_norm1.reshape(1, -1), w_norm2.reshape(1, -1),
-        w_own, own.reshape(1, -1), own.reshape(-1, 1), cos_o, sin_o, begin_s,
-    )[7]
+    gain_one = w_norm1.reshape(1, -1)
+    place_row, place_col = own.reshape(1, -1), own.reshape(-1, 1)
+    sizes = (blk_count, head_count, heads_local, kv_local)
+    gathered, weights, turned_q, kv, lse, attn_t, ao_t, middle, normed_two = front(
+        *sizes, inputs, gain_one, w_norm2.reshape(1, -1), w_own, place_row, place_col, cos_o, sin_o, begin_s
+    )
     scale_two = lax.rsqrt(jnp.mean(middle * middle, axis=-1, keepdims=True) + eps)
     unit_two = middle * scale_two
-    normed_two = (unit_two * w_norm2).astype(jnp.bfloat16)
     logits = jnp.dot(normed_two, router, preferred_element_type=jnp.float32)
     chosen = jnp.take_along_axis(logits, routes, axis=1)
     shifted = jnp.exp(chosen - jnp.max(chosen, axis=-1, keepdims=True))
@@ -668,11 +960,6 @@
     picked = returned[jnp.where(kept, target, 0)].astype(jnp.float32)
     mixed = jnp.sum(jnp.where(kept, gates, 0.0)[..., None] * picked, axis=1)
     output = (middle + mixed).astype(jnp.bfloat16)
-    query_all, key_all, value_all, out_all = fetch_attention(
-        w_query, key_weight, value_weight, w_out
-    )
-    gate_all, up_all, down_all = fetch_experts(w_gate, w_up, w_down)
-    keys_all, values_all = fetch_keys(rotated_key, value_rows)
     upstream = grad_out.astype(jnp.float32)
     d_gates = jnp.where(kept, jnp.sum(picked * upstream[:, None, :], axis=-1), 0.0)
     token_ids = jnp.broadcast_to(jnp.arange(rows, dtype=jnp.int32)[:, None], (rows, TOPK))
@@ -723,88 +1010,16 @@
     d_middle = upstream + scale_two * (
         weighted_two - unit_two * jnp.mean(unit_two * weighted_two, axis=-1, keepdims=True)
     )
-    d_branch = lax.all_gather(d_middle.astype(jnp.bfloat16), "head", axis=0, tiled=True)
-    grad_out_w = along_rows(attended_rows, d_branch)
-    d_attended = against(d_branch, out_all).astype(jnp.bfloat16)
-    d_heads = d_attended.reshape(group_rows, kv_local, head_groups, HEAD_SIZE)
-    delta = jnp.transpose(jnp.sum(d_heads.astype(jnp.float32) * attended32, axis=-1), (1, 2, 0))
-
-    def back_step(acc, index):
-        scores, allowed, key_block, value_block = block_scores(keys_all, values_all, index)
-        probs = jnp.where(allowed, jnp.exp(scores - log_total[..., None]), 0.0)
-        d_probs = jnp.einsum(
-            "qhgd,khd->hgqk", d_heads, value_block, preferred_element_type=jnp.float32
-        )
-        d_scores = (probs * (d_probs - delta[..., None])).astype(jnp.bfloat16)
-        acc = acc + jnp.einsum(
-            "hgqk,khd->qhgd", d_scores, key_block, preferred_element_type=jnp.float32
-        )
-        d_keys = (
-            jnp.einsum("hgqk,qhgd->khd", d_scores, query_heads, preferred_element_type=jnp.float32)
-            * scale
-        )
-        d_values = jnp.einsum(
-            "hgqk,qhgd->khd",
-            probs.astype(jnp.bfloat16),
-            d_heads,
-            preferred_element_type=jnp.float32,
-        )
-        return (
-            acc,
-            (
-                d_keys.reshape(group_rows, kv_local * HEAD_SIZE),
-                d_values.reshape(group_rows, kv_local * HEAD_SIZE),
-            ),
-        )
-
-    d_query_acc, (key_pieces, value_pieces) = lax.scan(
-        back_step, jnp.zeros((group_rows, kv_local, head_groups, HEAD_SIZE), jnp.float32), steps
-    )
-    d_key_rot, d_value_sum = (
-        lax.psum_scatter(
-            key_pieces.reshape(blk_count * group_rows, kv_local * HEAD_SIZE).astype(jnp.bfloat16),
-            "blk",
-            scatter_dimension=0,
-            tiled=True,
-        ).astype(jnp.float32),
-        lax.psum_scatter(
-            value_pieces.reshape(blk_count * group_rows, kv_local * HEAD_SIZE).astype(jnp.bfloat16),
-            "blk",
-            scatter_dimension=0,
-            tiled=True,
-        ).astype(jnp.float32),
-    )
-    d_query = (
-        turn_index(
-            d_query_acc.reshape(group_rows, heads_local, HEAD_SIZE) * scale,
-            cosine_table,
-            -sine_table,
-        )
-        .reshape(group_rows, heads_local * HEAD_SIZE)
-        .astype(jnp.bfloat16)
-    )
-    d_key = (
-        turn_index(d_key_rot.reshape(group_rows, kv_local, HEAD_SIZE), cosine_table, -sine_table)
-        .reshape(group_rows, kv_local * HEAD_SIZE)
-        .astype(jnp.bfloat16)
-    )
-    d_value = d_value_sum.astype(jnp.bfloat16)
-    grad_query_w = along_rows(gathered, d_query)
-    grad_key_w = along_rows(gathered, d_key)
-    grad_value_w = along_rows(gathered, d_value)
-    total = against(d_query, query_all)
-    total = total + against(d_key, key_all)
-    d_normed = lax.psum_scatter(
-        (total + against(d_value, value_all)).astype(jnp.bfloat16),
-        "head",
-        scatter_dimension=0,
-        tiled=True,
-    ).astype(jnp.float32)
-    weighted_one = d_normed * w_norm1
-    grad_norm1 = jnp.sum(d_normed * unit_one, axis=0)
-    grad_inputs = d_middle + scale_one * (
-        weighted_one - unit_one * jnp.mean(unit_one * weighted_one, axis=-1, keepdims=True)
-    )
+    small = jnp.concatenate(
+        [grad_router.T, grad_norm2[None], jnp.zeros((7, MODEL_WIDTH), F32)], axis=0
+    )
+    small = small.reshape(40, head_count, -1).transpose(1, 0, 2)
+    grad_inputs, grad_w, grad_norm1, small = back(
+        *sizes, inputs, gain_one, d_middle, weights, gathered, ao_t, turned_q, kv, lse, attn_t,
+        place_row, place_col, cos_s, sin_s, begin_s, small
+    )
+    small = small.transpose(1, 0, 2).reshape(40, MODEL_WIDTH)
+    qw, kw = heads_local * HEAD_SIZE, kv_local * HEAD_SIZE
     grad_gate = jnp.einsum(
         "secd,secf->edf", arrived, d_gate_pre, preferred_element_type=jnp.float32
     )
@@ -813,18 +1028,6 @@
         "secf,secd->efd", activated, d_returned, preferred_element_type=jnp.float32
     )
     sharded = (
-        lax.psum_scatter(
-            grad_query_w.astype(jnp.bfloat16), "blk", scatter_dimension=0, tiled=True
-        ).astype(jnp.float32),
-        lax.psum_scatter(
-            grad_key_w.astype(jnp.bfloat16), "blk", scatter_dimension=0, tiled=True
-        ).astype(jnp.float32),
-        lax.psum_scatter(
-            grad_value_w.astype(jnp.bfloat16), "blk", scatter_dimension=0, tiled=True
-        ).astype(jnp.float32),
-        lax.psum_scatter(
-            grad_out_w.astype(jnp.bfloat16), "blk", scatter_dimension=1, tiled=True
-        ).astype(jnp.float32),
         lax.psum_scatter(
             grad_gate.astype(jnp.bfloat16), "blk", scatter_dimension=1, tiled=True
         ).astype(jnp.float32),
@@ -835,20 +1038,19 @@
             grad_down.astype(jnp.bfloat16), "blk", scatter_dimension=2, tiled=True
         ).astype(jnp.float32),
     )
-    small = lax.psum((grad_norm1, grad_norm2, grad_router), ("blk", "head"))
     return (
         output,
         grad_inputs,
-        small[0],
+        grad_norm1.reshape(-1),
+        grad_w[:qw].T,
+        grad_w[qw : qw + kw].T,
+        grad_w[qw + kw : qw + 2 * kw].T,
+        grad_w[qw + 2 * kw :],
+        small[32],
+        small[:32].T,
         sharded[0],
         sharded[1],
         sharded[2],
-        sharded[3],
-        small[1],
-        small[2],
-        sharded[4],
-        sharded[5],
-        sharded[6],
     )
 
 

time: 1320 us -> 643 us (0.49)
  waiting for transfers between devices: 558 us -> 176 us
  matrix products: 213 us -> 72.2 us
  Pallas kernels: 59.8 us -> 198 us
  blocking collectives: 105 us -> 0 us
  local copies, waits for them, and re-layouts: 180 us -> 85.2 us
  other arithmetic: 132 us -> 68 us
  loops' own time: 17.5 us -> 0 us
    reduce_scatter x6 -> x0, waiting for transfers between devices: 145 us -> none  [the longest x1 29.8 us: on_device(): lax.psum_scatter(value_pieces.reshape(blk_count * group_rows, kv_local *...]
    dot_general x63 -> x0, matrix products: 134 us -> none  [the longest x8 31.6 us: back_step(): jnp.einsum('hgqk,qhgd->khd', probs.astype(jnp.bfloat16), d_heads, preferr...]
    psum x1 -> x0, waiting for transfers between devices: 125 us -> none  [on_device(): small = lax.psum((grad_norm1, grad_norm2, grad_router), ('blk', 'head'))]
    pallas_call x0 -> x1, Pallas kernels: none -> 89.7 us  [back(): pl.pallas_call(functools.partial(back_kernel, nb, nh, hl, kl), out_shape=...]
    reduce_scatter x1, waiting for transfers between devices: 86.1 us -> 3.91 us  [on_device(): lax.psum_scatter(grad_gate.astype(jnp.bfloat16), 'blk', scatter_dimension...]
    all_gather x4 -> x0, blocking collectives: 64.1 us -> none  [the longest x1 17.1 us: fetch_attention(): lax.all_gather(w_query, 'blk', axis=0, tiled=True)]
    dynamic_slice x80 -> x1, local copies, waits for them, and re-layouts: 63.5 us -> 0.76 us  [head_inputs(): own = lax.dynamic_slice_in_dim(token_place, b * group, group)]
    pallas_call x1, Pallas kernels: 59.8 us -> 109 us  [front(): pl.pallas_call(functools.partial(front_kernel, nb, nh, hl, kl), out_shape...]
  transfers between devices with their start and end apart: 22 -> 10, of which waited for: 12 -> 6; matrix products, arithmetic and copies ran while one was open for 27% -> 27% of each run, Pallas kernels for 5% -> 31%
where the time goes in v2:
time: 643 us; the launch traced here: 634 us
  Pallas kernels  198 us (31%)
  waiting for transfers between devices  176 us (27%)
  local copies, waits for them, and re-layouts  85.2 us (13%)
  matrix products  72.2 us (11%)
  other arithmetic  68 us (11%)
  starting transfers between devices  19.3 us (3%)
  between operations  15.2 us (2%)
    pallas_call x1, Pallas kernels, front(): pl.pallas_call(functools.partial(front_kernel, nb, nh, hl, kl), out_shape...  109 us
    reduce_scatter x1, waiting for transfers between devices, on_device(): lax.psum_scatter(grad_up.astype(jnp.bfloat16), 'blk', scatter_dimension=1...  95.4 us
    pallas_call x1, Pallas kernels, back(): pl.pallas_call(functools.partial(back_kernel, nb, nh, hl, kl), out_shape=...  89.7 us
    unnamed x77, local copies, waits for them, and re-layouts  39.2 us
    all_gather x1, waiting for transfers between devices, fetch_experts(): lax.all_gather(w_down, 'blk', axis=2, tiled=True)  24.9 us
    reduce_sum x1, other arithmetic, on_device(): slot_token = jnp.sum(jnp.where(match, token_ids[None], 0), axis=(1, 2))  23.5 us
    all_to_all x1, waiting for transfers between devices, on_device(): lax.all_to_all(d_arrived, 'head', split_axis=0, concat_axis=0, tiled=True)  17.5 us
    all_to_all x1, waiting for transfers between devices, on_device(): lax.all_to_all(expert_out, 'head', split_axis=0, concat_axis=0, tiled=True)  16.5 us
  transfers between devices with their start and end apart: 10, of which 6 were waited for; matrix products, arithmetic and copies ran while one was open for 27% of the time, Pallas kernels for 31%

profile of v2, /device:TPU:0, one launch (start us, length us, event | category | flops | bytes accessed | tf_op | source)
XLA Modules:
  0.0 634.0 jit_solution(10330800341723485961)
XLA Ops:
  13.3 108.8 %front.1 = (bf16[4,128,1024]{2,1,0:T(8,128)(2,1)S(1)}, bf16[8,128,768]{2,1,0:T(8,128)(2,1)S(1)}, bf16[2,256,256]{2,1,0:T(8,128)(2,1)S(1)}, bf16[8,2,256,256]{3,2...) custom-call(bf16[128,1024]{1,0:T(8,128)(2,1)S(1)} %copy-done.3, ...), custom_call_target="tpu_custom_call" | custom-call | tf_op jit(solution)/shard_map/front/pallas_call | solution.py:397
  127.2 7.0 %gather_fusion.4 = f32[1024]{0:T(1024)S(1)} fusion(f32[128,32]{0,1:T(8,128)S(1)} %fusion.51, s32[1024]{0:T(1024)S(1)} %reshape.339), kind=kCustom, calls=%fused_computation.4 | custom fusion | bytes 16384 | tf_op jit(solution)/shard_map/jit(take_along_axis)/gather | solution.py:933
  143.7 9.0 %reduce-window.20 = s32[32,8,128]{2,1,0:T(8,128)S(1)} reduce-window(s32[32,8,128]{2,1,0:T(8,128)S(1)} %fusion.39, s32[]{:T(128)} %constant.25.clone.1), window={size=1x1x128 pad=0_0x0_0x127_0}, to_apply=%region_4.5 | reduce-window | flops 4161536 | bytes 262148 | tf_op jit(solution)/shard_map/reduce-window.1
  158.0 6.7 %fusion.13 = pred[1280,128]{1,0:T(8,128)(4,1)S(1)} fusion(s32[128,8]{0,1:T(8,128)S(1)} %get-tuple-element.120, pred[128,8]{0,1:T(8,128)(4,1)S(1)} %get-tuple-element.118), kind=kLoop, calls=%fused_computation.29 | loop fusion | flops 3768320 | bytes 168960 | tf_op jit(solution)/shard_map/reduce_or | solution.py:940
  172.7 9.6 %select_reduce_fusion.1 = f32[1280]{0:T(1024)S(1)} fusion(f32[128,8]{0,1:T(8,128)S(1)} %get-tuple-element.117, s32[128,8]{0,1:T(8,128)S(1)} %get-tuple-element.120, pred[128,8]{0,1:T(8,128)(4,1)S(1)} %get-tuple-element.118), kind=kLoop, calls=%fused_computation.26 | loop fusion | flops 5241600 | bytes 14336 | tf_op jit(solution)/shard_map/reduce_sum | solution.py:967
  182.4 23.5 %select_reduce_fusion = s32[1280]{0:T(1024)S(1)} fusion(s32[128,8]{0,1:T(8,128)S(1)} %get-tuple-element.120, pred[128,8]{0,1:T(8,128)(4,1)S(1)} %get-tuple-element.118), kind=kLoop, calls=%fused_computation.25 | loop fusion | flops 5241600 | bytes 10240 | tf_op jit(solution)/shard_map/reduce_sum | solution.py:966
  206.0 5.7 gather_fusion.3
  220.6 7.4 %fusion.2 = f32[8,4,40,512]{3,2,1,0:T(8,128)} fusion(bf16[8,1024,512]{2,1,0:T(8,128)(2,1)} %all-gather.6.cloned.1.call-done, bf16[4,8,40,1024]{3,2,1,0:T(8,128)(2,1)} %all-to-all-done), kind=kOutput, calls=%fused_computation.11 | convolution fusion | flops 1342177280 | bytes 13631488 | tf_op jit(solution)/shard_map/secd,edf->secf/dot_general | solution.py:950
  228.1 7.7 %fusion.6 = f32[8,4,40,512]{3,2,1,0:T(8,128)} fusion(bf16[8,1024,512]{2,1,0:T(8,128)(2,1)} %all-gather.4.cloned.1.call-done, bf16[4,8,40,1024]{3,2,1,0:T(8,128)(2,1)} %all-to-all-done), kind=kOutput, calls=%fused_computation.15 | convolution fusion | flops 1342177280 | bytes 13631488 | tf_op jit(solution)/shard_map/secd,edf->secf/dot_general | solution.py:949
  235.7 15.4 %all-to-all-done.2 = bf16[4,8,40,1024]{3,2,1,0:T(8,128)(2,1)} async-done(((bf16[4,8,40,1024]{3,2,1,0:T(8,128)(2,1)}), bf16[4,8,40,1024]{3,2,1,0:T(8,128)(2,1)}, u32[]{:S(2)}, u32[]{:S(2)}) %all-to-all-start.2) | async-done | bytes 2621472 | tf_op jit(solution)/shard_map/all_to_all | solution.py:969
  251.1 24.9 %all-gather.8.cloned.1.call-done = bf16[8,512,1024]{2,1,0:T(8,128)(2,1)} async-done(((bf16[8,512,128]{2,1,0:T(8,128)(2,1)}), bf16[8,512,1024]{2,1,0:T(8,128)(2,1)}) %all-gather.8.cloned.1.call-update) | async-done | bytes 8388624 | tf_op jit(solution)/shard_map/all_gather | solution.py:889
  276.0 10.0 %fusion.19 = (bf16[4,8,40,512]{3,2,0,1:T(8,128)(2,1)}, bf16[4,8,40,512]{3,2,0,1:T(8,128)(2,1)S(1)}, bf16[4,8,40,512]{3,2,0,1:T(8,128)(2,1)S(1)}) fusion(f32[8,4,40,512]{3,2,1,0:T(8,128)} %fusion.2, f32[8,4,40,512]{3,2,1,0:T(8,128)} %fusion.6, bf16[8,512,1024]{2,1,0:T(8,128)(2,1)} %all-gather.8.cloned.1.call-done, bf16[4,8,40,1024]{3,2,1,0:T(8,128)(2,1)} %all-to-all-done.2), kind=kOutput, calls=%fused_computation.38 | convolution fusion | flops 1352007680 | bytes 20185088 | tf_op jit(solution)/shard_map/secd,efd->secf/dot_general | solution.py:976
  287.0 7.3 %bitcast_convert_fusion = bf16[8,512,1024]{2,1,0:T(8,128)(2,1)} fusion(bf16[4,8,40,512]{3,2,0,1:T(8,128)(2,1)S(1)} %get-tuple-element.122, bf16[4,8,40,1024]{3,2,1,0:T(8,128)(2,1)} %all-to-all-done.2), kind=kOutput, calls=%fused_computation.6 | convolution fusion | flops 1346371584 | bytes 12320768 | tf_op jit(solution)/shard_map/secf,secd->efd/dot_general | solution.py:1027
  294.4 12.8 %copy.182 = bf16[8,512,1024]{1,0,2:T(8,128)(2,1)} copy(bf16[8,512,1024]{2,1,0:T(8,128)(2,1)} %bitcast_convert_fusion) | data formatting | bytes 16777216
  307.1 12.2 %copy.186 = bf16[128,8,8,512]{3,1,2,0:T(8,128)(2,1)} copy(bf16[128,8,8,512]{3,2,1,0:T(8,128)(2,1)} %bitcast.172) | data formatting | bytes 16777216
  319.4 7.8 %bitcast_convert_fusion.2 = bf16[8,1024,512]{2,1,0:T(8,128)(2,1)} fusion(bf16[4,8,40,1024]{3,2,1,0:T(8,128)(2,1)} %all-to-all-done, bf16[4,8,40,512]{3,2,0,1:T(8,128)(2,1)} %get-tuple-element.121), kind=kOutput, calls=%fused_computation.8 | convolution fusion | flops 1346371584 | bytes 12320768 | tf_op jit(solution)/shard_map/secd,secf->edf/dot_general | solution.py:1023
  327.4 7.4 %bitcast_convert_fusion.1 = bf16[8,1024,512]{2,1,0:T(8,128)(2,1)} fusion(bf16[4,8,40,1024]{3,2,1,0:T(8,128)(2,1)} %all-to-all-done, bf16[4,8,40,512]{3,2,0,1:T(8,128)(2,1)S(1)} %get-tuple-element.123), kind=kOutput, calls=%fused_computation.7 | convolution fusion | flops 1346371584 | bytes 12320768 | tf_op jit(solution)/shard_map/secd,secf->edf/dot_general | solution.py:1026
  346.7 6.4 %fusion = f32[8,4,40,1024]{3,2,1,0:T(8,128)S(1)} fusion(bf16[4,8,40,512]{3,2,0,1:T(8,128)(2,1)S(1)} %get-tuple-element.123, bf16[8,1024,512]{2,1,0:T(8,128)(2,1)} %all-gather.6.cloned.1.call-done), kind=kOutput, calls=%fused_computation.9 | convolution fusion | flops 1342177280 | bytes 14942208 | tf_op jit(solution)/shard_map/secf,edf->secd/dot_general | solution.py:988
  353.1 6.5 %fusion.16 = bf16[4,8,40,1024]{3,2,0,1:T(8,128)(2,1)S(1)} fusion(f32[8,4,40,1024]{3,2,1,0:T(8,128)S(1)} %fusion, bf16[4,8,40,512]{3,2,0,1:T(8,128)(2,1)S(1)} %copy-done.17, bf16[8,1024,512]{2,1,0:T(8,128)(2,1)} %all-gather.4.cloned.1.call-done), kind=kOutput, calls=%fused_computation.33 | convolution fusion | flops 1344798720 | bytes 17563648 | tf_op jit(solution)/shard_map/secf,edf->secd/dot_general | solution.py:983
  361.4 16.5 %all-to-all-done.1 = bf16[4,8,40,1024]{3,2,1,0:T(8,128)(2,1)} async-done(((bf16[4,8,40,1024]{3,2,1,0:T(8,128)(2,1)}), bf16[4,8,40,1024]{3,2,1,0:T(8,128)(2,1)}, u32[]{:S(2)}, u32[]{:S(2)}) %all-to-all-start.1) | async-done | bytes 2621472 | tf_op jit(solution)/shard_map/all_to_all | solution.py:957
  385.1 7.1 %gather_fusion.2 = bf16[1024,1024]{1,0:T(8,128)(2,1)S(1)} fusion(bf16[1280,1024]{1,0:T(8,128)(2,1)} %bitcast.23, s32[1024]{0:T(1024)S(1)} %broadcast_clamp_fusion), kind=kCustom, calls=%fused_computation.2 | custom fusion | bytes 4198400 | tf_op jit(solution)/shard_map/gather | solution.py:960
  395.6 17.5 %all-to-all-done.3 = bf16[4,8,40,1024]{3,2,1,0:T(8,128)(2,1)} async-done(((bf16[4,8,40,1024]{3,2,1,0:T(8,128)(2,1)}), bf16[4,8,40,1024]{3,2,1,0:T(8,128)(2,1)}, u32[]{:S(2)}, u32[]{:S(2)}) %all-to-all-start.3) | async-done | bytes 2621472 | tf_op jit(solution)/shard_map/all_to_all | solution.py:990
  418.9 89.7 %back.1 = (f32[128,1024]{1,0:T(8,128)}, f32[768,128]{1,0:T(8,128)}, f32[1,1024]{1,0:T(1,128)}, f32[4,40,256]{2,1,0:T(8,128)}) custom-call(bf16[128,1024]{1,0:T(8,128)(2,1)} %inputs.3, f32[1,1024]{1,0:T(1,128)} %bitcast.169, f32[128,1024]{1,0:T(8,128)} %get-tuple-element.124.d_middle, bf16[8,128,768]{2,1,0:T(8,128)(2,1)} %copy-done.2, ...), custom_call_target="tpu_custom_call" | custom-call | tf_op jit(solution)/shard_map/back/pallas_call | solution.py:821
  527.1 95.4 %reduce-scatter.8.cloned.1.call-done = bf16[8,128,512]{2,1,0:T(8,128)(2,1)} async-done(((bf16[8,1024,512]{2,1,0:T(8,128)(2,1)}), bf16[8,128,512]{2,1,0:T(8,128)(2,1)}) %reduce-scatter.8.cloned.1.call-update) | async-done | bytes 1048592 | tf_op jit(solution)/shard_map/reduce_scatter | solution.py:1034
  (172 shorter events, 96.7 us)
Async XLA Ops:
  7.2 119.9 %copy-start = (bf16[1024,32]{0,1:T(8,128)(2,1)S(1)}, bf16[1024,32]{0,1:T(8,128)(2,1)}, u32[]{:S(2)}) copy-start(bf16[1024,32]{0,1:T(8,128)(2,1)} %param.25) | copy-start | bytes 196612
  7.3 6.0 copy-start.3
  7.3 6.0 copy-start.12
  7.3 6.0 copy-start.9
  7.3 213.3 %all-gather.6.cloned.1.call-start = ((), (), s32[]{:S(2)}) async-start(), calls=%async_computation.8 | async-start | bytes 9437184 | tf_op jit(solution)/shard_map/all_gather | solution.py:888
  8.0 220.0 %all-gather.4.cloned.1.call-start = ((), (), s32[]{:S(2)}) async-start(), calls=%async_computation.7 | async-start | bytes 9437184 | tf_op jit(solution)/shard_map/all_gather | solution.py:887
  8.8 267.2 %all-gather.8.cloned.1.call-start = ((), (), s32[]{:S(2)}) async-start(), calls=%async_computation.9 | async-start | bytes 9437184 | tf_op jit(solution)/shard_map/all_gather | solution.py:889
  10.4 123.9 %copy-start.8 = (s32[512]{0:T(512)}, s32[512]{0:T(512)S(1)}, u32[]{:S(2)}) copy-start(s32[512]{0:T(512)S(1)} %dynamic_slice.3) | copy-start | bytes 6148
  10.6 123.8 %copy-start.1 = (s32[512,1]{1,0:T(8,128)}, s32[512,1]{1,0:T(8,128)S(1)}, u32[]{:S(2)}) copy-start(s32[512,1]{1,0:T(8,128)S(1)} %copy.151.place_col) | copy-start | bytes 6148
  11.3 123.0 %copy-start.10 = (s32[512]{0:T(512)}, s32[512]{0:T(512)S(1)}, u32[]{:S(2)}) copy-start(s32[512]{0:T(512)S(1)} %get-tuple-element.114) | copy-start | bytes 6148
  127.2 7.3 %copy-start.27 = (s32[128,8]{0,1:T(8,128)S(1)}, s32[128,8]{0,1:T(8,128)}, u32[]{:S(2)}) copy-start(s32[128,8]{0,1:T(8,128)} %param.27) | copy-start | bytes 12292
  167.7 48.3 %all-to-all-start = ((bf16[4,8,40,1024]{3,2,1,0:T(8,128)(2,1)}), bf16[4,8,40,1024]{3,2,1,0:T(8,128)(2,1)}, u32[]{:S(2)}, u32[]{:S(2)}) async-start(bf16[4,8,40,1024]{3,2,1,0:T(8,128)(2,1)} %bitcast.13), calls=%async_computation | async-start | bytes 5242880 | tf_op jit(solution)/shard_map/all_to_all | solution.py:942
  216.0 35.1 %all-to-all-start.2 = ((bf16[4,8,40,1024]{3,2,1,0:T(8,128)(2,1)}), bf16[4,8,40,1024]{3,2,1,0:T(8,128)(2,1)}, u32[]{:S(2)}, u32[]{:S(2)}) async-start(bf16[4,8,40,1024]{3,2,1,0:T(8,128)(2,1)} %multiply_convert_fusion), calls=%async_computation.2 | async-start | bytes 5242880 | tf_op jit(solution)/shard_map/all_to_all | solution.py:969
  220.6 295.7 %reduce-scatter.10.cloned.1.call-start = ((), (), s32[]{:S(2)}) async-start(), calls=%async_computation.12 | async-start | bytes 9437184
  319.3 205.0 %reduce-scatter.6.cloned.1.call-start = ((), (), s32[]{:S(2)}) async-start(), calls=%async_computation.10 | async-start | bytes 9437184 | tf_op jit(solution)/shard_map/reduce_scatter | solution.py:1031
  327.2 295.3 %reduce-scatter.8.cloned.1.call-start = ((), (), s32[]{:S(2)}) async-start(), calls=%async_computation.11 | async-start | bytes 9437184 | tf_op jit(solution)/shard_map/reduce_scatter | solution.py:1034
  342.1 35.8 %all-to-all-start.1 = ((bf16[4,8,40,1024]{3,2,1,0:T(8,128)(2,1)}), bf16[4,8,40,1024]{3,2,1,0:T(8,128)(2,1)}, u32[]{:S(2)}, u32[]{:S(2)}) async-start(bf16[4,8,40,1024]{3,2,1,0:T(8,128)(2,1)} %copy.163), calls=%async_computation.1 | async-start | bytes 5242880 | tf_op jit(solution)/shard_map/all_to_all | solution.py:957
  346.6 6.4 %copy-start.17 = (bf16[4,8,40,512]{3,2,0,1:T(8,128)(2,1)S(1)}, bf16[4,8,40,512]{3,2,0,1:T(8,128)(2,1)}, u32[]{:S(2)}) copy-start(bf16[4,8,40,512]{3,2,0,1:T(8,128)(2,1)} %get-tuple-element.121) | copy-start | bytes 3932164
  377.9 35.2 %all-to-all-start.3 = ((bf16[4,8,40,1024]{3,2,1,0:T(8,128)(2,1)}), bf16[4,8,40,1024]{3,2,1,0:T(8,128)(2,1)}, u32[]{:S(2)}, u32[]{:S(2)}) async-start(bf16[4,8,40,1024]{3,2,1,0:T(8,128)(2,1)} %copy.166), calls=%async_computation.3 | async-start | bytes 5242880 | tf_op jit(solution)/shard_map/all_to_all | solution.py:990
  392.1 21.0 %copy-start.16 = (pred[1280,128]{1,0:T(8,128)(4,1)S(1)}, pred[1280,128]{1,0:T(8,128)(4,1)}, u32[]{:S(2)}) copy-start(pred[1280,128]{1,0:T(8,128)(4,1)} %copy-done.15) | copy-start | bytes 491524
  394.6 21.3 %copy-start.29 = (f32[128]{0:T(128)S(1)}, f32[128]{0:T(128)}, u32[]{:S(2)}) copy-start(f32[128]{0:T(128)} %add_rsqrt_fusion) | copy-start | bytes 1540
  394.6 22.0 %copy-start.20 = (bf16[1024,128]{1,0:T(8,128)(2,1)S(1)}, bf16[1024,128]{1,0:T(8,128)(2,1)}, u32[]{:S(2)}) copy-start(bf16[1024,128]{1,0:T(8,128)(2,1)} %copy.181) | copy-start | bytes 786436
  520.4 104.9 %copy-start.21 = (f32[128,1024]{1,0:T(8,128)S(1)}, f32[128,1024]{1,0:T(8,128)}, u32[]{:S(2)}) copy-start(f32[128,1024]{1,0:T(8,128)} %get-tuple-element.152) | copy-start | bytes 1572868
  527.1 99.0 %copy-start.28 = (f32[1,1024]{1,0:T(1,128)S(1)}, f32[1,1024]{1,0:T(1,128)}, u32[]{:S(2)}) copy-start(f32[1,1024]{1,0:T(1,128)} %get-tuple-element.35) | copy-start | bytes 12292
  (18 other events, 46.2 us)
Sparse Core Ops, SparseCore 0:
  9.7 100.6 all-gather.5
  112.1 81.1 all-gather.3
  194.9 81.0 all-gather.7
  319.4 87.8 reduce-scatter.9
  409.4 114.7 reduce-scatter.5
  526.4 96.0 reduce-scatter.7

commit v3 on v2

--- a/solution.py
+++ b/solution.py
@@ -172,11 +172,41 @@
     return jnp.concatenate(pieces, axis=0)
 
 
+def pick_targets(slots, pair_rows):
+    lane = lax.broadcasted_iota(jnp.int32, slots.shape, 1)
+    kept = (slots >= 0) & (slots < CAP)
+    return jnp.where(kept, slots + jnp.where(lane >= pair_rows // 2, CAP, 0), -1)
+
+
+def hits(target_row, pair_rows):
+    return lax.broadcasted_iota(jnp.int32, (2 * CAP, pair_rows), 0) == target_row
+
+
+def diagonal():
+    shape = (2 * CAP, 2 * CAP)
+    return lax.broadcasted_iota(jnp.int32, shape, 0) == lax.broadcasted_iota(jnp.int32, shape, 1)
+
+
+def to_row(column):
+    return jnp.sum(jnp.where(diagonal(), column, 0.0), axis=0, keepdims=True)
+
+
+def to_column(row):
+    return jnp.sum(jnp.where(diagonal(), row, 0.0), axis=1, keepdims=True)
+
+
+def split_product(dot, left, right):
+    high = left.astype(BF)
+    low = (left - high.astype(F32)).astype(BF)
+    return dot(high, right) + dot(low, right)
+
+
 def front_kernel(
     nb,
     nh,
     hl,
     kl,
+    repeat,
     inputs,
     w_norm1,
     w_norm2,
@@ -186,6 +216,9 @@
     cos,
     sin,
     begin,
+    grad_out,
+    table,
+    router_t,
     xg,
     wg,
     qt,
@@ -195,6 +228,11 @@
     ao_t,
     middle,
     n2,
+    slots,
+    own_gates,
+    in_gate,
+    in_rows,
+    in_g,
     ao,
     perm,
     top,
@@ -207,6 +245,23 @@
     kv_send,
     kv_recv,
     o_sems,
+    slot_all,
+    g_all,
+    n2_all,
+    gates,
+    out_rows,
+    out_g,
+    out_gate,
+    s_send,
+    s_recv,
+    g_send,
+    g_recv,
+    n_send,
+    n_recv,
+    row_sems,
+    g_sems,
+    gate_sems,
+    local_sems,
 ):
     at = Place(nb, nh)
     rows = inputs.shape[0]
@@ -219,6 +274,8 @@
     unit = hidden * lax.rsqrt(jnp.mean(hidden * hidden, axis=-1, keepdims=True) + eps)
     xg[at.h] = (unit * w_norm1[...]).astype(BF)
     wg[at.b] = w_own[...]
+    slot_all[at.b] = table[...]
+    g_all[at.b] = grad_out[...]
     at.meet()
     x_copies = [
         remote(xg.at[at.h], xg.at[at.h], x_sems.at[0, k], x_sems.at[1, k], at.in_head(at.head_peer(k)))
@@ -228,11 +285,84 @@
         c.start()
     weights = Relay(at, wg, w_send, w_recv)
     weights.begin()
+    slot_relay = Relay(at, slot_all, s_send, s_recv)
+    slot_relay.begin()
+    g_relay = Relay(at, g_all, g_send, g_recv)
+    g_relay.begin()
+    pair = 2 * rows
+    own_expert = (at.b // repeat) * nh
+
+    def go(buf_out, buf_in, sems, z, k):
+        peer = at.head_peer(k)
+        return remote(
+            buf_out.at[z, peer],
+            buf_in.at[z, at.h],
+            sems.at[0, z, k],
+            sems.at[1, z, k],
+            at.in_head(peer),
+        )
+
+    def keep(buf_out, buf_in, j, z):
+        return pltpu.make_async_copy(buf_out.at[z, at.h], buf_in.at[z, at.h], local_sems.at[j, z])
+
+    def outward(relay, body, first, last):
+        def step(t, unused):
+            d, side = t // 2, lax.rem(t, 2)
+            z = jnp.where(side == 0, at.z - d, at.z + d)
+            pl.when((side == 0) & (d > 0))(lambda: relay.hop(d))
+
+            @pl.when((z >= 0) & (z < at.nz) & ((d > 0) | (side == 0)))
+            def _():
+                relay.take_sibling(z)
+                body(z)
+
+            return 0
+
+        lax.fori_loop(2 * first, 2 * last, step, 0)
+
+    def send_g(z):
+        x = g_all[pl.ds(2 * z, 2)].reshape(pair, MODEL_WIDTH)
+        for k in list(range(1, nh)) + [0]:
+            peer = at.head_peer(k)
+            hit = hits(pick_targets(slots[z, pl.ds(own_expert + peer, 1)], pair), pair)
+            out_g[z, peer] = nn(jnp.where(hit, 1.0, 0.0).astype(BF), x).astype(BF)
+            if k == 0:
+                keep(out_g, in_g, 0, z).start()
+            else:
+                go(out_g, in_g, g_sems, z, k).start()
+
+    def send_rows(z):
+        x = n2_all[pl.ds(2 * z, 2)].reshape(pair, MODEL_WIDTH)
+        routed = slots[z] >= 0
+        logits = jnp.where(routed, nt(router_t[...], x), -1e30)
+        shifted = jnp.exp(logits - jnp.max(logits, axis=0, keepdims=True))
+        shifted = jnp.where(routed, shifted, 0.0)
+        gates[z] = shifted / jnp.sum(shifted, axis=0, keepdims=True)
+        for k in list(range(1, nh)) + [0]:
+            peer = at.head_peer(k)
+            hit = hits(pick_targets(slots[z, pl.ds(own_expert + peer, 1)], pair), pair)
+            gate_row = gates[z, pl.ds(own_expert + peer, 1)]
+            gate = to_row(jnp.sum(jnp.where(hit, gate_row, 0.0), axis=1, keepdims=True))
+            out_rows[z, peer] = nn(jnp.where(hit, 1.0, 0.0).astype(BF), x).astype(BF)
+            if k == 0:
+                keep(out_rows, in_rows, 1, z).start()
+                in_gate[z, at.h] = gate
+            else:
+                go(out_rows, in_rows, row_sems, z, k).start()
+                out_gate[z, peer] = gate
+                go(out_gate, in_gate, gate_sems, z, k).start()
+
     perm[...] = jnp.where(
         place_row[...] == sorted_place(at, half, (group, group), 0), 1.0, 0.0
     ).astype(BF)
     for i in range(1, nb // 2):
+        slot_relay.hop(i)
         weights.hop(i)
+    for z in range(nb // 2):
+        slot_relay.take_sibling(z)
+    for z in range(nb // 2):
+        slots[z] = jnp.concatenate([slot_all[2 * z], slot_all[2 * z + 1]], axis=1)
+    outward(g_relay, send_g, 0, 1)
     for z in range(nb // 2):
         weights.take_sibling(z)
     for c in x_copies:
@@ -262,6 +392,7 @@
     q_cols = (nt(qkv_t[:qw], order) * (1.0 / math.sqrt(HEAD_SIZE))).astype(BF)
     qt[0] = q_cols[:, :half]
     qt[1] = q_cols[:, half:]
+    outward(g_relay, send_g, 1, 2)
     top[...] = jnp.full(top.shape, -1e30, F32)
     total[...] = jnp.zeros(total.shape, F32)
     attn_t[...] = jnp.zeros(attn_t.shape, F32)
@@ -352,6 +483,7 @@
         )
         c.start()
         o_copies.append(c)
+    outward(g_relay, send_g, 2, at.nz)
     for k in range(1, nh):
         o_copies[k - 1].wait_recv()
         middle[...] += out_recv[lax.rem(at.h + nh - k, nh)].astype(F32)
@@ -359,7 +491,13 @@
     n2[...] = (
         mid * lax.rsqrt(jnp.mean(mid * mid, axis=-1, keepdims=True) + eps) * w_norm2[...]
     ).astype(BF)
-    weights.finish()
+    n2_all[at.b] = n2[...]
+    n_relay = Relay(at, n2_all, n_send, n_recv)
+    n_relay.begin()
+    outward(n_relay, send_rows, 0, at.nz)
+    own_gates[...] = jnp.where(at.core == 0, gates[at.z, :, :rows], gates[at.z, :, rows:])
+    for relay in (weights, slot_relay, g_relay, n_relay):
+        relay.finish()
     for c in x_copies + o_copies:
         c.wait_send()
 
@@ -387,15 +525,36 @@
 
     lax.fori_loop(0, nb, drain, 0)
 
-
-def front(nb, nh, hl, kl, inputs, w_norm1, w_norm2, w_own, place_row, place_col, cos, sin, begin):
+    def end(z, unused):
+        for k in range(1, nh):
+            for move in (
+                go(out_g, in_g, g_sems, z, k),
+                go(out_rows, in_rows, row_sems, z, k),
+                go(out_gate, in_gate, gate_sems, z, k),
+            ):
+                move.wait_recv()
+                move.wait_send()
+        keep(out_g, in_g, 0, z).wait()
+        keep(out_rows, in_rows, 1, z).wait()
+        return 0
+
+    lax.fori_loop(0, at.nz, end, 0)
+
+
+def front(nb, nh, hl, kl, repeat, *operands):
+    inputs, w_own = operands[0], operands[3]
     rows = inputs.shape[0]
     group, half = rows * nh, rows * nh // 2
+    nz = nb // 2
     dl, wide = w_own.shape
     qw, kw = hl * HEAD_SIZE, kl * HEAD_SIZE
     shape = jax.ShapeDtypeStruct
+    dma = pltpu.SemaphoreType.DMA
+    chunk = (nz, nh, 2 * CAP, MODEL_WIDTH)
+    line = (nz, nh, 1, 2 * CAP)
+    relay_sems = [dma((3, nb)), dma((nb,))]
     return pl.pallas_call(
-        functools.partial(front_kernel, nb, nh, hl, kl),
+        functools.partial(front_kernel, nb, nh, hl, kl, repeat),
         out_shape=(
             shape((nh, rows, MODEL_WIDTH), BF),
             shape((nb, dl, wide), BF),
@@ -406,9 +565,14 @@
             shape((qw, group), BF),
             shape((rows, MODEL_WIDTH), F32),
             shape((rows, MODEL_WIDTH), BF),
+            shape((nz, E, 2 * rows), jnp.int32),
+            shape((E, rows), F32),
+            shape(line, F32),
+            shape(chunk, BF),
+            shape(chunk, BF),
         ),
-        in_specs=[VMEM] * 9,
-        out_specs=[VMEM] * 9,
+        in_specs=[VMEM] * 12,
+        out_specs=[VMEM] * 12 + [ANY] * 2,
         scratch_shapes=[
             pltpu.VMEM((group, qw), BF),
             pltpu.VMEM((group, group), BF),
@@ -416,16 +580,30 @@
             pltpu.VMEM((2, max(hl, 8), half), F32),
             pltpu.VMEM((nh, rows, MODEL_WIDTH), BF),
             pltpu.VMEM((nh, rows, MODEL_WIDTH), BF),
-            pltpu.SemaphoreType.DMA((2, nh)),
-            pltpu.SemaphoreType.DMA((3, nb)),
-            pltpu.SemaphoreType.DMA((nb,)),
-            pltpu.SemaphoreType.DMA((2, nb)),
-            pltpu.SemaphoreType.DMA((nb,)),
-            pltpu.SemaphoreType.DMA((2, nh)),
+            dma((2, nh)),
+            dma((3, nb)),
+            dma((nb,)),
+            dma((2, nb)),
+            dma((nb,)),
+            dma((2, nh)),
+            pltpu.VMEM((nb, E, rows), jnp.int32),
+            pltpu.VMEM((nb, rows, MODEL_WIDTH), BF),
+            pltpu.VMEM((nb, rows, MODEL_WIDTH), BF),
+            pltpu.VMEM((nz, E, 2 * rows), F32),
+            pltpu.VMEM(chunk, BF),
+            pltpu.VMEM(chunk, BF),
+            pltpu.VMEM(line, F32),
+            *relay_sems,
+            *relay_sems,
+            *relay_sems,
+            dma((2, nz, nh)),
+            dma((2, nz, nh)),
+            dma((2, nz, nh)),
+            dma((2, nz)),
         ],
-        compiler_params=pltpu.CompilerParams(collective_id=1, vmem_limit_bytes=48 * 2**20),
+        compiler_params=pltpu.CompilerParams(collective_id=1, vmem_limit_bytes=60 * 2**20),
         name="front",
-    )(inputs, w_norm1, w_norm2, w_own, place_row, place_col, cos, sin, begin)
+    )(*operands)
 
 
 def seq_begin(token_position, lengths):
@@ -456,6 +634,74 @@
     return own, begin_s.reshape(2, 1, half), cos_o, sin_o, cos_s, sin_s, w_own
 
 
+def slot_table(nb, nh, repeat, routes, slot_order):
+    local = E // nh
+    mine = (routes % local) * nh + routes // local
+    match = mine.T[:, None, :] == jnp.arange(E, dtype=jnp.int32)[None, :, None]
+    order = jnp.min(jnp.where(match, slot_order.T[:, None, :], 1 << 20), axis=0)
+    before = jnp.sum((order[:, :, None] < order[:, None, :]).astype(jnp.int32), axis=1)
+    return jnp.where(order < (1 << 20), before, -1)
+
+
+def experts_kernel(nz, nh, x_ref, g_ref, gate_ref, w, d_rows, scaled, d_gate_row, grads, sums):
+    step = pl.program_id(0)
+    fr = w.shape[-1]
+    nb, dl = grads.shape[0], grads.shape[2]
+
+    @pl.when(step == 0)
+    def _():
+        sums[...] = jnp.zeros(sums.shape, F32)
+
+    x = x_ref[0].reshape(nh * 2 * CAP, MODEL_WIDTH)
+    gate = jnp.concatenate([to_column(gate_ref[0, h]) for h in range(nh)], axis=0)
+    w_gate = w[:, 0].reshape(MODEL_WIDTH, fr)
+    w_up = w[:, 1].reshape(MODEL_WIDTH, fr)
+    w_down_t = w[:, 2].reshape(MODEL_WIDTH, fr)
+    gate_pre, up_pre = nn(x, w_gate), nn(x, w_up)
+    sigma = 1.0 / (1.0 + jnp.exp(-gate_pre))
+    swish = gate_pre * sigma
+    activated = (swish * up_pre).astype(BF)
+    out = nt(activated, w_down_t).astype(BF).astype(F32)
+    g = g_ref[0].reshape(nh * 2 * CAP, MODEL_WIDTH).astype(F32)
+    d_gate = jnp.sum(out * g, axis=1, keepdims=True)
+    d_out = (gate * g).astype(BF)
+    scaled[0] = (gate * out).astype(BF).reshape(nh, 2 * CAP, MODEL_WIDTH)
+    d_act = nn(d_out, w_down_t)
+    d_gate_pre = (d_act * up_pre * sigma * (1.0 + gate_pre * (1.0 - sigma))).astype(BF)
+    d_up_pre = (d_act * swish).astype(BF)
+    back_rows = (nt(d_gate_pre, w_gate) + nt(d_up_pre, w_up)).astype(BF)
+    d_rows[0] = back_rows.reshape(nh, 2 * CAP, MODEL_WIDTH)
+    for h in range(nh):
+        d_gate_row[0, h] = to_row(d_gate[h * 2 * CAP : (h + 1) * 2 * CAP])
+    sums[0] += tn(x, d_gate_pre)
+    sums[1] += tn(x, d_up_pre)
+    sums[2] += tn(d_out, activated)
+
+    @pl.when(step == nz - 1)
+    def _():
+        for j in range(3):
+            for p in range(nb):
+                grads[p, j] = sums[j, p * dl : (p + 1) * dl].astype(BF)
+
+
+def experts(nz, nh, x, g, gate, w):
+    fr = w.shape[-1]
+    shape = jax.ShapeDtypeStruct
+    wide = pl.BlockSpec((1,) + x.shape[1:], lambda i: (i, 0, 0, 0))
+    line = pl.BlockSpec((1,) + gate.shape[1:], lambda i: (i, 0, 0, 0))
+    whole = pl.BlockSpec(w.shape, lambda i: (0, 0, 0, 0))
+    return pl.pallas_call(
+        functools.partial(experts_kernel, nz, nh),
+        grid=(nz,),
+        out_shape=(shape(x.shape, BF), shape(x.shape, BF), shape(gate.shape, F32), shape(w.shape, BF)),
+        in_specs=[wide, wide, line, whole],
+        out_specs=[wide, wide, line, whole],
+        scratch_shapes=[pltpu.VMEM((3, MODEL_WIDTH, fr), F32)],
+        compiler_params=pltpu.CompilerParams(vmem_limit_bytes=60 * 2**20),
+        name="experts",
+    )(x, g, gate, w)
+
+
 class Scatter:
     def __init__(self, at, sib_out, sib_in, z_out, z_in, sems):
         self.at, self.sib_out, self.sib_in, self.z_out, self.z_in = at, sib_out, sib_in, z_out, z_in
@@ -561,9 +807,17 @@
     nh,
     hl,
     kl,
+    repeat,
     inputs,
     w_norm1,
-    d_middle,
+    w_norm2,
+    middle,
+    n2,
+    grad_out,
+    router_t,
+    slots,
+    own_gates,
+    d_gate_rows,
     wg,
     xg,
     ao_t,
@@ -576,7 +830,9 @@
     cos,
     sin,
     begin,
-    small,
+    d_rows,
+    scaled,
+    output,
     grad_in,
     grad_w,
     grad_n1,
@@ -603,6 +859,21 @@
     o_sems,
     n_sems,
     s_sems,
+    small,
+    back_rows,
+    in_dgate,
+    own_part,
+    d_middle,
+    dg_out,
+    dg_in,
+    sc_bufs,
+    sc_sems,
+    mix_sems,
+    ret_sems,
+    eout_sems,
+    dgate_sems,
+    dg_sems,
+    local_sems,
 ):
     at = Place(nb, nh)
     nz = at.nz
@@ -614,14 +885,129 @@
     dl = MODEL_WIDTH // nb
     scale = 1.0 / math.sqrt(HEAD_SIZE)
 
+    pair = 2 * rows
+    own_expert = (at.b // repeat) * nh
+    at.meet()
+
+    def go(buf_out, buf_in, sems, z, k):
+        peer = at.head_peer(k)
+        return remote(
+            buf_out.at[z, peer],
+            buf_in.at[z, at.h],
+            sems.at[0, z, k],
+            sems.at[1, z, k],
+            at.in_head(peer),
+        )
+
+    def keep(buf_out, j, z):
+        return pltpu.make_async_copy(buf_out.at[z, at.h], back_rows.at[z, at.h], local_sems.at[j, z])
+
+    def far_first(body):
+        def step(t, unused):
+            body(lax.rem(at.z + 1 + t, nz))
+            return 0
+
+        lax.fori_loop(0, nz, step, 0)
+
+    def send_back(z):
+        for k in range(1, nh):
+            go(d_rows, back_rows, ret_sems, z, k).start()
+            go(d_gate_rows, in_dgate, dgate_sems, z, k).start()
+        keep(d_rows, 0, z).start()
+        in_dgate[z, at.h] = d_gate_rows[z, at.h]
+
+    far_first(send_back)
+    n2_scatter = Scatter(at, *(sc_bufs.at[j] for j in range(4)), sc_sems)
+
+    def dg_copy(p):
+        return remote(
+            dg_out.at[p], dg_in.at[at.b], dg_sems.at[0, p], dg_sems.at[1, at.b], at.in_blk(p)
+        )
+
+    def masks_of(z):
+        return [
+            hits(pick_targets(slots[z, pl.ds(own_expert + h, 1)], pair), pair) for h in range(nh)
+        ]
+
+    def spread(z, masks, scatter):
+        hit_rows = jnp.concatenate([jnp.where(m, 1.0, 0.0).astype(BF) for m in masks], axis=0)
+        part = tn(hit_rows, back_rows[z].reshape(nh * 2 * CAP, MODEL_WIDTH))
+        own_part[0] = part[:rows]
+        own_part[1] = part[rows:]
+        scatter.give_sibling(z, own_part[1 - at.core])
+
+        @pl.when(z != at.z)
+        def _():
+            scatter.give(z, own_part[at.core] + scatter.from_sibling(z))
+
+    def gathered_part(scatter):
+        own_part[2] = own_part[at.core] + scatter.from_sibling(at.z)
+        for z in range(nz):
+
+            @pl.when(at.z != z)
+            def _():
+                own_part[2] += scatter.taken(z)
+
+        return own_part[2]
+
+    def gather_back(z):
+        for k in range(1, nh):
+            go(d_rows, back_rows, ret_sems, z, k).wait_recv()
+            go(d_gate_rows, in_dgate, dgate_sems, z, k).wait_recv()
+        keep(d_rows, 0, z).wait()
+        masks = masks_of(z)
+        d_gates = jnp.concatenate(
+            [
+                jnp.sum(jnp.where(m, to_column(in_dgate[z, h]), 0.0), axis=0, keepdims=True)
+                for h, m in enumerate(masks)
+            ],
+            axis=0,
+        )
+        dg_out[2 * z] = d_gates[:, :rows]
+        dg_out[2 * z + 1] = d_gates[:, rows:]
+        pl.when(z == at.z)(lambda: dg_copy(at.sibling).start())
+
+        @pl.when(z != at.z)
+        def _():
+            dg_copy(2 * z).start()
+            dg_copy(2 * z + 1).start()
+
+        spread(z, masks, n2_scatter)
+
+    far_first(gather_back)
+    dg_in[at.b] = dg_out[at.b]
+    for k in range(1, nb):
+        p = at.blk_peer(k)
+        remote(dg_out.at[p], dg_in.at[p], dg_sems.at[0, p], dg_sems.at[1, p], at.in_blk(p)).wait_recv()
+    d_gates = jnp.concatenate(
+        [sum_slots(dg_in.at[pl.ds(i * repeat, repeat)], repeat) for i in range(nb // repeat)], axis=0
+    )
+    d_logits = own_gates[...] * (
+        d_gates - jnp.sum(own_gates[...] * d_gates, axis=0, keepdims=True)
+    )
+    from_logits = split_product(tn, d_logits, router_t[...])
+    g_router = split_product(nn, d_logits, n2[...])
+    mid = middle[...]
+    factor_two = lax.rsqrt(jnp.mean(mid * mid, axis=-1, keepdims=True) + eps)
+    unit_two = mid * factor_two
+    d_n2 = gathered_part(n2_scatter) + from_logits
+    weighted_two = d_n2 * w_norm2[...]
+    d_middle[...] = grad_out[...].astype(F32) + factor_two * (
+        weighted_two - unit_two * jnp.mean(unit_two * weighted_two, axis=-1, keepdims=True)
+    )
     dbg[at.h] = d_middle[...].astype(BF)
-    at.meet()
     d_copies = [
         remote(dbg.at[at.h], dbg.at[at.h], d_sems.at[0, k], d_sems.at[1, k], at.in_head(at.head_peer(k)))
         for k in range(1, nh)
     ]
     for c in d_copies:
         c.start()
+    g_norm = jnp.sum(d_n2 * unit_two, axis=0, keepdims=True)
+    slab = MODEL_WIDTH // nh
+    for h in range(nh):
+        cols = slice(h * slab, (h + 1) * slab)
+        small[h, :E] = g_router[:, cols]
+        small[h, E:] = jnp.broadcast_to(g_norm[:, cols], (8, slab))
     totals = Total(at, small, s_head, s_blk, small_sum, s_sems)
     totals.begin(0)
     perm[...] = jnp.where(
@@ -630,6 +1016,13 @@
     dq_t[...] = jnp.zeros(dq_t.shape, F32)
     for c in d_copies:
         c.wait_recv()
+
+    def send_scaled(z):
+        for k in range(1, nh):
+            go(scaled, back_rows, eout_sems, z, k).start()
+        keep(scaled, 1, z).start()
+
+    far_first(send_scaled)
     totals.end(0)
     totals.begin(1)
     d_branch = dbg[...].reshape(group, MODEL_WIDTH)
@@ -733,10 +1126,10 @@
         turned = turn_rows(turned, cos[:, cols], -sin[:, cols])
         d_sorted_t.append(jnp.concatenate([turned, both[kw:]], axis=0).astype(BF))
     back = jnp.where(place_col[...] == sorted_place(at, half, (group, group), 1), 1.0, 0.0).astype(BF)
-    d_rows = (
+    turned_back = (
         nt(back[:, :half], d_sorted_t[0]) + nt(back[:, half:], d_sorted_t[1])
     ).astype(BF)
-    d_rows_ref[...] = d_rows.reshape(nh, rows, width)
+    d_rows_ref[...] = turned_back.reshape(nh, rows, width)
     d_cols = (nn(d_sorted_t[0], perm[:half]) + nn(d_sorted_t[1], perm[half:])).astype(BF)
     o_copies = []
     for k in range(1, nh):
@@ -764,6 +1157,16 @@
         return 0
 
     lax.fori_loop(0, nz - 1, w_along, 0)
+    n2_scatter.finish()
+    mix_scatter = Scatter(at, *(sc_bufs.at[j] for j in range(4)), mix_sems)
+
+    def mix(z):
+        for k in range(1, nh):
+            go(scaled, back_rows, eout_sems, z, k).wait_recv()
+        keep(scaled, 1, z).wait()
+        spread(z, masks_of(z), mix_scatter)
+
+    far_first(mix)
     for k in range(1, nh):
         o_copies[k - 1].wait_recv()
         own_normed = own_normed + out_recv[lax.rem(at.h + nh - k, nh)].astype(F32)
@@ -802,32 +1205,46 @@
         c.wait_recv()
     grad_n1[...] = sum_slots(n1_blk, nb)
     totals.end(2)
+    output[...] = (middle[...] + gathered_part(mix_scatter)).astype(BF)
     totals.finish()
     scatter.finish()
+    mix_scatter.finish()
+
+    def drain(z):
+        for k in range(1, nh):
+            go(d_rows, back_rows, ret_sems, z, k).wait_send()
+            go(d_gate_rows, in_dgate, dgate_sems, z, k).wait_send()
+            go(scaled, back_rows, eout_sems, z, k).wait_send()
+
+    far_first(drain)
+    for k in range(1, nb):
+        dg_copy(at.blk_peer(k)).wait_send()
     w_scatter.finish()
     for c in d_copies + o_copies + n1_copies + n1_blk_copies:
         c.wait_send()
 
 
-def back(nb, nh, hl, kl, *operands):
-    inputs, kv, small = operands[0], operands[7], operands[15]
-    rows = inputs.shape[0]
+def back(nb, nh, hl, kl, repeat, *operands):
+    rows = operands[0].shape[0]
     group, half = rows * nh, rows * nh // 2
     nz, dl = nb // 2, MODEL_WIDTH // nb
     qw, kw = hl * HEAD_SIZE, kl * HEAD_SIZE
     width = qw + 2 * kw
     shape = jax.ShapeDtypeStruct
-    chunk = small.shape[1:]
+    dma = pltpu.SemaphoreType.DMA
+    chunk = (E + 8, MODEL_WIDTH // nh)
+    line = (nz, nh, 1, 2 * CAP)
     return pl.pallas_call(
-        functools.partial(back_kernel, nb, nh, hl, kl),
+        functools.partial(back_kernel, nb, nh, hl, kl, repeat),
         out_shape=(
+            shape((rows, MODEL_WIDTH), BF),
             shape((rows, MODEL_WIDTH), F32),
             shape((width + qw, dl), F32),
             shape((1, MODEL_WIDTH), F32),
             shape((nh,) + chunk, F32),
         ),
-        in_specs=[VMEM] * 16,
-        out_specs=[VMEM] * 4,
+        in_specs=[VMEM] * 22 + [ANY] * 2,
+        out_specs=[VMEM] * 5,
         scratch_shapes=[
             pltpu.VMEM((nh, rows, MODEL_WIDTH), BF),
             pltpu.VMEM((group, group), BF),
@@ -845,49 +1262,31 @@
             pltpu.VMEM((nb, 1, MODEL_WIDTH), F32),
             pltpu.VMEM((nh,) + chunk, F32),
             pltpu.VMEM((nb,) + chunk, F32),
-            pltpu.SemaphoreType.DMA((2, nh)),
-            pltpu.SemaphoreType.DMA((4, nz)),
-            pltpu.SemaphoreType.DMA((4, nz)),
-            pltpu.SemaphoreType.DMA((2, nh)),
-            pltpu.SemaphoreType.DMA((2, nh + nb)),
-            pltpu.SemaphoreType.DMA((2, 3, max(nh, nb))),
+            dma((2, nh)),
+            dma((4, nz)),
+            dma((4, nz)),
+            dma((2, nh)),
+            dma((2, nh + nb)),
+            dma((2, 3, max(nh, nb))),
+            pltpu.VMEM((nh,) + chunk, F32),
+            pltpu.VMEM((nz, nh, 2 * CAP, MODEL_WIDTH), BF),
+            pltpu.VMEM(line, F32),
+            pltpu.VMEM((3, rows, MODEL_WIDTH), F32),
+            pltpu.VMEM((rows, MODEL_WIDTH), F32),
+            pltpu.VMEM((nb, nh, rows), F32),
+            pltpu.VMEM((nb, nh, rows), F32),
+            pltpu.VMEM((4, nz, rows, MODEL_WIDTH), BF),
+            dma((4, nz)),
+            dma((4, nz)),
+            dma((2, nz, nh)),
+            dma((2, nz, nh)),
+            dma((2, nz, nh)),
+            dma((2, nb)),
+            dma((2, nz)),
         ],
-        compiler_params=pltpu.CompilerParams(collective_id=2, vmem_limit_bytes=56 * 2**20),
+        compiler_params=pltpu.CompilerParams(collective_id=2, vmem_limit_bytes=60 * 2**20),
         name="back",
     )(*operands)
-
-
-def slot_numbers(routes, slot_order):
-    flat_expert = routes.reshape(-1)
-    rank = slot_order.reshape(-1)
-    count = flat_expert.shape[0]
-    by_rank = jnp.zeros((count,), jnp.int32).at[rank].set(jnp.arange(count, dtype=jnp.int32))
-    expert_sorted = flat_expert[by_rank]
-    onehot = (expert_sorted[:, None] == jnp.arange(E, dtype=jnp.int32)[None, :]).astype(jnp.int32)
-    before = jnp.cumsum(onehot, axis=0) - onehot
-    slot_sorted = jnp.sum(before * onehot, axis=1)
-    slot = slot_sorted[rank].reshape(routes.shape)
-    return (slot, slot < CAP)
-
-
-def along_rows(left, right):
-    return lax.dot_general(
-        left, right, (((0,), (0,)), ((), ())), preferred_element_type=jnp.float32
-    )
-
-
-def against(left, right):
-    return lax.dot_general(
-        left, right, (((1,), (1,)), ((), ())), preferred_element_type=jnp.float32
-    )
-
-
-def fetch_experts(w_gate, w_up, w_down):
-    return (
-        lax.all_gather(w_gate, "blk", axis=1, tiled=True),
-        lax.all_gather(w_up, "blk", axis=1, tiled=True),
-        lax.all_gather(w_down, "blk", axis=2, tiled=True),
-    )
 
 
 def on_device(
@@ -909,135 +1308,99 @@
     grad_out,
 ):
     rows = inputs.shape[0]
-    blk_count = lax.axis_size("blk")
-    head_count = lax.axis_size("head")
-    group_rows = rows * head_count
-    heads_local = w_query.shape[1] // HEAD_SIZE
-    kv_local = key_weight.shape[1] // HEAD_SIZE
-    head_groups = heads_local // kv_local
-    experts_local = E // head_count
-    scale = 1.0 / math.sqrt(HEAD_SIZE)
-    gate_all, up_all, down_all = fetch_experts(w_gate, w_up, w_down)
+    nb, nh = lax.axis_size("blk"), lax.axis_size("head")
+    nz = nb // 2
+    hl = w_query.shape[1] // HEAD_SIZE
+    kl = key_weight.shape[1] // HEAD_SIZE
+    local, dl, hidden_units = w_gate.shape
+    repeat = nb // local
+    fr = hidden_units // repeat
+    qw, kw = hl * HEAD_SIZE, kl * HEAD_SIZE
+
+    def by_part(v):
+        v = v.reshape(local, dl, repeat, fr).transpose(0, 2, 1, 3)
+        return v.reshape(nb, dl, fr)
+
+    projections = jnp.stack(
+        [by_part(w_gate), by_part(w_up), by_part(w_down.transpose(0, 2, 1))], axis=1
+    )
+    projections = lax.all_to_all(projections, "blk", split_axis=0, concat_axis=0, tiled=True)
     own, begin_s, cos_o, sin_o, cos_s, sin_s, w_own = head_inputs(
-        blk_count, head_count, rows, token_place, lengths, w_query, key_weight, value_weight, w_out
+        nb, nh, rows, token_place, lengths, w_query, key_weight, value_weight, w_out
     )
-    gain_one = w_norm1.reshape(1, -1)
+    gain_one, gain_two = w_norm1.reshape(1, -1), w_norm2.reshape(1, -1)
     place_row, place_col = own.reshape(1, -1), own.reshape(-1, 1)
-    sizes = (blk_count, head_count, heads_local, kv_local)
-    gathered, weights, turned_q, kv, lse, attn_t, ao_t, middle, normed_two = front(
-        *sizes, inputs, gain_one, w_norm2.reshape(1, -1), w_own, place_row, place_col, cos_o, sin_o, begin_s
+    sizes = (nb, nh, hl, kl, repeat)
+    router_t = router.T.reshape(nh, local, MODEL_WIDTH).transpose(1, 0, 2).reshape(E, MODEL_WIDTH)
+    (
+        gathered,
+        weights,
+        turned_q,
+        kv,
+        lse,
+        attn_t,
+        ao_t,
+        middle,
+        normed_two,
+        slots,
+        own_gates,
+        in_gate,
+        in_rows,
+        in_g,
+    ) = front(
+        *sizes,
+        inputs,
+        gain_one,
+        gain_two,
+        w_own,
+        place_row,
+        place_col,
+        cos_o,
+        sin_o,
+        begin_s,
+        grad_out,
+        slot_table(nb, nh, repeat, routes, slot_order),
+        router_t,
     )
-    scale_two = lax.rsqrt(jnp.mean(middle * middle, axis=-1, keepdims=True) + eps)
-    unit_two = middle * scale_two
-    logits = jnp.dot(normed_two, router, preferred_element_type=jnp.float32)
-    chosen = jnp.take_along_axis(logits, routes, axis=1)
-    shifted = jnp.exp(chosen - jnp.max(chosen, axis=-1, keepdims=True))
-    gates = shifted / jnp.sum(shifted, axis=-1, keepdims=True)
-    slot, kept = slot_numbers(routes, slot_order)
-    target = routes * CAP + slot
-    slot_ids = jnp.arange(E * CAP, dtype=jnp.int32)
-    match = (target[None, :, :] == slot_ids[:, None, None]) & kept[None, :, :]
-    dispatch = jnp.any(match, axis=-1).astype(jnp.bfloat16)
-    buffer = jnp.dot(dispatch, normed_two, preferred_element_type=jnp.float32).astype(jnp.bfloat16)
-    arrived = lax.all_to_all(
-        buffer.reshape(head_count, experts_local, CAP, MODEL_WIDTH),
-        "head",
-        split_axis=0,
-        concat_axis=0,
-        tiled=True,
+    d_rows, scaled, d_gate_rows, grads = experts(nz, nh, in_rows, in_g, in_gate, projections)
+    grads = lax.all_to_all(grads, "blk", split_axis=0, concat_axis=0, tiled=True)
+    output, grad_inputs, grad_w, grad_norm1, small = back(
+        *sizes,
+        inputs,
+        gain_one,
+        gain_two,
+        middle,
+        normed_two,
+        grad_out,
+        router_t,
+        slots,
+        own_gates,
+        d_gate_rows,
+        weights,
+        gathered,
+        ao_t,
+        turned_q,
+        kv,
+        lse,
+        attn_t,
+        place_row,
+        place_col,
+        cos_s,
+        sin_s,
+        begin_s,
+        d_rows,
+        scaled,
     )
-    gate_pre = jnp.einsum("secd,edf->secf", arrived, gate_all, preferred_element_type=jnp.float32)
-    up_pre = jnp.einsum("secd,edf->secf", arrived, up_all, preferred_element_type=jnp.float32)
-    sigma = jax.nn.sigmoid(gate_pre)
-    swish = gate_pre * sigma
-    activated = (swish * up_pre).astype(jnp.bfloat16)
-    expert_out = jnp.einsum(
-        "secf,efd->secd", activated, down_all, preferred_element_type=jnp.float32
-    ).astype(jnp.bfloat16)
-    returned = lax.all_to_all(expert_out, "head", split_axis=0, concat_axis=0, tiled=True).reshape(
-        E * CAP, MODEL_WIDTH
+
+    small = small.transpose(1, 0, 2).reshape(E + 8, MODEL_WIDTH)
+    grad_router = (
+        small[:E].reshape(local, nh, MODEL_WIDTH).transpose(1, 0, 2).reshape(E, MODEL_WIDTH).T
     )
-    picked = returned[jnp.where(kept, target, 0)].astype(jnp.float32)
-    mixed = jnp.sum(jnp.where(kept, gates, 0.0)[..., None] * picked, axis=1)
-    output = (middle + mixed).astype(jnp.bfloat16)
-    upstream = grad_out.astype(jnp.float32)
-    d_gates = jnp.where(kept, jnp.sum(picked * upstream[:, None, :], axis=-1), 0.0)
-    token_ids = jnp.broadcast_to(jnp.arange(rows, dtype=jnp.int32)[:, None], (rows, TOPK))
-    slot_token = jnp.sum(jnp.where(match, token_ids[None], 0), axis=(1, 2))
-    slot_gate = jnp.sum(jnp.where(match, gates[None], 0.0), axis=(1, 2))
-    d_slots = (slot_gate[:, None] * upstream[slot_token]).astype(jnp.bfloat16)
-    d_returned = lax.all_to_all(
-        d_slots.reshape(head_count, experts_local, CAP, MODEL_WIDTH),
-        "head",
-        split_axis=0,
-        concat_axis=0,
-        tiled=True,
-    )
-    d_activated = jnp.einsum(
-        "secd,efd->secf", d_returned, down_all, preferred_element_type=jnp.float32
-    )
-    d_gate_pre = (d_activated * up_pre * sigma * (1.0 + gate_pre * (1.0 - sigma))).astype(
-        jnp.bfloat16
-    )
-    d_up_pre = (d_activated * swish).astype(jnp.bfloat16)
-    d_arrived = jnp.einsum(
-        "secf,edf->secd", d_gate_pre, gate_all, preferred_element_type=jnp.float32
-    )
-    d_arrived = (
-        d_arrived
-        + jnp.einsum("secf,edf->secd", d_up_pre, up_all, preferred_element_type=jnp.float32)
-    ).astype(jnp.bfloat16)
-    d_buffer = lax.all_to_all(d_arrived, "head", split_axis=0, concat_axis=0, tiled=True).reshape(
-        E * CAP, MODEL_WIDTH
-    )
-    d_normed_two = along_rows(dispatch, d_buffer)
-    weighted = jnp.sum(gates * d_gates, axis=-1, keepdims=True)
-    d_chosen = gates * (d_gates - weighted)
-    route_hits = routes[..., None] == jnp.arange(E, dtype=jnp.int32)[None, None, :]
-    d_logits = jnp.sum(jnp.where(route_hits, d_chosen[..., None], 0.0), axis=1)
-    router_wide = router.astype(jnp.float32)
-    d_normed_two = d_normed_two + lax.dot_general(
-        d_logits, router_wide, (((1,), (1,)), ((), ())), precision=lax.Precision.HIGHEST
-    )
-    grad_router = lax.dot_general(
-        normed_two.astype(jnp.float32),
-        d_logits,
-        (((0,), (0,)), ((), ())),
-        precision=lax.Precision.HIGHEST,
-    )
-    weighted_two = d_normed_two * w_norm2
-    grad_norm2 = jnp.sum(d_normed_two * unit_two, axis=0)
-    d_middle = upstream + scale_two * (
-        weighted_two - unit_two * jnp.mean(unit_two * weighted_two, axis=-1, keepdims=True)
-    )
-    small = jnp.concatenate(
-        [grad_router.T, grad_norm2[None], jnp.zeros((7, MODEL_WIDTH), F32)], axis=0
-    )
-    small = small.reshape(40, head_count, -1).transpose(1, 0, 2)
-    grad_inputs, grad_w, grad_norm1, small = back(
-        *sizes, inputs, gain_one, d_middle, weights, gathered, ao_t, turned_q, kv, lse, attn_t,
-        place_row, place_col, cos_s, sin_s, begin_s, small
-    )
-    small = small.transpose(1, 0, 2).reshape(40, MODEL_WIDTH)
-    qw, kw = heads_local * HEAD_SIZE, kv_local * HEAD_SIZE
-    grad_gate = jnp.einsum(
-        "secd,secf->edf", arrived, d_gate_pre, preferred_element_type=jnp.float32
-    )
-    grad_up = jnp.einsum("secd,secf->edf", arrived, d_up_pre, preferred_element_type=jnp.float32)
-    grad_down = jnp.einsum(
-        "secf,secd->efd", activated, d_returned, preferred_element_type=jnp.float32
-    )
-    sharded = (
-        lax.psum_scatter(
-            grad_gate.astype(jnp.bfloat16), "blk", scatter_dimension=1, tiled=True
-        ).astype(jnp.float32),
-        lax.psum_scatter(
-            grad_up.astype(jnp.bfloat16), "blk", scatter_dimension=1, tiled=True
-        ).astype(jnp.float32),
-        lax.psum_scatter(
-            grad_down.astype(jnp.bfloat16), "blk", scatter_dimension=2, tiled=True
-        ).astype(jnp.float32),
-    )
+
+    def whole_part(v):
+        v = v.reshape(local, repeat, dl, fr).transpose(0, 2, 1, 3)
+        return v.reshape(local, dl, hidden_units).astype(F32)
+
     return (
         output,
         grad_inputs,
@@ -1046,49 +1409,52 @@
         grad_w[qw : qw + kw].T,
         grad_w[qw + kw : qw + 2 * kw].T,
         grad_w[qw + 2 * kw :],
-        small[32],
-        small[:32].T,
-        sharded[0],
-        sharded[1],
-        sharded[2],
+        small[E],
+        grad_router,
+        whole_part(grads[:, 0]),
+        whole_part(grads[:, 1]),
+        whole_part(grads[:, 2]).transpose(0, 2, 1),
     )
 
 
 def solution(mesh):
+    rows, whole = P(("blk", "head"), None), P()
+    pair, out = P("blk", "head"), P("head", "blk")
+    first, last = P("head", "blk", None), P("head", None, "blk")
     return jax.shard_map(
         on_device,
         mesh=mesh,
         in_specs=(
-            P(("blk", "head"), None),
-            P(),
-            P(),
-            P(),
-            P("blk", "head"),
-            P("blk", "head"),
-            P("blk", "head"),
-            P("head", "blk"),
-            P(),
-            P(),
-            P(("blk", "head"), None),
-            P(("blk", "head"), None),
-            P("head", "blk", None),
-            P("head", "blk", None),
-            P("head", None, "blk"),
-            P(("blk", "head"), None),
+            rows,
+            whole,
+            whole,
+            whole,
+            pair,
+            pair,
+            pair,
+            out,
+            whole,
+            whole,
+            rows,
+            rows,
+            first,
+            first,
+            last,
+            rows,
         ),
         out_specs=(
-            P(("blk", "head"), None),
-            P(("blk", "head"), None),
-            P(),
-            P("blk", "head"),
-            P("blk", "head"),
-            P("blk", "head"),
-            P("head", "blk"),
-            P(),
-            P(),
-            P("head", "blk", None),
-            P("head", "blk", None),
-            P("head", None, "blk"),
+            rows,
+            rows,
+            whole,
+            pair,
+            pair,
+            pair,
+            out,
+            whole,
+            whole,
+            first,
+            first,
+            last,
         ),
         check_vma=False,
     )

time: 643 us -> 405 us (0.63); the launches traced: 634 us -> 404 us
  waiting for transfers between devices: 176 us -> 0.01 us
  Pallas kernels: 198 us -> 365 us
  matrix products: 72.2 us -> 0 us
  local copies, waits for them, and re-layouts: 85.2 us -> 19 us
  other arithmetic: 68 us -> 9.24 us
  between operations: 15.2 us -> 0.89 us
  starting transfers between devices: 19.3 us -> 10.3 us
    pallas_call x2 -> x3, Pallas kernels: 198 us -> 365 us  [the longest x1 175 us: back(): pl.pallas_call(functools.partial(back_kernel, nb, nh, hl, kl, repeat), ou...]
    reduce_scatter x2 -> x0, waiting for transfers between devices: 99.3 us -> none  [the longest x1 95.4 us: on_device(): lax.psum_scatter(grad_up.astype(jnp.bfloat16), 'blk', scatter_dimension=1...]
    dot_general x14 -> x0, matrix products: 72.2 us -> none  [the longest x1 9.99 us: on_device(): jnp.einsum('secd,efd->secf', d_returned, down_all, preferred_element_type...]
    all_to_all x4 -> x2, waiting for transfers between devices: 49.4 us -> 0.01 us  [the longest x1 0.01 us: on_device(): lax.all_to_all(projections, 'blk', split_axis=0, concat_axis=0, tiled=True)]
    reduce_sum x8 -> x1, other arithmetic: 35.8 us -> 0.69 us  [slot_table(): jnp.sum((order[:, :, None] < order[:, None, :]).astype(jnp.int32), axis=1)]
    gather x9 -> x0, local copies, waits for them, and re-layouts: 29.2 us -> none  [the longest x5 7.37 us: on_device(): chosen = jnp.take_along_axis(logits, routes, axis=1)]
    unnamed x77 -> x41, local copies, waits for them, and re-layouts: 39.2 us -> 10.9 us
    all_gather x3 -> x0, waiting for transfers between devices: 24.9 us -> none  [the longest x1 24.9 us: fetch_experts(): lax.all_gather(w_down, 'blk', axis=2, tiled=True)]
  transfers between devices with their start and end apart: 10 -> 2, of which waited for: 6 -> 0; matrix products, arithmetic and copies ran while one was open for 27% -> 4% of each run, Pallas kernels for 31% -> 85%
where the time goes in v3:
time: 405 us; the launch traced here: 404 us
  Pallas kernels  365 us (90%)
  local copies, waits for them, and re-layouts  19 us (5%)
  starting transfers between devices  10.3 us (3%)
  other arithmetic  9.24 us (2%)
    pallas_call x1, Pallas kernels, back(): pl.pallas_call(functools.partial(back_kernel, nb, nh, hl, kl, repeat), ou...  175 us
    pallas_call x1, Pallas kernels, front(): pl.pallas_call(functools.partial(front_kernel, nb, nh, hl, kl, repeat), o...  167 us
    pallas_call x1, Pallas kernels, experts(): pl.pallas_call(functools.partial(experts_kernel, nz, nh), grid=(nz,), out...  22.5 us
    unnamed x41, local copies, waits for them, and re-layouts  10.9 us
  transfers between devices with their start and end apart: 2, of which 0 were waited for; matrix products, arithmetic and copies ran while one was open for 4% of the time, Pallas kernels for 85%

profile of v3, /device:TPU:0, one launch (start us, length us, event | category | flops | bytes accessed | tf_op | source)
XLA Modules:
  0.0 404.4 jit_solution(3373364828276375946)
XLA Ops:
  0.7 1.6 copy.59
  2.5 2.0 pad_maximum_fusion
  4.5 6.5 %all-to-all-start = ((bf16[8,3,128,512]{3,2,1,0:T(8,128)(2,1)}), bf16[8,3,128,512]{3,2,1,0:T(8,128)(2,1)S(1)}, u32[]{:S(2)}, u32[]{:S(2)}) async-start(bf16[8,3,128,512]{3,2,1,0:T(8,128)(2,1)} %pad_maximum_fusion), calls=%async_computation | async-start | bytes 6291456 | tf_op jit(solution)/shard_map/all_to_all | solution.py:1327
  12.1 0.8 dynamic_slice.3
  12.9 0.9 copy.58.place_col
  15.3 0.8 subtract_convert_fusion
  16.7 1.2 multiply_sine_fusion
  17.9 167.5 %front.1 = (bf16[4,128,1024]{2,1,0:T(8,128)(2,1)}, bf16[8,128,768]{2,1,0:T(8,128)(2,1)}, bf16[2,256,256]{2,1,0:T(8,128)(2,1)}, bf16[8,2,256,256]{3,2,1,0:T(8,128...) custom-call(bf16[128,1024]{1,0:T(8,128)(2,1)} %inputs.3, ...), custom_call_target="tpu_custom_call" | custom-call | tf_op jit(solution)/shard_map/front/pallas_call | solution.py:556
  185.4 1.7 copy-done
  187.1 22.5 %experts.1 = (bf16[4,4,80,1024]{3,2,1,0:T(8,128)(2,1)}, bf16[4,4,80,1024]{3,2,1,0:T(8,128)(2,1)}, f32[4,4,1,80]{3,2,1,0:T(1,128)}, bf16[8,3,128,512]{3,2,1,0:T(8,128)(2,1)}) custom-call(bf16[4,4,80,1024]{3,2,1,0:T(8,128)(2,1)} %get-tuple-element.39.x_ref, bf16[4,4,80,1024]{3,2,1,0:T(8,128)(2,1)} %get-tuple-element.40.g_ref, ...), custom_call_target="tpu_custom_call" | custom-call | tf_op jit(solution)/shard_map/experts/pallas_call | solution.py:693
  209.6 3.8 all-to-all-start.1
  213.4 175.0 %back.1 = (bf16[128,1024]{1,0:T(8,128)(2,1)}, f32[128,1024]{1,0:T(8,128)}, f32[768,128]{1,0:T(8,128)}, f32[1,1024]{1,0:T(1,128)}, f32[4,40,256]{2,1,0:T(8,128)}) custom-call(bf16[128,1024]{1,0:T(8,128)(2,1)} %inputs.3, f32[1,1024]{1,0:T(1,128)} %bitcast.72, f32[1,1024]{1,0:T(1,128)} %bitcast.74, f32[128,1024]{1,0:T(8,128)} %get-tuple-element.35.middle, ...), custom_call_target="tpu_custom_call" | custom-call | tf_op jit(solution)/shard_map/back/pallas_call | solution.py:1237
  388.4 1.4 slice.48
  389.7 0.9 slice.49
  390.9 0.7 copy.69
  391.6 0.9 slice_bitcast_fusion.4
  392.5 0.7 copy.65
  393.2 0.7 copy.64
  393.9 1.6 fusion.9
  395.6 0.8 copy.63
  396.3 3.0 convert_bitcast_fusion
  399.3 2.9 copy.66
  402.3 0.7 copy.74
  403.0 0.8 copy.75
  (50 shorter events, 4.2 us)
Async XLA Ops:
  0.6 1.7 copy-start.1
  0.7 1.8 copy-start.2
  4.5 6.5 %copy-start.15 = (s32[4]{0:T(128)S(1)}, s32[4]{0:T(128)}, u32[]{:S(2)}) copy-start(s32[4]{0:T(128)} %param.18) | copy-start | bytes 52
  4.5 6.8 %copy-start.5 = (bf16[256,128]{1,0:T(8,128)(2,1)S(1)}, bf16[256,128]{1,0:T(8,128)(2,1)}, u32[]{:S(2)}) copy-start(bf16[256,128]{1,0:T(8,128)(2,1)} %param.23) | copy-start | bytes 196612
  4.5 6.9 %copy-start.6 = (bf16[1024,32]{0,1:T(8,128)(2,1)S(1)}, bf16[1024,32]{0,1:T(8,128)(2,1)}, u32[]{:S(2)}) copy-start(bf16[1024,32]{0,1:T(8,128)(2,1)} %param.25) | copy-start | bytes 196612
  4.5 9.4 %copy-start.12 = (s32[128,8]{0,1:T(8,128)S(1)}, s32[128,8]{0,1:T(8,128)}, u32[]{:S(2)}) copy-start(s32[128,8]{0,1:T(8,128)} %param.26) | copy-start | bytes 12292
  4.5 9.4 %copy-start.14 = (s32[128,8]{0,1:T(8,128)S(1)}, s32[128,8]{0,1:T(8,128)}, u32[]{:S(2)}) copy-start(s32[128,8]{0,1:T(8,128)} %param.27) | copy-start | bytes 12292
  4.5 9.4 %copy-start.7 = (bf16[128,256]{1,0:T(8,128)(2,1)S(1)}, bf16[128,256]{1,0:T(8,128)(2,1)}, u32[]{:S(2)}) copy-start(bf16[128,256]{1,0:T(8,128)(2,1)} %param.20) | copy-start | bytes 196612
  4.5 9.4 %copy-start.10 = (bf16[128,128]{1,0:T(8,128)(2,1)S(1)}, bf16[128,128]{1,0:T(8,128)(2,1)}, u32[]{:S(2)}) copy-start(bf16[128,128]{1,0:T(8,128)(2,1)} %param.22) | copy-start | bytes 98308
  4.5 9.4 %copy-start.11 = (bf16[128,128]{1,0:T(8,128)(2,1)S(1)}, bf16[128,128]{1,0:T(8,128)(2,1)}, u32[]{:S(2)}) copy-start(bf16[128,128]{1,0:T(8,128)(2,1)} %param.21) | copy-start | bytes 98308
  4.5 180.9 %all-to-all-start = ((bf16[8,3,128,512]{3,2,1,0:T(8,128)(2,1)}), bf16[8,3,128,512]{3,2,1,0:T(8,128)(2,1)S(1)}, u32[]{:S(2)}, u32[]{:S(2)}) async-start(bf16[8,3,128,512]{3,2,1,0:T(8,128)(2,1)} %pad_maximum_fusion), calls=%async_computation | async-start | bytes 6291456 | tf_op jit(solution)/shard_map/all_to_all | solution.py:1327
  12.9 5.1 %copy-start.8 = (s32[512]{0:T(512)}, s32[512]{0:T(512)S(1)}, u32[]{:S(2)}) copy-start(s32[512]{0:T(512)S(1)} %dynamic_slice.3) | copy-start | bytes 6148
  13.8 4.1 %copy-start.9 = (s32[512]{0:T(512)}, s32[512]{0:T(512)S(1)}, u32[]{:S(2)}) copy-start(s32[512]{0:T(512)S(1)} %get-tuple-element.106) | copy-start | bytes 6148
  185.4 1.7 copy-start
  209.6 186.8 %all-to-all-start.1 = ((bf16[8,3,128,512]{3,2,1,0:T(8,128)(2,1)}), bf16[8,3,128,512]{3,2,1,0:T(8,128)(2,1)S(1)}, u32[]{:S(2)}, u32[]{:S(2)}) async-start(bf16[8,3,128,512]{3,2,1,0:T(8,128)(2,1)} %get-tuple-element.57), calls=%async_computation.1 | async-start | bytes 6291456 | tf_op jit(solution)/shard_map/all_to_all | solution.py:1366
  399.3 3.0 copy-start.4
  399.3 3.7 copy-start.3
  399.3 4.5 %copy-start.13 = (f32[1,1024]{1,0:T(1,128)S(1)}, f32[1,1024]{1,0:T(1,128)}, u32[]{:S(2)}) copy-start(f32[1,1024]{1,0:T(1,128)} %get-tuple-element.54) | copy-start | bytes 12292

commit v4 on v3

--- a/solution.py
+++ b/solution.py
@@ -18,6 +18,8 @@
 ANY = pl.BlockSpec(memory_space=pl.ANY)
 BF = jnp.bfloat16
 F32 = jnp.float32
+FRONT_DEAL = (0.1, 0.6)
+BACK_DEAL = (0.1, 0.4, 0.55)
 
 eps = 1e-06
 rope_base = 10000.0
@@ -44,6 +46,34 @@
         device_id=device,
         device_id_type=MESH,
     )
+
+
+def start_pieces(copy, src, dst, count, *rest):
+    rows = src.shape[0] // count
+    for i in range(count):
+        part = pl.ds(i * rows, rows)
+        copy(src.at[part], dst.at[part], *rest).start()
+
+
+class Copy:
+    def __init__(self, src, dst, count, *rest):
+        self.src, self.dst, self.count, self.rest = src, dst, count, rest
+
+    def start(self):
+        start_pieces(remote, self.src, self.dst, self.count, *self.rest)
+
+    def wait_send(self):
+        remote(self.src, self.dst, *self.rest).wait_send()
+
+    def wait_recv(self):
+        remote(self.src, self.dst, *self.rest).wait_recv()
+
+
+def piece_count(shape, size):
+    count = max(1, shape[0] * shape[1] * 2 // size)
+    while shape[0] % (16 * count):
+        count -= 1
+    return count
 
 
 class Place:
@@ -79,12 +109,12 @@
 
 
 class Relay:
-    def __init__(self, at, buf, send, recv):
-        self.at, self.buf, self.send, self.recv = at, buf, send, recv
+    def __init__(self, at, buf, send, recv, count=1):
+        self.at, self.buf, self.send, self.recv, self.count = at, buf, send, recv, count
 
     def copy(self, s, way, device):
-        return remote(
-            self.buf.at[s], self.buf.at[s], self.send.at[way, s], self.recv.at[s], device
+        return Copy(
+            self.buf.at[s], self.buf.at[s], self.count, self.send.at[way, s], self.recv.at[s], device
         )
 
     def right(self, s):
@@ -148,6 +178,47 @@
             self.hop(i)
         for z in range(self.at.nz):
             self.take_sibling(z)
+
+
+class Deal:
+    def __init__(self, at, chunk, arrived, sems, local_sems):
+        self.at, self.chunk, self.arrived = at, chunk, arrived
+        self.sems, self.local_sems = sems, local_sems
+
+    def ends(self, j, k):
+        at = self.at
+        p = at.blk_peer(k)
+        return (
+            self.chunk(j, p),
+            self.arrived[j].at[at.b],
+            self.sems.at[0, j, k],
+            self.sems.at[1, j, k],
+            at.in_blk(p),
+        )
+
+    def own(self, j):
+        at = self.at
+        return pltpu.make_async_copy(
+            self.chunk(j, at.b), self.arrived[j].at[at.b], self.local_sems.at[j]
+        )
+
+    def start(self, first, last):
+        for i in range(first, last):
+            remote(*self.ends(i % 3, 1 + i // 3)).start()
+        if first == 0 < last:
+            for j in range(3):
+                self.own(j).start()
+
+    def end(self):
+        for j in range(3):
+            for k in range(1, self.at.nb):
+                move = remote(*self.ends(j, k))
+                move.wait_recv()
+                move.wait_send()
+            self.own(j).wait()
+
+    def share(self, part):
+        return int(3 * (self.at.nb - 1) * part)
 
 
 def sorted_place(at, half, shape, axis):
@@ -219,6 +290,9 @@
     grad_out,
     table,
     router_t,
+    w_gate,
+    w_up,
+    w_down,
     xg,
     wg,
     qt,
@@ -233,6 +307,9 @@
     in_gate,
     in_rows,
     in_g,
+    gate_in,
+    up_in,
+    down_in,
     ao,
     perm,
     top,
@@ -262,6 +339,8 @@
     g_sems,
     gate_sems,
     local_sems,
+    deal_sems,
+    deal_local,
 ):
     at = Place(nb, nh)
     rows = inputs.shape[0]
@@ -287,16 +366,27 @@
     weights.begin()
     slot_relay = Relay(at, slot_all, s_send, s_recv)
     slot_relay.begin()
-    g_relay = Relay(at, g_all, g_send, g_recv)
+    g_relay = Relay(at, g_all, g_send, g_recv, 4)
     g_relay.begin()
     pair = 2 * rows
     own_expert = (at.b // repeat) * nh
 
-    def go(buf_out, buf_in, sems, z, k):
+    def chunk(j, p):
+        w_j = (w_gate, w_up, w_down)[j]
+        if repeat == 1:
+            return w_j.at[p]
+        fr = w_gate.shape[2] // repeat
+        part = pl.ds(pl.multiple_of(lax.rem(p, repeat) * fr, fr), fr)
+        return w_j.at[p // repeat, part] if j == 2 else w_j.at[p // repeat, :, part]
+
+    deal = Deal(at, chunk, (gate_in, up_in, down_in), deal_sems, deal_local)
+
+    def go(buf_out, buf_in, sems, z, k, count=1):
         peer = at.head_peer(k)
-        return remote(
+        return Copy(
             buf_out.at[z, peer],
             buf_in.at[z, at.h],
+            count,
             sems.at[0, z, k],
             sems.at[1, z, k],
             at.in_head(peer),
@@ -329,7 +419,7 @@
             if k == 0:
                 keep(out_g, in_g, 0, z).start()
             else:
-                go(out_g, in_g, g_sems, z, k).start()
+                go(out_g, in_g, g_sems, z, k, 5).start()
 
     def send_rows(z):
         x = n2_all[pl.ds(2 * z, 2)].reshape(pair, MODEL_WIDTH)
@@ -363,6 +453,7 @@
     for z in range(nb // 2):
         slots[z] = jnp.concatenate([slot_all[2 * z], slot_all[2 * z + 1]], axis=1)
     outward(g_relay, send_g, 0, 1)
+    deal.start(0, deal.share(FRONT_DEAL[0]))
     for z in range(nb // 2):
         weights.take_sibling(z)
     for c in x_copies:
@@ -456,6 +547,7 @@
         return 0
 
     lax.fori_loop(0, 4 * (nb // 2), visit, 0)
+    deal.start(deal.share(FRONT_DEAL[0]), deal.share(FRONT_DEAL[1]))
     for second in range(2):
         sums = total[second]
         for a in range(hl):
@@ -495,6 +587,7 @@
     n_relay = Relay(at, n2_all, n_send, n_recv)
     n_relay.begin()
     outward(n_relay, send_rows, 0, at.nz)
+    deal.start(deal.share(FRONT_DEAL[1]), deal.share(1))
     own_gates[...] = jnp.where(at.core == 0, gates[at.z, :, :rows], gates[at.z, :, rows:])
     for relay in (weights, slot_relay, g_relay, n_relay):
         relay.finish()
@@ -539,10 +632,13 @@
         return 0
 
     lax.fori_loop(0, at.nz, end, 0)
+    deal.end()
 
 
 def front(nb, nh, hl, kl, repeat, *operands):
     inputs, w_own = operands[0], operands[3]
+    hidden_units = operands[12].shape[2]
+    fr = hidden_units // repeat
     rows = inputs.shape[0]
     group, half = rows * nh, rows * nh // 2
     nz = nb // 2
@@ -570,9 +666,12 @@
             shape(line, F32),
             shape(chunk, BF),
             shape(chunk, BF),
+            shape((nb, dl, fr), BF),
+            shape((nb, dl, fr), BF),
+            shape((nb, fr, dl), BF),
         ),
-        in_specs=[VMEM] * 12,
-        out_specs=[VMEM] * 12 + [ANY] * 2,
+        in_specs=[VMEM] * 12 + [ANY] * 3,
+        out_specs=[VMEM] * 12 + [ANY] * 5,
         scratch_shapes=[
             pltpu.VMEM((group, qw), BF),
             pltpu.VMEM((group, group), BF),
@@ -600,6 +699,8 @@
             dma((2, nz, nh)),
             dma((2, nz, nh)),
             dma((2, nz)),
+            dma((2, 3, nb)),
+            dma((3,)),
         ],
         compiler_params=pltpu.CompilerParams(collective_id=1, vmem_limit_bytes=60 * 2**20),
         name="front",
@@ -643,69 +744,103 @@
     return jnp.where(order < (1 << 20), before, -1)
 
 
-def experts_kernel(nz, nh, x_ref, g_ref, gate_ref, w, d_rows, scaled, d_gate_row, grads, sums):
+def experts_kernel(
+    nz,
+    nh,
+    x_ref,
+    g_ref,
+    gate_ref,
+    w_gate_ref,
+    w_up_ref,
+    w_down_ref,
+    d_rows,
+    scaled,
+    d_gate_row,
+    grad_gate,
+    grad_up,
+    grad_down,
+    w_down,
+    sum_gate,
+    sum_up,
+    sum_down,
+):
     step = pl.program_id(0)
-    fr = w.shape[-1]
-    nb, dl = grads.shape[0], grads.shape[2]
+    nb, dl, fr = w_gate_ref.shape
 
     @pl.when(step == 0)
     def _():
-        sums[...] = jnp.zeros(sums.shape, F32)
+        w_down[...] = jnp.concatenate([w_down_ref[p] for p in range(nb)], axis=1)
+        for total in (sum_gate, sum_up, sum_down):
+            total[...] = jnp.zeros(total.shape, F32)
 
     x = x_ref[0].reshape(nh * 2 * CAP, MODEL_WIDTH)
     gate = jnp.concatenate([to_column(gate_ref[0, h]) for h in range(nh)], axis=0)
-    w_gate = w[:, 0].reshape(MODEL_WIDTH, fr)
-    w_up = w[:, 1].reshape(MODEL_WIDTH, fr)
-    w_down_t = w[:, 2].reshape(MODEL_WIDTH, fr)
+    w_gate = w_gate_ref[...].reshape(MODEL_WIDTH, fr)
+    w_up = w_up_ref[...].reshape(MODEL_WIDTH, fr)
     gate_pre, up_pre = nn(x, w_gate), nn(x, w_up)
     sigma = 1.0 / (1.0 + jnp.exp(-gate_pre))
     swish = gate_pre * sigma
     activated = (swish * up_pre).astype(BF)
-    out = nt(activated, w_down_t).astype(BF).astype(F32)
+    out = nn(activated, w_down[...]).astype(BF).astype(F32)
     g = g_ref[0].reshape(nh * 2 * CAP, MODEL_WIDTH).astype(F32)
     d_gate = jnp.sum(out * g, axis=1, keepdims=True)
     d_out = (gate * g).astype(BF)
     scaled[0] = (gate * out).astype(BF).reshape(nh, 2 * CAP, MODEL_WIDTH)
-    d_act = nn(d_out, w_down_t)
+    d_act = nt(d_out, w_down[...])
     d_gate_pre = (d_act * up_pre * sigma * (1.0 + gate_pre * (1.0 - sigma))).astype(BF)
     d_up_pre = (d_act * swish).astype(BF)
     back_rows = (nt(d_gate_pre, w_gate) + nt(d_up_pre, w_up)).astype(BF)
     d_rows[0] = back_rows.reshape(nh, 2 * CAP, MODEL_WIDTH)
     for h in range(nh):
         d_gate_row[0, h] = to_row(d_gate[h * 2 * CAP : (h + 1) * 2 * CAP])
-    sums[0] += tn(x, d_gate_pre)
-    sums[1] += tn(x, d_up_pre)
-    sums[2] += tn(d_out, activated)
+    sum_gate[...] += tn(x, d_gate_pre)
+    sum_up[...] += tn(x, d_up_pre)
+    sum_down[...] += tn(activated, d_out)
 
     @pl.when(step == nz - 1)
     def _():
-        for j in range(3):
-            for p in range(nb):
-                grads[p, j] = sums[j, p * dl : (p + 1) * dl].astype(BF)
-
-
-def experts(nz, nh, x, g, gate, w):
-    fr = w.shape[-1]
+        for p in range(nb):
+            own = slice(p * dl, (p + 1) * dl)
+            grad_gate[p] = sum_gate[own].astype(BF)
+            grad_up[p] = sum_up[own].astype(BF)
+            grad_down[p] = sum_down[:, own].astype(BF)
+
+
+def experts(nz, nh, x, g, gate, w_gate, w_up, w_down):
+    nb, dl, fr = w_gate.shape
     shape = jax.ShapeDtypeStruct
     wide = pl.BlockSpec((1,) + x.shape[1:], lambda i: (i, 0, 0, 0))
     line = pl.BlockSpec((1,) + gate.shape[1:], lambda i: (i, 0, 0, 0))
-    whole = pl.BlockSpec(w.shape, lambda i: (0, 0, 0, 0))
+    deep = pl.BlockSpec(w_gate.shape, lambda i: (0, 0, 0))
+    flat = pl.BlockSpec(w_down.shape, lambda i: (0, 0, 0))
     return pl.pallas_call(
         functools.partial(experts_kernel, nz, nh),
         grid=(nz,),
-        out_shape=(shape(x.shape, BF), shape(x.shape, BF), shape(gate.shape, F32), shape(w.shape, BF)),
-        in_specs=[wide, wide, line, whole],
-        out_specs=[wide, wide, line, whole],
-        scratch_shapes=[pltpu.VMEM((3, MODEL_WIDTH, fr), F32)],
+        out_shape=(
+            shape(x.shape, BF),
+            shape(x.shape, BF),
+            shape(gate.shape, F32),
+            shape(w_gate.shape, BF),
+            shape(w_up.shape, BF),
+            shape(w_down.shape, BF),
+        ),
+        in_specs=[wide, wide, line, deep, deep, flat],
+        out_specs=[wide, wide, line, deep, deep, flat],
+        scratch_shapes=[
+            pltpu.VMEM((fr, MODEL_WIDTH), BF),
+            pltpu.VMEM((MODEL_WIDTH, fr), F32),
+            pltpu.VMEM((MODEL_WIDTH, fr), F32),
+            pltpu.VMEM((fr, MODEL_WIDTH), F32),
+        ],
         compiler_params=pltpu.CompilerParams(vmem_limit_bytes=60 * 2**20),
         name="experts",
-    )(x, g, gate, w)
+    )(x, g, gate, w_gate, w_up, w_down)
 
 
 class Scatter:
-    def __init__(self, at, sib_out, sib_in, z_out, z_in, sems):
-        self.at, self.sib_out, self.sib_in, self.z_out, self.z_in = at, sib_out, sib_in, z_out, z_in
-        self.sems = sems
+    def __init__(self, at, bufs, sems):
+        self.at, self.sems = at, sems
+        self.sib_out, self.sib_in, self.z_out, self.z_in = (bufs.at[j] for j in range(4))
 
     def across(self, z):
         return remote(
@@ -717,13 +852,27 @@
         )
 
     def along(self, z):
+        at = self.at
+        slot = jnp.where(z == at.z - 1, at.nz, z)
+        ahead = jnp.clip(jnp.where(z > at.z, at.z + 1, at.z - 1), 0, at.nz - 1)
         return remote(
             self.z_out.at[z],
-            self.z_in.at[self.at.z],
+            self.z_in.at[slot],
             self.sems.at[2, z],
-            self.sems.at[3, self.at.z],
-            self.at.in_blk(2 * z + self.at.core),
-        )
+            self.sems.at[3, slot],
+            at.in_blk(2 * ahead + at.core),
+        )
+
+    def arrived(self, slot):
+        at = self.at
+        remote(
+            self.z_out.at[0],
+            self.z_in.at[slot],
+            self.sems.at[2, 0],
+            self.sems.at[3, slot],
+            at.in_blk(at.sibling),
+        ).wait_recv()
+        return self.z_in[slot].astype(F32)
 
     def give_sibling(self, z, value):
         self.sib_out[z] = value.astype(BF)
@@ -734,18 +883,23 @@
         return self.sib_in[z].astype(F32)
 
     def give(self, z, value):
-        self.z_out[z] = value.astype(BF)
+        at = self.at
+        joins = ((z > at.z) & (at.z > 0)) | ((z < at.z) & (at.z < at.nz - 1))
+
+        @pl.when(joins)
+        def _():
+            self.z_out[z] = (value + self.arrived(z)).astype(BF)
+
+        @pl.when(jnp.logical_not(joins))
+        def _():
+            self.z_out[z] = value.astype(BF)
+
         self.along(z).start()
 
-    def taken(self, z):
-        remote(
-            self.z_out.at[z],
-            self.z_in.at[z],
-            self.sems.at[2, z],
-            self.sems.at[3, z],
-            self.at.in_blk(2 * z + self.at.core),
-        ).wait_recv()
-        return self.z_in[z].astype(F32)
+    def take(self, add):
+        at = self.at
+        pl.when(at.z > 0)(lambda: add(self.arrived(at.z), True))
+        pl.when(at.z < at.nz - 1)(lambda: add(self.arrived(at.nz), False))
 
     def finish(self):
         at = self.at
@@ -832,11 +986,17 @@
     begin,
     d_rows,
     scaled,
+    gate_sum,
+    up_sum,
+    down_sum,
     output,
     grad_in,
     grad_w,
     grad_n1,
     small_sum,
+    gate_in,
+    up_in,
+    down_in,
     dbg,
     perm,
     d_rows_ref,
@@ -874,6 +1034,8 @@
     dgate_sems,
     dg_sems,
     local_sems,
+    deal_sems,
+    deal_local,
 ):
     at = Place(nb, nh)
     nz = at.nz
@@ -889,11 +1051,12 @@
     own_expert = (at.b // repeat) * nh
     at.meet()
 
-    def go(buf_out, buf_in, sems, z, k):
+    def go(buf_out, buf_in, sems, z, k, count=1):
         peer = at.head_peer(k)
-        return remote(
+        return Copy(
             buf_out.at[z, peer],
             buf_in.at[z, at.h],
+            count,
             sems.at[0, z, k],
             sems.at[1, z, k],
             at.in_head(peer),
@@ -904,10 +1067,16 @@
 
     def far_first(body):
         def step(t, unused):
-            body(lax.rem(at.z + 1 + t, nz))
+            d, side = nz - 1 - t // 2, lax.rem(t, 2)
+            z = jnp.where(side == 0, at.z - d, at.z + d)
+
+            @pl.when((z >= 0) & (z < nz) & ((d > 0) | (side == 0)))
+            def _():
+                body(z)
+
             return 0
 
-        lax.fori_loop(0, nz, step, 0)
+        lax.fori_loop(0, 2 * nz, step, 0)
 
     def send_back(z):
         for k in range(1, nh):
@@ -917,7 +1086,9 @@
         in_dgate[z, at.h] = d_gate_rows[z, at.h]
 
     far_first(send_back)
-    n2_scatter = Scatter(at, *(sc_bufs.at[j] for j in range(4)), sc_sems)
+    sums_of = (gate_sum, up_sum, down_sum)
+    deal = Deal(at, lambda j, p: sums_of[j].at[p], (gate_in, up_in, down_in), deal_sems, deal_local)
+    n2_scatter = Scatter(at, sc_bufs, sc_sems)
 
     def dg_copy(p):
         return remote(
@@ -942,12 +1113,11 @@
 
     def gathered_part(scatter):
         own_part[2] = own_part[at.core] + scatter.from_sibling(at.z)
-        for z in range(nz):
-
-            @pl.when(at.z != z)
-            def _():
-                own_part[2] += scatter.taken(z)
-
+
+        def add(value, from_left):
+            own_part[2] += value
+
+        scatter.take(add)
         return own_part[2]
 
     def gather_back(z):
@@ -974,6 +1144,7 @@
 
         spread(z, masks, n2_scatter)
 
+    deal.start(0, deal.share(BACK_DEAL[0]))
     far_first(gather_back)
     dg_in[at.b] = dg_out[at.b]
     for k in range(1, nb):
@@ -1019,12 +1190,13 @@
 
     def send_scaled(z):
         for k in range(1, nh):
-            go(scaled, back_rows, eout_sems, z, k).start()
+            go(scaled, back_rows, eout_sems, z, k, 5).start()
         keep(scaled, 1, z).start()
 
     far_first(send_scaled)
     totals.end(0)
     totals.begin(1)
+    deal.start(deal.share(BACK_DEAL[0]), deal.share(BACK_DEAL[1]))
     d_branch = dbg[...].reshape(group, MODEL_WIDTH)
     w = wg[...].reshape(MODEL_WIDTH, width + qw)
     d_attn_t = nn(d_branch, w[:, width:]).T.astype(BF)
@@ -1068,7 +1240,7 @@
             dq_t[second, rows_a] += tn(key, d_scores)
         return jnp.concatenate(d_keys + d_values, axis=0)
 
-    scatter = Scatter(at, *(kv_bufs.at[j] for j in range(4)), kv_sems)
+    scatter = Scatter(at, kv_bufs, kv_sems)
 
     def visit(step, unused):
         i = nz - 1 - step // 4
@@ -1112,11 +1284,12 @@
 
     weight_part(width, ao_t[...])
     own_kv[at.core] += scatter.from_sibling(at.z)
-    for z in range(nz):
-
-        @pl.when(at.z != z)
-        def _():
-            own_kv[jnp.where(at.z < z, 0, 1)] += scatter.taken(z)
+
+    def add_kv(value, from_left):
+        own_kv[1 if from_left else 0] += value
+
+    scatter.take(add_kv)
+    deal.start(deal.share(BACK_DEAL[1]), deal.share(BACK_DEAL[2]))
 
     d_sorted_t = []
     for second in range(2):
@@ -1142,23 +1315,20 @@
         o_copies.append(c)
     own_normed = nt(d_rows_ref[at.h], w[:, :width])
     weight_part(0, d_cols)
-    w_scatter = Scatter(at, *(w_bufs.at[j] for j in range(4)), w_sems)
-
-    def w_sib(step, unused):
-        z = lax.rem(at.z + 1 + step, nz)
+    w_scatter = Scatter(at, w_bufs, w_sems)
+
+    def w_pass(z):
         w_scatter.give_sibling(z, w_part[2 * z + 1 - at.core])
-        return 0
-
-    lax.fori_loop(0, nz, w_sib, 0)
-
-    def w_along(step, unused):
-        z = lax.rem(at.z + 1 + step, nz)
-        w_scatter.give(z, w_part[2 * z + at.core] + w_scatter.from_sibling(z))
-        return 0
-
-    lax.fori_loop(0, nz - 1, w_along, 0)
+
+    def w_along(z):
+        pl.when(z != at.z)(
+            lambda: w_scatter.give(z, w_part[2 * z + at.core] + w_scatter.from_sibling(z))
+        )
+
+    far_first(w_pass)
+    far_first(w_along)
     n2_scatter.finish()
-    mix_scatter = Scatter(at, *(sc_bufs.at[j] for j in range(4)), mix_sems)
+    mix_scatter = Scatter(at, sc_bufs, mix_sems)
 
     def mix(z):
         for k in range(1, nh):
@@ -1167,6 +1337,7 @@
         spread(z, masks_of(z), mix_scatter)
 
     far_first(mix)
+    deal.start(deal.share(BACK_DEAL[2]), deal.share(1))
     for k in range(1, nh):
         o_copies[k - 1].wait_recv()
         own_normed = own_normed + out_recv[lax.rem(at.h + nh - k, nh)].astype(F32)
@@ -1193,13 +1364,12 @@
     ]
     for c in n1_blk_copies:
         c.start()
-    total_w = w_part[at.b] + w_scatter.from_sibling(at.z)
-    grad_w[...] = total_w
-    for z in range(nz):
-
-        @pl.when(at.z != z)
-        def _():
-            grad_w[...] += w_scatter.taken(z)
+    grad_w[...] = w_part[at.b] + w_scatter.from_sibling(at.z)
+
+    def add_w(value, from_left):
+        grad_w[...] += value
+
+    w_scatter.take(add_w)
 
     for c in n1_blk_copies:
         c.wait_recv()
@@ -1217,6 +1387,7 @@
             go(scaled, back_rows, eout_sems, z, k).wait_send()
 
     far_first(drain)
+    deal.end()
     for k in range(1, nb):
         dg_copy(at.blk_peer(k)).wait_send()
     w_scatter.finish()
@@ -1242,9 +1413,10 @@
             shape((width + qw, dl), F32),
             shape((1, MODEL_WIDTH), F32),
             shape((nh,) + chunk, F32),
+            *(shape(v.shape, BF) for v in operands[-3:]),
         ),
-        in_specs=[VMEM] * 22 + [ANY] * 2,
-        out_specs=[VMEM] * 5,
+        in_specs=[VMEM] * 22 + [ANY] * 5,
+        out_specs=[VMEM] * 5 + [ANY] * 3,
         scratch_shapes=[
             pltpu.VMEM((nh, rows, MODEL_WIDTH), BF),
             pltpu.VMEM((group, group), BF),
@@ -1253,9 +1425,9 @@
             pltpu.VMEM((2, max(hl, 8), half), F32),
             pltpu.VMEM((2, qw, half), F32),
             pltpu.VMEM((2, 2 * kw, half), F32),
-            pltpu.VMEM((4, nz, 2 * kw, half), BF),
+            pltpu.VMEM((4, nz + 1, 2 * kw, half), BF),
             pltpu.VMEM((nb, width + qw, dl), F32),
-            pltpu.VMEM((4, nz, width + qw, dl), BF),
+            pltpu.VMEM((4, nz + 1, width + qw, dl), BF),
             pltpu.VMEM((nh, rows, MODEL_WIDTH), BF),
             pltpu.VMEM((nh, rows, MODEL_WIDTH), BF),
             pltpu.VMEM((nh, 1, MODEL_WIDTH), F32),
@@ -1263,8 +1435,8 @@
             pltpu.VMEM((nh,) + chunk, F32),
             pltpu.VMEM((nb,) + chunk, F32),
             dma((2, nh)),
-            dma((4, nz)),
-            dma((4, nz)),
+            dma((4, nz + 1)),
+            dma((4, nz + 1)),
             dma((2, nh)),
             dma((2, nh + nb)),
             dma((2, 3, max(nh, nb))),
@@ -1275,16 +1447,18 @@
             pltpu.VMEM((rows, MODEL_WIDTH), F32),
             pltpu.VMEM((nb, nh, rows), F32),
             pltpu.VMEM((nb, nh, rows), F32),
-            pltpu.VMEM((4, nz, rows, MODEL_WIDTH), BF),
-            dma((4, nz)),
-            dma((4, nz)),
+            pltpu.VMEM((4, nz + 1, rows, MODEL_WIDTH), BF),
+            dma((4, nz + 1)),
+            dma((4, nz + 1)),
             dma((2, nz, nh)),
             dma((2, nz, nh)),
             dma((2, nz, nh)),
             dma((2, nb)),
             dma((2, nz)),
+            dma((2, 3, nb)),
+            dma((3,)),
         ],
-        compiler_params=pltpu.CompilerParams(collective_id=2, vmem_limit_bytes=60 * 2**20),
+        compiler_params=pltpu.CompilerParams(collective_id=2, vmem_limit_bytes=62 * 2**20),
         name="back",
     )(*operands)
 
@@ -1317,14 +1491,6 @@
     fr = hidden_units // repeat
     qw, kw = hl * HEAD_SIZE, kl * HEAD_SIZE
 
-    def by_part(v):
-        v = v.reshape(local, dl, repeat, fr).transpose(0, 2, 1, 3)
-        return v.reshape(nb, dl, fr)
-
-    projections = jnp.stack(
-        [by_part(w_gate), by_part(w_up), by_part(w_down.transpose(0, 2, 1))], axis=1
-    )
-    projections = lax.all_to_all(projections, "blk", split_axis=0, concat_axis=0, tiled=True)
     own, begin_s, cos_o, sin_o, cos_s, sin_s, w_own = head_inputs(
         nb, nh, rows, token_place, lengths, w_query, key_weight, value_weight, w_out
     )
@@ -1347,6 +1513,7 @@
         in_gate,
         in_rows,
         in_g,
+        *projections,
     ) = front(
         *sizes,
         inputs,
@@ -1361,10 +1528,12 @@
         grad_out,
         slot_table(nb, nh, repeat, routes, slot_order),
         router_t,
+        w_gate,
+        w_up,
+        w_down,
     )
-    d_rows, scaled, d_gate_rows, grads = experts(nz, nh, in_rows, in_g, in_gate, projections)
-    grads = lax.all_to_all(grads, "blk", split_axis=0, concat_axis=0, tiled=True)
-    output, grad_inputs, grad_w, grad_norm1, small = back(
+    d_rows, scaled, d_gate_rows, *sums = experts(nz, nh, in_rows, in_g, in_gate, *projections)
+    output, grad_inputs, grad_w, grad_norm1, small, *sums = back(
         *sizes,
         inputs,
         gain_one,
@@ -1390,6 +1559,7 @@
         begin_s,
         d_rows,
         scaled,
+        *sums,
     )
 
     small = small.transpose(1, 0, 2).reshape(E + 8, MODEL_WIDTH)
@@ -1397,9 +1567,10 @@
         small[:E].reshape(local, nh, MODEL_WIDTH).transpose(1, 0, 2).reshape(E, MODEL_WIDTH).T
     )
 
-    def whole_part(v):
-        v = v.reshape(local, repeat, dl, fr).transpose(0, 2, 1, 3)
-        return v.reshape(local, dl, hidden_units).astype(F32)
+    def whole_part(v, axis):
+        v = v.reshape((local, repeat) + v.shape[1:])
+        v = v if repeat == 1 else jnp.moveaxis(v, 1, axis)
+        return v.reshape((local, dl, hidden_units) if axis == 2 else (local, hidden_units, dl)).astype(F32)
 
     return (
         output,
@@ -1411,9 +1582,9 @@
         grad_w[qw + 2 * kw :],
         small[E],
         grad_router,
-        whole_part(grads[:, 0]),
-        whole_part(grads[:, 1]),
-        whole_part(grads[:, 2]).transpose(0, 2, 1),
+        whole_part(sums[0], 2),
+        whole_part(sums[1], 2),
+        whole_part(sums[2], 1),
     )
 
 

time: 405 us -> 361 us (0.89)
  Pallas kernels: 365 us -> 332 us
  starting transfers between devices: 10.3 us -> 0 us
  local copies, waits for them, and re-layouts: 19 us -> 14.4 us
    pallas_call x1, Pallas kernels: 167 us -> 139 us  [front(): pl.pallas_call(functools.partial(front_kernel, nb, nh, hl, kl, repeat), o...]
    all_to_all x2 -> x0, starting transfers between devices: 10.3 us -> none  [the longest x1 6.47 us: on_device(): lax.all_to_all(projections, 'blk', split_axis=0, concat_axis=0, tiled=True)]
    unnamed x41 -> x23, local copies, waits for them, and re-layouts: 10.9 us -> 5.27 us
    convert_element_type x0 -> x3, other arithmetic: none -> 4.67 us  [whole_part(): v.reshape((local, dl, hidden_units) if axis == 2 else (local, hidden_unit...]
    pallas_call x1, Pallas kernels: 175 us -> 171 us  [back(): pl.pallas_call(functools.partial(back_kernel, nb, nh, hl, kl, repeat), ou...]
  transfers between devices with their start and end apart: 2 -> 0, of which waited for: 0 -> 0; matrix products, arithmetic and copies ran while one was open for 4% -> 0% of each run, Pallas kernels for 85% -> 0%
where the time goes in v4:
time: 361 us
  Pallas kernels  332 us (92%)
  local copies, waits for them, and re-layouts  14.4 us (4%)
  other arithmetic  13.2 us (4%)
    pallas_call x1, Pallas kernels, back(): pl.pallas_call(functools.partial(back_kernel, nb, nh, hl, kl, repeat), ou...  171 us
    pallas_call x1, Pallas kernels, front(): pl.pallas_call(functools.partial(front_kernel, nb, nh, hl, kl, repeat), o...  139 us
    pallas_call x1, Pallas kernels, experts(): pl.pallas_call(functools.partial(experts_kernel, nz, nh), grid=(nz,), out...  22.7 us

profile of v4, /device:TPU:0, one launch (start us, length us, event | category | flops | bytes accessed | tf_op | source)
XLA Modules:
  0.0 360.7 jit_solution(9878371304276016792)
XLA Ops:
  0.6 0.8 reduce-window.9
  2.2 0.8 dynamic_slice.3
  3.0 0.7 select_reduce_fusion.1
  3.7 0.8 subtract_convert_fusion
  7.3 0.9 copy.50
  8.2 0.9 copy.62
  9.7 1.6 pad_maximum_fusion.w_own
  11.3 1.2 multiply_sine_fusion
  12.5 0.9 copy.52.place_col
  13.4 139.0 %front.1 = (bf16[4,128,1024]{2,1,0:T(8,128)(2,1)}, bf16[8,128,768]{2,1,0:T(8,128)(2,1)}, bf16[2,256,256]{2,1,0:T(8,128)(2,1)}, bf16[8,2,256,256]{3,2,1,0:T(8,128...) custom-call(bf16[128,1024]{1,0:T(8,128)(2,1)} %inputs.3, ...), custom_call_target="tpu_custom_call" | custom-call | tf_op jit(solution)/shard_map/front/pallas_call | solution.py:652
  152.4 22.7 %experts.1 = (bf16[4,4,80,1024]{3,2,1,0:T(8,128)(2,1)}, bf16[4,4,80,1024]{3,2,1,0:T(8,128)(2,1)}, f32[4,4,1,80]{3,2,1,0:T(1,128)}, bf16[8,128,512]{2,1,0:T(8,128...) custom-call(bf16[4,4,80,1024]{3,2,1,0:T(8,128)(2,1)} %get-tuple-element.47.x_ref, ...), custom_call_target="tpu_custom_call" | custom-call | tf_op jit(solution)/shard_map/experts/pallas_call | solution.py:816
  175.1 170.7 %back.1 = (bf16[128,1024]{1,0:T(8,128)(2,1)}, f32[128,1024]{1,0:T(8,128)}, f32[768,128]{1,0:T(8,128)}, f32[1,1024]{1,0:T(1,128)}, f32[4,40,256]{2,1,0:T(8,128)},...) custom-call(bf16[128,1024]{1,0:T(8,128)(2,1)} %inputs.3, ...), custom_call_target="tpu_custom_call" | custom-call | tf_op jit(solution)/shard_map/back/pallas_call | solution.py:1408
  345.8 1.4 slice.36
  347.2 0.9 slice.37
  348.3 0.7 copy.61
  349.1 0.9 slice_bitcast_fusion.1
  350.0 1.7 fusion.7
  351.7 0.7 copy.58
  352.4 0.7 copy.57
  353.2 0.8 copy.56
  353.9 1.6 convert_element_type.25
  355.5 1.6 convert_element_type.26
  357.1 1.5 convert_element_type.27
  359.3 0.8 copy.67
  (29 shorter events, 5.6 us)
Async XLA Ops:
  3.0 10.4 %copy-start.5 = (s32[512]{0:T(512)}, s32[512]{0:T(512)S(1)}, u32[]{:S(2)}) copy-start(s32[512]{0:T(512)S(1)} %dynamic_slice.3) | copy-start | bytes 6148
  3.7 9.6 %copy-start.6 = (s32[512]{0:T(512)}, s32[512]{0:T(512)S(1)}, u32[]{:S(2)}) copy-start(s32[512]{0:T(512)S(1)} %get-tuple-element.122) | copy-start | bytes 6148
  345.8 8.1 %copy-start.2 = (bf16[8,128,512]{2,1,0:T(8,128)(2,1)S(1)}, bf16[8,128,512]{2,1,0:T(8,128)(2,1)}, u32[]{:S(2)}) copy-start(bf16[8,128,512]{2,1,0:T(8,128)(2,1)} %get-tuple-element.71) | copy-start | bytes 3145732
  350.0 5.6 %copy-start.1 = (bf16[8,128,512]{2,1,0:T(8,128)(2,1)S(1)}, bf16[8,128,512]{2,1,0:T(8,128)(2,1)}, u32[]{:S(2)}) copy-start(bf16[8,128,512]{2,1,0:T(8,128)(2,1)} %get-tuple-element.72) | copy-start | bytes 3145732
  355.5 1.6 copy-start
  357.1 1.5 copy-start.4
  357.1 2.2 copy-start.3
  357.1 3.0 copy-start.7

commit v5 on v4

--- a/solution.py
+++ b/solution.py
@@ -16,10 +16,11 @@
 MESH = pl.DeviceIdType.MESH
 VMEM = pl.BlockSpec(memory_space=pltpu.VMEM)
 ANY = pl.BlockSpec(memory_space=pl.ANY)
+SMEM = pl.BlockSpec(memory_space=pltpu.SMEM)
 BF = jnp.bfloat16
 F32 = jnp.float32
-FRONT_DEAL = (0.1, 0.6)
-BACK_DEAL = (0.1, 0.4, 0.55)
+FRONT_DEAL = (0.25, 0.8)
+BACK_DEAL = (0.25, 0.42, 0.6)
 
 eps = 1e-06
 rope_base = 10000.0
@@ -203,11 +204,17 @@
         )
 
     def start(self, first, last):
-        for i in range(first, last):
-            remote(*self.ends(i % 3, 1 + i // 3)).start()
-        if first == 0 < last:
+        nb = self.at.nb
+        if first == 0:
             for j in range(3):
                 self.own(j).start()
+        rest = [(0, k) for k in range(nb // 2 + 1, nb)]
+        rest += [(j, k) for k in range(1, nb) for j in (1, 2)]
+        for j, k in rest[int(len(rest) * first) : int(len(rest) * last)]:
+            remote(*self.ends(j, k)).start()
+
+    def one(self, z):
+        remote(*self.ends(0, 1 + z)).start()
 
     def end(self):
         for j in range(3):
@@ -217,15 +224,33 @@
                 move.wait_send()
             self.own(j).wait()
 
-    def share(self, part):
-        return int(3 * (self.at.nb - 1) * part)
-
 
 def sorted_place(at, half, shape, axis):
     s = lax.broadcasted_iota(jnp.int32, shape, axis)
     return jnp.where(
         s < half, at.b * half + s, (2 * at.nb - 1 - at.b) * half + s - half
     )
+
+
+def begin_of(place, lengths):
+    start, begin = 0, jnp.zeros_like(place)
+    for i in range(lengths.shape[0] - 1):
+        start = start + lengths[i]
+        begin = begin + jnp.where(place >= start, lengths[i], 0)
+    return begin
+
+
+def rotation(place, begin):
+    shape = (HEAD_SIZE // 2, place.shape[1])
+    index = lax.broadcasted_iota(jnp.int32, shape, 0).astype(F32)
+    freq = jnp.exp(index * (-2.0 * math.log(rope_base) / HEAD_SIZE))
+    angle = freq * (place - begin).astype(F32)
+    return jnp.cos(angle), jnp.sin(angle)
+
+
+def column_of(row):
+    wide = jnp.broadcast_to(row.astype(F32), (128, row.shape[1]))
+    return wide.T[:, :1].astype(jnp.int32)
 
 
 def block_base(at, b, second, half):
@@ -282,11 +307,8 @@
     w_norm1,
     w_norm2,
     w_own,
-    place_row,
-    place_col,
-    cos,
-    sin,
-    begin,
+    places,
+    lengths,
     grad_out,
     table,
     router_t,
@@ -341,6 +363,7 @@
     local_sems,
     deal_sems,
     deal_local,
+    begin,
 ):
     at = Place(nb, nh)
     rows = inputs.shape[0]
@@ -442,8 +465,14 @@
                 out_gate[z, peer] = gate
                 go(out_gate, in_gate, gate_sems, z, k).start()
 
+    place_row = places[at.b]
+    cos, sin = rotation(place_row, begin_of(place_row, lengths))
+    in_order = begin_of(sorted_place(at, half, (1, group), 1), lengths)
+    begin[0] = in_order[:, :half]
+    begin[1] = in_order[:, half:]
+    place_col = column_of(place_row)
     perm[...] = jnp.where(
-        place_row[...] == sorted_place(at, half, (group, group), 0), 1.0, 0.0
+        place_row == sorted_place(at, half, (group, group), 0), 1.0, 0.0
     ).astype(BF)
     for i in range(1, nb // 2):
         slot_relay.hop(i)
@@ -453,7 +482,7 @@
     for z in range(nb // 2):
         slots[z] = jnp.concatenate([slot_all[2 * z], slot_all[2 * z + 1]], axis=1)
     outward(g_relay, send_g, 0, 1)
-    deal.start(0, deal.share(FRONT_DEAL[0]))
+    deal.start(0, FRONT_DEAL[0])
     for z in range(nb // 2):
         weights.take_sibling(z)
     for c in x_copies:
@@ -462,7 +491,7 @@
     w = wg[...].reshape(MODEL_WIDTH, width + qw)
     qkv_t = nn(x, w[:, :width]).T
     qkv_t = jnp.concatenate(
-        [turn_rows(qkv_t[: qw + kw], cos[...], sin[...]), qkv_t[qw + kw :]], axis=0
+        [turn_rows(qkv_t[: qw + kw], cos, sin), qkv_t[qw + kw :]], axis=0
     ).astype(BF)
     order = perm[...]
     kv_rows = nt(order, qkv_t[qw:]).astype(BF)
@@ -547,14 +576,14 @@
         return 0
 
     lax.fori_loop(0, 4 * (nb // 2), visit, 0)
-    deal.start(deal.share(FRONT_DEAL[0]), deal.share(FRONT_DEAL[1]))
+    deal.start(FRONT_DEAL[0], FRONT_DEAL[1])
     for second in range(2):
         sums = total[second]
         for a in range(hl):
             rows_a = slice(a * HEAD_SIZE, (a + 1) * HEAD_SIZE)
             attn_t[second, rows_a] = attn_t[second, rows_a] / sums[a : a + 1]
     lse[...] = top[...] + jnp.log(total[...])
-    back = jnp.where(place_col[...] == sorted_place(at, half, (group, group), 1), 1.0, 0.0).astype(BF)
+    back = jnp.where(place_col == sorted_place(at, half, (group, group), 1), 1.0, 0.0).astype(BF)
     attn_rows = (
         nt(back[:, :half], attn_t[0].astype(BF)) + nt(back[:, half:], attn_t[1].astype(BF))
     ).astype(BF)
@@ -586,8 +615,13 @@
     n2_all[at.b] = n2[...]
     n_relay = Relay(at, n2_all, n_send, n_recv)
     n_relay.begin()
-    outward(n_relay, send_rows, 0, at.nz)
-    deal.start(deal.share(FRONT_DEAL[1]), deal.share(1))
+
+    def send_both(z):
+        send_rows(z)
+        deal.one(z)
+
+    outward(n_relay, send_both, 0, at.nz)
+    deal.start(FRONT_DEAL[1], 1)
     own_gates[...] = jnp.where(at.core == 0, gates[at.z, :, :rows], gates[at.z, :, rows:])
     for relay in (weights, slot_relay, g_relay, n_relay):
         relay.finish()
@@ -637,7 +671,7 @@
 
 def front(nb, nh, hl, kl, repeat, *operands):
     inputs, w_own = operands[0], operands[3]
-    hidden_units = operands[12].shape[2]
+    hidden_units = operands[9].shape[2]
     fr = hidden_units // repeat
     rows = inputs.shape[0]
     group, half = rows * nh, rows * nh // 2
@@ -670,7 +704,7 @@
             shape((nb, dl, fr), BF),
             shape((nb, fr, dl), BF),
         ),
-        in_specs=[VMEM] * 12 + [ANY] * 3,
+        in_specs=[VMEM] * 5 + [SMEM] + [VMEM] * 3 + [ANY] * 3,
         out_specs=[VMEM] * 12 + [ANY] * 5,
         scratch_shapes=[
             pltpu.VMEM((group, qw), BF),
@@ -701,38 +735,11 @@
             dma((2, nz)),
             dma((2, 3, nb)),
             dma((3,)),
+            pltpu.VMEM((2, 1, half), jnp.int32),
         ],
         compiler_params=pltpu.CompilerParams(collective_id=1, vmem_limit_bytes=60 * 2**20),
         name="front",
     )(*operands)
-
-
-def seq_begin(token_position, lengths):
-    starts = jnp.cumsum(lengths) - lengths
-    inside = token_position[:, None] >= starts[None, 1:]
-    return jnp.sum(jnp.where(inside, lengths[None, :-1], 0), axis=1)
-
-
-def rotation_rows(token_position, begin_index):
-    half = HEAD_SIZE // 2
-    freq = jnp.exp(
-        jnp.arange(half, dtype=F32) * (-2.0 * math.log(rope_base) / HEAD_SIZE)
-    )
-    angle = freq[:, None] * (token_position - begin_index).astype(F32)[None, :]
-    return jnp.cos(angle), jnp.sin(angle)
-
-
-def head_inputs(nb, nh, rows, token_place, lengths, w_query, key_weight, value_weight, w_out):
-    group, half = rows * nh, rows * nh // 2
-    b = lax.axis_index("blk")
-    own = lax.dynamic_slice_in_dim(token_place, b * group, group)
-    s = jnp.arange(group, dtype=jnp.int32)
-    in_order = jnp.where(s < half, b * half + s, (2 * nb - 1 - b) * half + s - half)
-    begin_s = seq_begin(in_order, lengths)
-    cos_o, sin_o = rotation_rows(own, seq_begin(own, lengths))
-    cos_s, sin_s = rotation_rows(in_order, begin_s)
-    w_own = jnp.concatenate([w_query, key_weight, value_weight, w_out.T], axis=1)
-    return own, begin_s.reshape(2, 1, half), cos_o, sin_o, cos_s, sin_s, w_own
 
 
 def slot_table(nb, nh, repeat, routes, slot_order):
@@ -979,11 +986,8 @@
     kv,
     lse,
     attn_t,
-    place_row,
-    place_col,
-    cos,
-    sin,
-    begin,
+    places,
+    lengths,
     d_rows,
     scaled,
     gate_sum,
@@ -1036,6 +1040,8 @@
     local_sems,
     deal_sems,
     deal_local,
+    begin,
+    *loaded,
 ):
     at = Place(nb, nh)
     nz = at.nz
@@ -1086,8 +1092,25 @@
         in_dgate[z, at.h] = d_gate_rows[z, at.h]
 
     far_first(send_back)
+    load_sems = loaded[-1]
+    sources = (wg, xg, ao_t, qt, kv, attn_t)
+    loads = [
+        pltpu.make_async_copy(src, dst, load_sems.at[i])
+        for i, (src, dst) in enumerate(zip(sources, loaded[:-1]))
+    ]
+    for c in loads:
+        c.start()
+    wg, xg, ao_t, qt, kv, attn_t = loaded[:-1]
+    place_row = places[at.b]
+    sorted_row = sorted_place(at, half, (1, group), 1)
+    in_order = begin_of(sorted_row, lengths)
+    begin[0] = in_order[:, :half]
+    begin[1] = in_order[:, half:]
+    cos, sin = rotation(sorted_row, in_order)
+    place_col = column_of(place_row)
     sums_of = (gate_sum, up_sum, down_sum)
     deal = Deal(at, lambda j, p: sums_of[j].at[p], (gate_in, up_in, down_in), deal_sems, deal_local)
+    deal.start(0, BACK_DEAL[0])
     n2_scatter = Scatter(at, sc_bufs, sc_sems)
 
     def dg_copy(p):
@@ -1143,8 +1166,8 @@
             dg_copy(2 * z + 1).start()
 
         spread(z, masks, n2_scatter)
-
-    deal.start(0, deal.share(BACK_DEAL[0]))
+        deal.one(z)
+
     far_first(gather_back)
     dg_in[at.b] = dg_out[at.b]
     for k in range(1, nb):
@@ -1182,7 +1205,7 @@
     totals = Total(at, small, s_head, s_blk, small_sum, s_sems)
     totals.begin(0)
     perm[...] = jnp.where(
-        place_row[...] == sorted_place(at, half, (group, group), 0), 1.0, 0.0
+        place_row == sorted_place(at, half, (group, group), 0), 1.0, 0.0
     ).astype(BF)
     dq_t[...] = jnp.zeros(dq_t.shape, F32)
     for c in d_copies:
@@ -1196,7 +1219,9 @@
     far_first(send_scaled)
     totals.end(0)
     totals.begin(1)
-    deal.start(deal.share(BACK_DEAL[0]), deal.share(BACK_DEAL[1]))
+    deal.start(BACK_DEAL[0], BACK_DEAL[1])
+    for c in loads:
+        c.wait()
     d_branch = dbg[...].reshape(group, MODEL_WIDTH)
     w = wg[...].reshape(MODEL_WIDTH, width + qw)
     d_attn_t = nn(d_branch, w[:, width:]).T.astype(BF)
@@ -1269,6 +1294,7 @@
         return 0
 
     lax.fori_loop(0, 4 * nz, visit, 0)
+    deal.start(BACK_DEAL[1], BACK_DEAL[2])
     totals.end(1)
     totals.begin(2)
     wide = 256
@@ -1289,7 +1315,6 @@
         own_kv[1 if from_left else 0] += value
 
     scatter.take(add_kv)
-    deal.start(deal.share(BACK_DEAL[1]), deal.share(BACK_DEAL[2]))
 
     d_sorted_t = []
     for second in range(2):
@@ -1298,7 +1323,7 @@
         turned = jnp.concatenate([dq_t[second] * scale, both[:kw]], axis=0)
         turned = turn_rows(turned, cos[:, cols], -sin[:, cols])
         d_sorted_t.append(jnp.concatenate([turned, both[kw:]], axis=0).astype(BF))
-    back = jnp.where(place_col[...] == sorted_place(at, half, (group, group), 1), 1.0, 0.0).astype(BF)
+    back = jnp.where(place_col == sorted_place(at, half, (group, group), 1), 1.0, 0.0).astype(BF)
     turned_back = (
         nt(back[:, :half], d_sorted_t[0]) + nt(back[:, half:], d_sorted_t[1])
     ).astype(BF)
@@ -1337,7 +1362,7 @@
         spread(z, masks_of(z), mix_scatter)
 
     far_first(mix)
-    deal.start(deal.share(BACK_DEAL[2]), deal.share(1))
+    deal.start(BACK_DEAL[2], 1)
     for k in range(1, nh):
         o_copies[k - 1].wait_recv()
         own_normed = own_normed + out_recv[lax.rem(at.h + nh - k, nh)].astype(F32)
@@ -1415,7 +1440,7 @@
             shape((nh,) + chunk, F32),
             *(shape(v.shape, BF) for v in operands[-3:]),
         ),
-        in_specs=[VMEM] * 22 + [ANY] * 5,
+        in_specs=[VMEM] * 10 + [ANY] * 4 + [ANY, VMEM, ANY] + [VMEM, SMEM] + [ANY] * 5,
         out_specs=[VMEM] * 5 + [ANY] * 3,
         scratch_shapes=[
             pltpu.VMEM((nh, rows, MODEL_WIDTH), BF),
@@ -1457,6 +1482,9 @@
             dma((2, nz)),
             dma((2, 3, nb)),
             dma((3,)),
+            pltpu.VMEM((2, 1, half), jnp.int32),
+            *(pltpu.VMEM(operands[i].shape, operands[i].dtype) for i in (10, 11, 12, 13, 14, 16)),
+            dma((6,)),
         ],
         compiler_params=pltpu.CompilerParams(collective_id=2, vmem_limit_bytes=62 * 2**20),
         name="back",
@@ -1491,11 +1519,9 @@
     fr = hidden_units // repeat
     qw, kw = hl * HEAD_SIZE, kl * HEAD_SIZE
 
-    own, begin_s, cos_o, sin_o, cos_s, sin_s, w_own = head_inputs(
-        nb, nh, rows, token_place, lengths, w_query, key_weight, value_weight, w_out
-    )
+    w_own = jnp.concatenate([w_query, key_weight, value_weight, w_out.T], axis=1)
+    places = token_place.reshape(nb, 1, rows * nh)
     gain_one, gain_two = w_norm1.reshape(1, -1), w_norm2.reshape(1, -1)
-    place_row, place_col = own.reshape(1, -1), own.reshape(-1, 1)
     sizes = (nb, nh, hl, kl, repeat)
     router_t = router.T.reshape(nh, local, MODEL_WIDTH).transpose(1, 0, 2).reshape(E, MODEL_WIDTH)
     (
@@ -1520,11 +1546,8 @@
         gain_one,
         gain_two,
         w_own,
-        place_row,
-        place_col,
-        cos_o,
-        sin_o,
-        begin_s,
+        places,
+        lengths,
         grad_out,
         slot_table(nb, nh, repeat, routes, slot_order),
         router_t,
@@ -1552,11 +1575,8 @@
         kv,
         lse,
         attn_t,
-        place_row,
-        place_col,
-        cos_s,
-        sin_s,
-        begin_s,
+        places,
+        lengths,
         d_rows,
         scaled,
         *sums,

time: 361 us -> 337 us (0.934)
  Pallas kernels: 332 us -> 314 us
  other arithmetic: 13.2 us -> 8.97 us
    pallas_call x1, Pallas kernels: 171 us -> 152 us  [back(): pl.pallas_call(functools.partial(back_kernel, nb, nh, hl, kl, repeat), ou...]
where the time goes in v5:
time: 337 us
  Pallas kernels  314 us (93%)
  local copies, waits for them, and re-layouts  12.7 us (4%)
  other arithmetic  8.97 us (3%)
    pallas_call x1, Pallas kernels, back(): pl.pallas_call(functools.partial(back_kernel, nb, nh, hl, kl, repeat), ou...  152 us
    pallas_call x1, Pallas kernels, front(): pl.pallas_call(functools.partial(front_kernel, nb, nh, hl, kl, repeat), o...  139 us
    pallas_call x1, Pallas kernels, experts(): pl.pallas_call(functools.partial(experts_kernel, nz, nh), grid=(nz,), out...  22.7 us

profile of v5, /device:TPU:0, one launch (start us, length us, event | category | flops | bytes accessed | tf_op | source)
XLA Modules:
  0.0 336.8 jit_solution(5747147039426373682)
XLA Ops:
  0.6 0.7 fusion.2
  1.3 0.7 select_reduce_fusion
  2.1 0.7 convert_reduce_fusion
  2.8 0.6 compare_select_fusion.table
  3.4 0.9 copy.46
  4.3 0.9 copy.56
  5.2 0.6 reshape.61.router_t
  5.9 1.6 pad_maximum_fusion.w_own
  7.4 139.4 %front.1 = (bf16[4,128,1024]{2,1,0:T(8,128)(2,1)}, bf16[8,128,768]{2,1,0:T(8,128)(2,1)}, bf16[2,256,256]{2,1,0:T(8,128)(2,1)}, bf16[8,2,256,256]{3,2,1,0:T(8,128...) custom-call(bf16[128,1024]{1,0:T(8,128)(2,1)} %inputs.3, ...), custom_call_target="tpu_custom_call" | custom-call | tf_op jit(solution)/shard_map/front/pallas_call | solution.py:686
  146.9 22.7 %experts.1 = (bf16[4,4,80,1024]{3,2,1,0:T(8,128)(2,1)}, bf16[4,4,80,1024]{3,2,1,0:T(8,128)(2,1)}, f32[4,4,1,80]{3,2,1,0:T(1,128)}, bf16[8,128,512]{2,1,0:T(8,128...) custom-call(bf16[4,4,80,1024]{3,2,1,0:T(8,128)(2,1)} %get-tuple-element.47.x_ref, ...), custom_call_target="tpu_custom_call" | custom-call | tf_op jit(solution)/shard_map/experts/pallas_call | solution.py:823
  169.6 152.3 %back.1 = (bf16[128,1024]{1,0:T(8,128)(2,1)}, f32[128,1024]{1,0:T(8,128)}, f32[768,128]{1,0:T(8,128)}, f32[1,1024]{1,0:T(1,128)}, f32[4,40,256]{2,1,0:T(8,128)},...) custom-call(bf16[128,1024]{1,0:T(8,128)(2,1)} %inputs.3, ...), custom_call_target="tpu_custom_call" | custom-call | tf_op jit(solution)/shard_map/back/pallas_call | solution.py:1433
  321.9 1.4 slice.26
  323.3 0.9 slice.27
  324.4 0.7 copy.55
  325.2 0.9 slice_bitcast_fusion.1
  326.0 1.7 fusion.7
  327.8 0.7 copy.52
  328.5 0.7 copy.51
  329.2 0.8 copy.50
  330.0 1.6 convert_element_type.13
  331.6 1.6 convert_element_type.14
  333.2 1.5 convert_element_type.15
  334.7 0.7 copy.60
  335.4 0.8 copy.61
  (15 shorter events, 0.8 us)
Async XLA Ops:
  321.9 8.1 %copy-start.2 = (bf16[8,128,512]{2,1,0:T(8,128)(2,1)S(1)}, bf16[8,128,512]{2,1,0:T(8,128)(2,1)}, u32[]{:S(2)}) copy-start(bf16[8,128,512]{2,1,0:T(8,128)(2,1)} %get-tuple-element.71) | copy-start | bytes 3145732
  326.0 5.6 %copy-start.1 = (bf16[8,128,512]{2,1,0:T(8,128)(2,1)S(1)}, bf16[8,128,512]{2,1,0:T(8,128)(2,1)}, u32[]{:S(2)}) copy-start(bf16[8,128,512]{2,1,0:T(8,128)(2,1)} %get-tuple-element.72) | copy-start | bytes 3145732
  331.6 1.6 copy-start
  333.2 1.5 copy-start.4
  333.2 2.2 copy-start.3
  333.2 3.0 copy-start.5

commit v6 on v5

--- a/solution.py
+++ b/solution.py
@@ -19,8 +19,8 @@
 SMEM = pl.BlockSpec(memory_space=pltpu.SMEM)
 BF = jnp.bfloat16
 F32 = jnp.float32
-FRONT_DEAL = (0.25, 0.8)
-BACK_DEAL = (0.25, 0.42, 0.6)
+FRONT_DEAL = (0.36, 0.8)
+BACK_DEAL = (0.36, 0.5, 0.7)
 
 eps = 1e-06
 rope_base = 10000.0
@@ -418,11 +418,11 @@
     def keep(buf_out, buf_in, j, z):
         return pltpu.make_async_copy(buf_out.at[z, at.h], buf_in.at[z, at.h], local_sems.at[j, z])
 
-    def outward(relay, body, first, last):
+    def outward(relay, body, first, last, hopped=0):
         def step(t, unused):
             d, side = t // 2, lax.rem(t, 2)
             z = jnp.where(side == 0, at.z - d, at.z + d)
-            pl.when((side == 0) & (d > 0))(lambda: relay.hop(d))
+            pl.when((side == 0) & (d > hopped))(lambda: relay.hop(d))
 
             @pl.when((z >= 0) & (z < at.nz) & ((d > 0) | (side == 0)))
             def _():
@@ -576,6 +576,8 @@
         return 0
 
     lax.fori_loop(0, 4 * (nb // 2), visit, 0)
+    for i in range(2, min(3, at.nz)):
+        g_relay.hop(i)
     deal.start(FRONT_DEAL[0], FRONT_DEAL[1])
     for second in range(2):
         sums = total[second]
@@ -604,7 +606,7 @@
         )
         c.start()
         o_copies.append(c)
-    outward(g_relay, send_g, 2, at.nz)
+    outward(g_relay, send_g, 2, at.nz, 2)
     for k in range(1, nh):
         o_copies[k - 1].wait_recv()
         middle[...] += out_recv[lax.rem(at.h + nh - k, nh)].astype(F32)
@@ -995,7 +997,10 @@
     down_sum,
     output,
     grad_in,
-    grad_w,
+    grad_q,
+    grad_k,
+    grad_v,
+    grad_o,
     grad_n1,
     small_sum,
     gate_in,
@@ -1041,6 +1046,7 @@
     deal_sems,
     deal_local,
     begin,
+    grad_w,
     *loaded,
 ):
     at = Place(nb, nh)
@@ -1395,6 +1401,10 @@
         grad_w[...] += value
 
     w_scatter.take(add_w)
+    grad_q[...] = grad_w[:qw].T
+    grad_k[...] = grad_w[qw : qw + kw].T
+    grad_v[...] = grad_w[qw + kw : width].T
+    grad_o[...] = grad_w[width:]
 
     for c in n1_blk_copies:
         c.wait_recv()
@@ -1435,13 +1445,16 @@
         out_shape=(
             shape((rows, MODEL_WIDTH), BF),
             shape((rows, MODEL_WIDTH), F32),
-            shape((width + qw, dl), F32),
+            shape((dl, qw), F32),
+            shape((dl, kw), F32),
+            shape((dl, kw), F32),
+            shape((qw, dl), F32),
             shape((1, MODEL_WIDTH), F32),
             shape((nh,) + chunk, F32),
             *(shape(v.shape, BF) for v in operands[-3:]),
         ),
         in_specs=[VMEM] * 10 + [ANY] * 4 + [ANY, VMEM, ANY] + [VMEM, SMEM] + [ANY] * 5,
-        out_specs=[VMEM] * 5 + [ANY] * 3,
+        out_specs=[VMEM] * 8 + [ANY] * 3,
         scratch_shapes=[
             pltpu.VMEM((nh, rows, MODEL_WIDTH), BF),
             pltpu.VMEM((group, group), BF),
@@ -1483,6 +1496,7 @@
             dma((2, 3, nb)),
             dma((3,)),
             pltpu.VMEM((2, 1, half), jnp.int32),
+            pltpu.VMEM((width + qw, dl), F32),
             *(pltpu.VMEM(operands[i].shape, operands[i].dtype) for i in (10, 11, 12, 13, 14, 16)),
             dma((6,)),
         ],
@@ -1556,7 +1570,7 @@
         w_down,
     )
     d_rows, scaled, d_gate_rows, *sums = experts(nz, nh, in_rows, in_g, in_gate, *projections)
-    output, grad_inputs, grad_w, grad_norm1, small, *sums = back(
+    output, grad_inputs, grad_q, grad_k, grad_v, grad_o, grad_norm1, small, *sums = back(
         *sizes,
         inputs,
         gain_one,
@@ -1596,10 +1610,10 @@
         output,
         grad_inputs,
         grad_norm1.reshape(-1),
-        grad_w[:qw].T,
-        grad_w[qw : qw + kw].T,
-        grad_w[qw + kw : qw + 2 * kw].T,
-        grad_w[qw + 2 * kw :],
+        grad_q,
+        grad_k,
+        grad_v,
+        grad_o,
         small[E],
         grad_router,
         whole_part(sums[0], 2),

time: 337 us -> 330 us (0.979)
  Pallas kernels: 314 us -> 308 us
    pallas_call x1, Pallas kernels: 152 us -> 149 us  [back(): pl.pallas_call(functools.partial(back_kernel, nb, nh, hl, kl, repeat), ou...]
where the time goes in v6:
time: 330 us; the launch traced here: 329 us
  Pallas kernels  308 us (93%)
  local copies, waits for them, and re-layouts  10.4 us (3%)
  other arithmetic  10.2 us (3%)
    pallas_call x1, Pallas kernels, back(): pl.pallas_call(functools.partial(back_kernel, nb, nh, hl, kl, repeat), ou...  149 us
    pallas_call x1, Pallas kernels, front(): pl.pallas_call(functools.partial(front_kernel, nb, nh, hl, kl, repeat), o...  137 us
    pallas_call x1, Pallas kernels, experts(): pl.pallas_call(functools.partial(experts_kernel, nz, nh), grid=(nz,), out...  22.5 us

profile of v6, /device:TPU:0, one launch (start us, length us, event | category | flops | bytes accessed | tf_op | source)
XLA Modules:
  0.0 329.4 jit_solution(17733187315542221764)
XLA Ops:
  0.6 0.7 fusion.2
  1.3 0.7 select_reduce_fusion
  2.1 0.7 convert_reduce_fusion
  2.8 0.6 compare_select_fusion.table
  3.4 0.9 copy.37
  4.3 0.9 copy.44
  5.2 0.6 reshape.61.router_t
  5.9 1.6 pad_maximum_fusion.w_own
  7.4 136.6 %front.1 = (bf16[4,128,1024]{2,1,0:T(8,128)(2,1)}, bf16[8,128,768]{2,1,0:T(8,128)(2,1)}, bf16[2,256,256]{2,1,0:T(8,128)(2,1)}, bf16[8,2,256,256]{3,2,1,0:T(8,128...) custom-call(bf16[128,1024]{1,0:T(8,128)(2,1)} %inputs.3, ...), custom_call_target="tpu_custom_call" | custom-call | tf_op jit(solution)/shard_map/front/pallas_call | solution.py:688
  144.1 22.5 %experts.1 = (bf16[4,4,80,1024]{3,2,1,0:T(8,128)(2,1)}, bf16[4,4,80,1024]{3,2,1,0:T(8,128)(2,1)}, f32[4,4,1,80]{3,2,1,0:T(1,128)}, bf16[8,128,512]{2,1,0:T(8,128...) custom-call(bf16[4,4,80,1024]{3,2,1,0:T(8,128)(2,1)} %get-tuple-element.50.x_ref, ...), custom_call_target="tpu_custom_call" | custom-call | tf_op jit(solution)/shard_map/experts/pallas_call | solution.py:825
  166.6 148.9 %back.1 = (bf16[128,1024]{1,0:T(8,128)(2,1)}, f32[128,1024]{1,0:T(8,128)}, f32[128,256]{1,0:T(8,128)}, f32[128,128]{1,0:T(8,128)}, f32[128,128]{1,0:T(8,128)}, /...) custom-call(bf16[128,1024]{1,0:T(8,128)(2,1)} %inputs.3, ...), custom_call_target="tpu_custom_call" | custom-call | tf_op jit(solution)/shard_map/back/pallas_call | solution.py:1443
  315.5 1.4 slice.10
  316.8 1.0 slice.11
  318.0 0.7 copy.43
  318.8 2.8 convert_element_type.13
  321.6 1.6 convert_element_type.14
  323.3 1.5 convert_element_type.15
  324.7 0.7 copy.52
  325.4 0.8 copy.53
  326.2 0.6 copy.54
  326.8 0.7 copy.55
  327.5 0.6 copy.56
  328.1 0.6 copy.57
  328.7 0.7 copy.58
  (20 shorter events, 0.2 us)
Async XLA Ops:
  316.8 4.8 %copy-start.1 = (bf16[8,128,512]{2,1,0:T(8,128)(2,1)S(1)}, bf16[8,128,512]{2,1,0:T(8,128)(2,1)}, u32[]{:S(2)}) copy-start(bf16[8,128,512]{2,1,0:T(8,128)(2,1)} %get-tuple-element.78) | copy-start | bytes 3145732
  321.6 1.6 copy-start
  323.2 1.5 copy-start.3
  323.2 2.2 copy-start.2
  323.2 3.0 copy-start.8
  323.2 3.6 %copy-start.5 = (f32[128,256]{1,0:T(8,128)S(1)}, f32[128,256]{1,0:T(8,128)}, u32[]{:S(2)}) copy-start(f32[128,256]{1,0:T(8,128)} %get-tuple-element.95) | copy-start | bytes 393220
  323.2 4.2 %copy-start.7 = (f32[128,128]{1,0:T(8,128)S(1)}, f32[128,128]{1,0:T(8,128)}, u32[]{:S(2)}) copy-start(f32[128,128]{1,0:T(8,128)} %get-tuple-element.96) | copy-start | bytes 196612
  323.2 4.9 %copy-start.6 = (f32[128,128]{1,0:T(8,128)S(1)}, f32[128,128]{1,0:T(8,128)}, u32[]{:S(2)}) copy-start(f32[128,128]{1,0:T(8,128)} %get-tuple-element.97) | copy-start | bytes 196612
  323.3 5.5 %copy-start.4 = (f32[256,128]{1,0:T(8,128)S(1)}, f32[256,128]{1,0:T(8,128)}, u32[]{:S(2)}) copy-start(f32[256,128]{1,0:T(8,128)} %get-tuple-element.98) | copy-start | bytes 393220

commit v7 on v6

--- a/solution.py
+++ b/solution.py
@@ -390,7 +390,6 @@
     slot_relay = Relay(at, slot_all, s_send, s_recv)
     slot_relay.begin()
     g_relay = Relay(at, g_all, g_send, g_recv, 4)
-    g_relay.begin()
     pair = 2 * rows
     own_expert = (at.b // repeat) * nh
 
@@ -477,6 +476,7 @@
     for i in range(1, nb // 2):
         slot_relay.hop(i)
         weights.hop(i)
+    g_relay.begin()
     for z in range(nb // 2):
         slot_relay.take_sibling(z)
     for z in range(nb // 2):

time: 330 us -> 330 us (level)
  no operation moved by 1% of the time
where the time goes in v7:
time: 330 us
  Pallas kernels  308 us (93%)
  local copies, waits for them, and re-layouts  10.4 us (3%)
  other arithmetic  10.2 us (3%)
    pallas_call x1, Pallas kernels, back(): pl.pallas_call(functools.partial(back_kernel, nb, nh, hl, kl, repeat), ou...  149 us
    pallas_call x1, Pallas kernels, front(): pl.pallas_call(functools.partial(front_kernel, nb, nh, hl, kl, repeat), o...  137 us
    pallas_call x1, Pallas kernels, experts(): pl.pallas_call(functools.partial(experts_kernel, nz, nh), grid=(nz,), out...  22.5 us

profile of v7, /device:TPU:0, one launch (start us, length us, event | category | flops | bytes accessed | tf_op | source)
XLA Modules:
  0.0 329.6 jit_solution(8347992076713655170)
XLA Ops:
  0.6 0.7 fusion.2
  1.3 0.7 select_reduce_fusion
  2.1 0.7 convert_reduce_fusion
  2.8 0.6 compare_select_fusion.table
  3.4 0.9 copy.37
  4.3 0.9 copy.44
  5.2 0.6 reshape.61.router_t
  5.9 1.6 pad_maximum_fusion.w_own
  7.4 137.1 %front.1 = (bf16[4,128,1024]{2,1,0:T(8,128)(2,1)}, bf16[8,128,768]{2,1,0:T(8,128)(2,1)}, bf16[2,256,256]{2,1,0:T(8,128)(2,1)}, bf16[8,2,256,256]{3,2,1,0:T(8,128...) custom-call(bf16[128,1024]{1,0:T(8,128)(2,1)} %inputs.3, ...), custom_call_target="tpu_custom_call" | custom-call | tf_op jit(solution)/shard_map/front/pallas_call | solution.py:688
  144.5 22.5 %experts.1 = (bf16[4,4,80,1024]{3,2,1,0:T(8,128)(2,1)}, bf16[4,4,80,1024]{3,2,1,0:T(8,128)(2,1)}, f32[4,4,1,80]{3,2,1,0:T(1,128)}, bf16[8,128,512]{2,1,0:T(8,128...) custom-call(bf16[4,4,80,1024]{3,2,1,0:T(8,128)(2,1)} %get-tuple-element.50.x_ref, ...), custom_call_target="tpu_custom_call" | custom-call | tf_op jit(solution)/shard_map/experts/pallas_call | solution.py:825
  167.0 148.7 %back.1 = (bf16[128,1024]{1,0:T(8,128)(2,1)}, f32[128,1024]{1,0:T(8,128)}, f32[128,256]{1,0:T(8,128)}, f32[128,128]{1,0:T(8,128)}, f32[128,128]{1,0:T(8,128)}, /...) custom-call(bf16[128,1024]{1,0:T(8,128)(2,1)} %inputs.3, ...), custom_call_target="tpu_custom_call" | custom-call | tf_op jit(solution)/shard_map/back/pallas_call | solution.py:1443
  315.7 1.4 slice.10
  317.0 1.0 slice.11
  318.2 0.7 copy.43
  319.0 2.8 convert_element_type.13
  321.8 1.6 convert_element_type.14
  323.5 1.5 convert_element_type.15
  324.9 0.7 copy.52
  325.6 0.8 copy.53
  326.4 0.6 copy.54
  327.0 0.7 copy.55
  327.7 0.6 copy.56
  328.3 0.6 copy.57
  329.0 0.7 copy.58
  (20 shorter events, 0.2 us)
Async XLA Ops:
  317.0 4.8 %copy-start.1 = (bf16[8,128,512]{2,1,0:T(8,128)(2,1)S(1)}, bf16[8,128,512]{2,1,0:T(8,128)(2,1)}, u32[]{:S(2)}) copy-start(bf16[8,128,512]{2,1,0:T(8,128)(2,1)} %get-tuple-element.78) | copy-start | bytes 3145732
  321.8 1.6 copy-start
  323.4 1.5 copy-start.3
  323.4 2.2 copy-start.2
  323.4 3.0 copy-start.8
  323.4 3.6 %copy-start.5 = (f32[128,256]{1,0:T(8,128)S(1)}, f32[128,256]{1,0:T(8,128)}, u32[]{:S(2)}) copy-start(f32[128,256]{1,0:T(8,128)} %get-tuple-element.95) | copy-start | bytes 393220
  323.4 4.2 %copy-start.7 = (f32[128,128]{1,0:T(8,128)S(1)}, f32[128,128]{1,0:T(8,128)}, u32[]{:S(2)}) copy-start(f32[128,128]{1,0:T(8,128)} %get-tuple-element.96) | copy-start | bytes 196612
  323.4 4.9 %copy-start.6 = (f32[128,128]{1,0:T(8,128)S(1)}, f32[128,128]{1,0:T(8,128)}, u32[]{:S(2)}) copy-start(f32[128,128]{1,0:T(8,128)} %get-tuple-element.97) | copy-start | bytes 196612
  323.5 5.5 %copy-start.4 = (f32[256,128]{1,0:T(8,128)S(1)}, f32[256,128]{1,0:T(8,128)}, u32[]{:S(2)}) copy-start(f32[256,128]{1,0:T(8,128)} %get-tuple-element.98) | copy-start | bytes 393220
